TPU v7x, 32 devices: a whole 2x2x4 slice. The times are simulated.
32 devices in a mesh: dp: 4 (over y, x), mp: 8 (over z, core).
Axes of the slice: x: 2, y: 2, z: 4, core: 2. Of those that a mesh axis runs over, the one named last changes fastest.
Arguments:
- source_ids: int32 [8, 1024], P('dp'), may hold values from 0 to 32127
- target_ids: int32 [8, 1024], P('dp'), may hold values from 0 to 32127
- prefix: int32 [8], replicated, may hold values from 192 to 832
- attn_in: float32 [3, 1024, 2048], P(None, ('dp', 'mp')), may hold values from -0.1875 to 0.1875
- attn_out: float32 [3, 1024, 1024], P(None, ('dp', 'mp')), may hold values from -6 to 6
- ff_in: float32 [2, 1024, 5632], P(None, ('dp', 'mp')), may hold values from -0.1875 to 0.1875
- ff_out: float32 [2, 2816, 1024], P(None, ('dp', 'mp')), may hold values from -0.109375 to 0.109375
- table: float32 [32128, 1024], P('mp', 'dp')
- gains: float32 [7, 1024], P(None, ('dp', 'mp'))
- attn_in_mom: float32 [3, 1024, 2048], P(None, ('dp', 'mp')), may hold values from -1.4901161e-08 to 1.4901161e-08
- attn_out_mom: float32 [3, 1024, 1024], P(None, ('dp', 'mp')), may hold values from -1.4901161e-08 to 1.4901161e-08
- ff_in_mom: float32 [2, 1024, 5632], P(None, ('dp', 'mp')), may hold values from -1.4901161e-08 to 1.4901161e-08
- ff_out_mom: float32 [2, 2816, 1024], P(None, ('dp', 'mp')), may hold values from -1.4901161e-08 to 1.4901161e-08
- table_mom: float32 [32128, 1024], P('mp', 'dp'), may hold values from -7.450581e-09 to 7.450581e-09
- gains_mom: float32 [7, 1024], P(None, ('dp', 'mp')), may hold values from -8.940697e-08 to 8.940697e-08
- attn_in_avg: float32 [3, 1024, 2048], P(None, ('dp', 'mp')), may hold values from -0.1875 to 0.1875
- attn_out_avg: float32 [3, 1024, 1024], P(None, ('dp', 'mp')), may hold values from -6 to 6
- ff_in_avg: float32 [2, 1024, 5632], P(None, ('dp', 'mp')), may hold values from -0.1875 to 0.1875
- ff_out_avg: float32 [2, 2816, 1024], P(None, ('dp', 'mp')), may hold values from -0.109375 to 0.109375
- table_avg: float32 [32128, 1024], P('mp', 'dp'), may hold values from -8 to 8
- gains_avg: float32 [7, 1024], P(None, ('dp', 'mp')), may hold values from 0.5 to 1.5
Outputs:
- loss_sum: float32 [], replicated
- scored_count: float32 [], replicated
- grad_norm: float32 [], replicated
- new_attn_in: float32 [3, 1024, 2048], P(None, ('dp', 'mp'))
- new_attn_out: float32 [3, 1024, 1024], P(None, ('dp', 'mp'))
- new_ff_in: float32 [2, 1024, 5632], P(None, ('dp', 'mp'))
- new_ff_out: float32 [2, 2816, 1024], P(None, ('dp', 'mp'))
- new_table: float32 [32128, 1024], P('mp', 'dp')
- new_gains: float32 [7, 1024], P(None, ('dp', 'mp'))
- mom_attn_in: float32 [3, 1024, 2048], P(None, ('dp', 'mp'))
- mom_attn_out: float32 [3, 1024, 1024], P(None, ('dp', 'mp'))
- mom_ff_in: float32 [2, 1024, 5632], P(None, ('dp', 'mp'))
- mom_ff_out: float32 [2, 2816, 1024], P(None, ('dp', 'mp'))
- mom_table: float32 [32128, 1024], P('mp', 'dp')
- mom_gains: float32 [7, 1024], P(None, ('dp', 'mp'))
- avg_attn_in: float32 [3, 1024, 2048], P(None, ('dp', 'mp'))
- avg_attn_out: float32 [3, 1024, 1024], P(None, ('dp', 'mp'))
- avg_ff_in: float32 [2, 1024, 5632], P(None, ('dp', 'mp'))
- avg_ff_out: float32 [2, 2816, 1024], P(None, ('dp', 'mp'))
- avg_table: float32 [32128, 1024], P('mp', 'dp')
- avg_gains: float32 [7, 1024], P(None, ('dp', 'mp'))
All inputs are finite; a program needn't handle non-finite values.
Results may differ from a plain program's by a relative error of at most 0.0095.
The roundings to bfloat16 on the way count: a program that leaves them out, or rounds other values in their place, can miss the bound.
Values may be sent and summed in bfloat16 or wider, within the bound.
A program may use at most 384 MiB of HBM per device.

v0:
```python
from functools import partial

import jax
import jax.numpy as jnp
from jax import lax
from jax.sharding import PartitionSpec as P

D = 1024
HQ = 16
HK = 8
HD = 64
FF = 2816
LEN = 1024
QW = 1024
KW = 512
PARAMS = 59644928


MOMENTUM = 0.9
AVERAGE = 0.9
CLIP = 0.0002
EPS = 1e-06
layer_plan = ((0, 1, 0, 0, 3), (1, 3, 1, 3, 7))


def as_sent(shard):

    def short(part):
        return part.astype(jnp.bfloat16) if part.dtype == jnp.float32 else part

    return jax.tree.map(short, shard)


def joined(shard, axis, combine):
    everything = jax.tree.map(lambda part: lax.all_gather(part, axis), shard)
    first = jax.tree.map(lambda part: part[0], everything)

    def hop(k, so_far):
        return combine(so_far, jax.tree.map(lambda part: part[k], everything))

    return lax.fori_loop(1, lax.axis_size(axis), hop, first)


def step_rates():
    base_rate = 3.5 * PARAMS**0.5 / CLIP
    return (
        base_rate * D ** (-0.5),
        base_rate * max(QW // LEN, 1) ** (-0.5),
        base_rate * D ** (-0.5),
        base_rate * FF ** (-0.5),
        base_rate * 2.0,
        base_rate * 0.3,
    )


def norm_forward(stream, gain_row):
    inverse = lax.rsqrt(jnp.mean(stream * stream, axis=-1, keepdims=True) + EPS)
    return stream * inverse * gain_row


def norm_backward(stream, gain_row, grad_out):
    inverse = lax.rsqrt(jnp.mean(stream * stream, axis=-1, keepdims=True) + EPS)
    scaled = grad_out * gain_row
    d_input = inverse * scaled - stream * inverse**3 * jnp.mean(
        stream * scaled, axis=-1, keepdims=True
    )
    return (d_input, jnp.sum(grad_out * stream * inverse, axis=(0, 1)))


def project_keys(anchor, weight_in):
    own_rows = jnp.einsum(
        "brd,dk->brk", anchor, weight_in[:, QW:], preferred_element_type=jnp.float32
    )
    return lax.all_gather(own_rows.astype(jnp.bfloat16), "mp", axis=1, tiled=True)


def head_split(queries, keyvals):
    seq_count, row_count = queries.shape[:2]
    length = keyvals.shape[1]
    query_heads = queries.reshape(seq_count, row_count, HK, HQ // HK, HD)
    key_heads = keyvals[..., :KW].reshape(seq_count, length, HK, HD)
    value_heads = keyvals[..., KW:].reshape(seq_count, length, HK, HD)
    return (query_heads, key_heads, value_heads)


def scores_of(query_heads, key_heads, causal):
    row_count = query_heads.shape[1]
    length = key_heads.shape[1]
    scores = jnp.einsum(
        "brhgd,bkhd->bhgrk", query_heads, key_heads, preferred_element_type=jnp.float32
    ) * HD ** (-0.5)
    if causal:
        first_row = lax.axis_index("mp") * row_count
        allowed = (first_row + jnp.arange(row_count))[:, None] >= jnp.arange(length)[None, :]
        scores = jnp.where(allowed, scores, -1000000000.0)
    return scores


def attend_forward(queries, keyvals, causal):
    seq_count, row_count = queries.shape[:2]
    query_heads, key_heads, value_heads = head_split(queries, keyvals)
    scores = scores_of(query_heads, key_heads, causal)
    row_max = jnp.max(scores, axis=-1, keepdims=True)
    expo_terms = jnp.exp(scores - row_max)
    row_total = jnp.sum(expo_terms, axis=-1, keepdims=True)
    attn_probs = (expo_terms / row_total).astype(jnp.bfloat16)
    mixed = jnp.einsum(
        "bhgrk,bkhd->brhgd", attn_probs, value_heads, preferred_element_type=jnp.float32
    )
    return (
        mixed.reshape(seq_count, row_count, QW).astype(jnp.bfloat16),
        row_max + jnp.log(row_total),
    )


def attend_backward(queries, keyvals, causal, log_total, d_mixed):
    seq_count, row_count = queries.shape[:2]
    length = keyvals.shape[1]
    query_heads, key_heads, value_heads = head_split(queries, keyvals)
    attn_probs = jnp.exp(scores_of(query_heads, key_heads, causal) - log_total)
    d_heads = d_mixed.reshape(seq_count, row_count, HK, HQ // HK, HD)
    d_probs = jnp.einsum(
        "brhgd,bkhd->bhgrk", d_heads, value_heads, preferred_element_type=jnp.float32
    )
    d_scores = attn_probs * (d_probs - jnp.sum(attn_probs * d_probs, axis=-1, keepdims=True))
    d_scores = d_scores.astype(jnp.bfloat16)
    d_queries = jnp.einsum(
        "bhgrk,bkhd->brhgd", d_scores, key_heads, preferred_element_type=jnp.float32
    ) * HD ** (-0.5)
    d_keys = jnp.einsum(
        "bhgrk,brhgd->bkhd", d_scores, query_heads, preferred_element_type=jnp.float32
    ) * HD ** (-0.5)
    d_values = jnp.einsum(
        "bhgrk,brhgd->bkhd",
        attn_probs.astype(jnp.bfloat16),
        d_heads,
        preferred_element_type=jnp.float32,
    )
    d_keyvals = jnp.concatenate(
        [d_keys.reshape(seq_count, length, KW), d_values.reshape(seq_count, length, KW)], axis=-1
    )
    return (d_queries.reshape(seq_count, row_count, QW), d_keyvals)


def attention_forward(stream, source, weight_in, weight_out, gain_row, causal):
    normed = norm_forward(stream, gain_row).astype(jnp.bfloat16)
    anchor = normed if source is None else source
    queries = jnp.einsum(
        "brd,dq->brq", normed, weight_in[:, :QW], preferred_element_type=jnp.float32
    ).astype(jnp.bfloat16)
    keyvals = project_keys(anchor, weight_in)
    mixed, log_total = attend_forward(queries, keyvals, causal)
    branch = jnp.einsum("brq,qd->brd", mixed, weight_out, preferred_element_type=jnp.float32)
    return (stream + branch, (stream, log_total, mixed))


def attention_backward(saved, source, weight_in, weight_out, gain_row, causal, d_stream):
    stream, log_total, mixed = saved
    normed = norm_forward(stream, gain_row).astype(jnp.bfloat16)
    anchor = normed if source is None else source
    queries = jnp.einsum(
        "brd,dq->brq", normed, weight_in[:, :QW], preferred_element_type=jnp.float32
    ).astype(jnp.bfloat16)
    keyvals = project_keys(anchor, weight_in)
    d_branch = d_stream.astype(jnp.bfloat16)
    grad_out = jnp.einsum("brq,brd->qd", mixed, d_branch, preferred_element_type=jnp.float32)
    d_mixed = jnp.einsum(
        "brd,qd->brq", d_branch, weight_out, preferred_element_type=jnp.float32
    ).astype(jnp.bfloat16)
    d_queries, d_keyvals = attend_backward(queries, keyvals, causal, log_total, d_mixed)
    d_queries = d_queries.astype(jnp.bfloat16)
    d_keyvals = lax.psum_scatter(
        d_keyvals.astype(jnp.bfloat16), "mp", scatter_dimension=1, tiled=True
    )
    grad_in = jnp.concatenate(
        [
            jnp.einsum("brd,brq->dq", normed, d_queries, preferred_element_type=jnp.float32),
            jnp.einsum("brd,brk->dk", anchor, d_keyvals, preferred_element_type=jnp.float32),
        ],
        axis=1,
    )
    d_normed = jnp.einsum(
        "brq,dq->brd", d_queries, weight_in[:, :QW], preferred_element_type=jnp.float32
    )
    d_anchor = jnp.einsum(
        "brk,dk->brd", d_keyvals, weight_in[:, QW:], preferred_element_type=jnp.float32
    )
    if source is None:
        d_normed = d_normed + d_anchor
        d_anchor = None
    d_input, grad_gain = norm_backward(stream, gain_row, d_normed)
    return (d_stream + d_input, d_anchor, grad_in, grad_out, grad_gain)


def ffn_parts(stream, weight_in, gain_row):
    normed = norm_forward(stream, gain_row).astype(jnp.bfloat16)
    both = jnp.einsum("brd,df->brf", normed, weight_in, preferred_element_type=jnp.float32)
    return (normed, both)


def ffn_forward(stream, weight_in, weight_out, gain_row):
    normed, both = ffn_parts(stream, weight_in, gain_row)
    width = weight_out.shape[0]
    hidden_act = (jax.nn.gelu(both[..., :width], approximate=True) * both[..., width:]).astype(
        jnp.bfloat16
    )
    return stream + jnp.einsum(
        "brf,fd->brd", hidden_act, weight_out, preferred_element_type=jnp.float32
    )


def ffn_backward(stream, weight_in, weight_out, gain_row, d_stream):
    normed, both = ffn_parts(stream, weight_in, gain_row)
    width = weight_out.shape[0]
    gate_part = both[..., :width]
    up_part = both[..., width:]
    activated, gelu_pull = jax.vjp(partial(jax.nn.gelu, approximate=True), gate_part)
    hidden_act = (activated * up_part).astype(jnp.bfloat16)
    d_branch = d_stream.astype(jnp.bfloat16)
    grad_out = jnp.einsum("brf,brd->fd", hidden_act, d_branch, preferred_element_type=jnp.float32)
    d_hidden = jnp.einsum("brd,fd->brf", d_branch, weight_out, preferred_element_type=jnp.float32)
    d_both = jnp.concatenate(
        [gelu_pull(d_hidden * up_part)[0], d_hidden * activated], axis=-1
    ).astype(jnp.bfloat16)
    grad_in = jnp.einsum("brd,brf->df", normed, d_both, preferred_element_type=jnp.float32)
    d_normed = jnp.einsum("brf,df->brd", d_both, weight_in, preferred_element_type=jnp.float32)
    d_input, grad_gain = norm_backward(stream, gain_row, d_normed)
    return (d_stream + d_input, grad_in, grad_out, grad_gain)


def layer_forward(stream, source, gathered, causal):
    attn_in, attn_out, ffn_in, ffn_out, gain_rows = gathered
    gain_rows = gain_rows.astype(jnp.float32)
    block_count = attn_in.shape[0]
    saved_blocks = []
    for block_index in range(block_count):
        anchor = None if block_index == 0 else source
        stream, saved = attention_forward(
            stream,
            anchor,
            attn_in[block_index],
            attn_out[block_index],
            gain_rows[block_index],
            causal and block_index == 0,
        )
        saved_blocks.append(saved)
    ffn_input = stream
    stream = ffn_forward(stream, ffn_in[0], ffn_out[0], gain_rows[block_count])
    final_rows = norm_forward(stream, gain_rows[block_count + 1]).astype(jnp.bfloat16)
    return (final_rows, (saved_blocks, ffn_input, stream))


def layer_backward(saves, source, gathered, causal, d_final):
    attn_in, attn_out, ffn_in, ffn_out, gain_rows = gathered
    gain_rows = gain_rows.astype(jnp.float32)
    saved_blocks, ffn_input, last_stream = saves
    block_count = attn_in.shape[0]
    d_stream, gain_last = norm_backward(last_stream, gain_rows[block_count + 1], d_final)
    d_stream, ffn_grad_in, ffn_grad_out, gain_ffn = ffn_backward(
        ffn_input, ffn_in[0], ffn_out[0], gain_rows[block_count], d_stream
    )
    grads_in, grads_out, gain_grads = ([], [], [])
    d_source = None
    for block_index in reversed(range(block_count)):
        anchor = None if block_index == 0 else source
        d_stream, d_anchor, grad_in, grad_out, grad_gain = attention_backward(
            saved_blocks[block_index],
            anchor,
            attn_in[block_index],
            attn_out[block_index],
            gain_rows[block_index],
            causal and block_index == 0,
            d_stream,
        )
        if d_anchor is not None:
            d_source = d_anchor
        grads_in.insert(0, grad_in)
        grads_out.insert(0, grad_out)
        gain_grads.insert(0, grad_gain)
    layer_grads = (
        jnp.stack(grads_in),
        jnp.stack(grads_out),
        ffn_grad_in[None],
        ffn_grad_out[None],
        jnp.stack(gain_grads + [gain_ffn, gain_last]),
    )
    return (d_stream, d_source, layer_grads)


def update(weight, gradient, moment, average, rate, factor):
    clipped = gradient * factor
    moment_new = MOMENTUM * moment + (1 - MOMENTUM) * clipped
    weight_new = weight - rate * ((1 - MOMENTUM) * clipped + MOMENTUM * moment_new)
    average_new = AVERAGE * average + (1 - AVERAGE) * weight_new
    return (weight_new, moment_new, average_new)


def on_device(
    source_ids,
    target_ids,
    prefix,
    attn_in,
    attn_out,
    ff_in,
    ff_out,
    table,
    gains,
    attn_in_mom,
    attn_out_mom,
    ff_in_mom,
    ff_out_mom,
    table_mom,
    gains_mom,
    attn_in_avg,
    attn_out_avg,
    ff_in_avg,
    ff_out_avg,
    table_avg,
    gains_avg,
):
    seq_count, length = source_ids.shape
    row_count = length // lax.axis_size("mp")
    first_row = lax.axis_index("mp") * row_count
    decoder_ids = jnp.concatenate(
        [jnp.zeros((seq_count, 1), jnp.int32), target_ids[:, :-1]], axis=1
    )
    token_ids = jnp.stack([source_ids, decoder_ids])
    table_rows = lax.all_gather(table.astype(jnp.bfloat16), "dp", axis=1, tiled=True)
    vocab_part = table_rows.shape[0]
    offset = lax.axis_index("mp") * vocab_part
    local_ids = token_ids - offset
    inside = (local_ids >= 0) & (local_ids < vocab_part)
    looked = jnp.where(
        inside[..., None],
        table_rows[jnp.clip(local_ids, 0, vocab_part - 1)],
        jnp.zeros((), jnp.bfloat16),
    )
    embedded = lax.psum_scatter(
        looked.astype(jnp.float32).astype(jnp.bfloat16), "mp", scatter_dimension=2, tiled=True
    ).astype(jnp.float32)

    def owned_shards(plan):
        attn_first, attn_last, ffn_index, gain_first, gain_last = plan
        return (
            attn_in[attn_first:attn_last].astype(jnp.bfloat16),
            attn_out[attn_first:attn_last].astype(jnp.bfloat16),
            ff_in[ffn_index : ffn_index + 1].astype(jnp.bfloat16),
            ff_out[ffn_index : ffn_index + 1].astype(jnp.bfloat16),
            gains[gain_first:gain_last].astype(jnp.bfloat16),
        )

    def fetch_layer(plan):
        return lax.all_gather(as_sent(owned_shards(plan)), ("dp", "mp"), axis=1, tiled=True)

    def fetch_again(plan):
        return lax.all_gather(as_sent(owned_shards(plan)), ("dp", "mp"), axis=1, tiled=True)

    def reduce_grads(layer_grads):
        return lax.psum_scatter(layer_grads, ("dp", "mp"), scatter_dimension=1, tiled=True)

    enc_weights = fetch_layer(layer_plan[0])
    encoded, enc_saves = layer_forward(embedded[0], None, enc_weights, False)
    dec_weights = fetch_layer(layer_plan[1])
    decoded, dec_saves = layer_forward(embedded[1], encoded, dec_weights, True)
    final_all = lax.all_gather(decoded, "mp", axis=1, tiled=True)
    vocab_ids = offset + jnp.arange(vocab_part)

    def head_logits(hidden_rows):
        return jnp.einsum(
            "ld,vd->lv", hidden_rows, table_rows, preferred_element_type=jnp.float32
        ) * D ** (-0.5)

    def head_stats(item_pair):
        hidden_rows, target_row = item_pair
        logits = head_logits(hidden_rows)
        row_max = jnp.max(logits, axis=-1)
        row_total = jnp.sum(jnp.exp(logits - row_max[:, None]), axis=-1)
        picked = jnp.sum(jnp.where(vocab_ids[None, :] == target_row[:, None], logits, 0.0), axis=-1)
        return (row_max, row_total, picked)

    row_max, row_total, picked = lax.map(head_stats, (final_all, target_ids))

    def combine(left_part, right_part):
        joint_max = jnp.maximum(left_part[0], right_part[0])
        joint_total = left_part[1] * jnp.exp(left_part[0] - joint_max) + right_part[1] * jnp.exp(
            right_part[0] - joint_max
        )
        return (joint_max, joint_total, left_part[2] + right_part[2])

    row_max, row_total, picked = joined((row_max, row_total, picked), "mp", combine)
    log_norm = row_max + jnp.log(row_total)
    prefix_group = lax.dynamic_slice_in_dim(prefix, lax.axis_index("dp") * seq_count, seq_count)
    scored = (jnp.arange(length)[None, :] >= prefix_group[:, None]).astype(jnp.float32)
    scored_count = jnp.sum((length - prefix).astype(jnp.float32))

    def head_back(table_sum, seq_items):
        hidden_rows, target_row, weight_row, norm_row = seq_items
        logits = head_logits(hidden_rows)
        hits = (vocab_ids[None, :] == target_row[:, None]).astype(jnp.float32)
        d_logits = (
            (jnp.exp(logits - norm_row[:, None]) - hits) * (weight_row / scored_count)[:, None]
        ).astype(jnp.bfloat16)
        d_hidden = jnp.einsum(
            "lv,vd->ld", d_logits, table_rows, preferred_element_type=jnp.float32
        ) * D ** (-0.5)
        table_term = jnp.einsum(
            "lv,ld->vd", d_logits, hidden_rows, preferred_element_type=jnp.float32
        ) * D ** (-0.5)
        return (table_sum + table_term, d_hidden)

    head_table, d_final_all = lax.scan(
        head_back,
        jnp.zeros((vocab_part, table_rows.shape[1]), jnp.float32),
        (final_all, target_ids, scored, log_norm),
    )
    d_final = lax.psum_scatter(
        d_final_all.astype(jnp.bfloat16), "mp", scatter_dimension=1, tiled=True
    ).astype(jnp.float32)
    dec_weights = fetch_again(layer_plan[1])
    d_decoded, d_encoded, dec_grads = layer_backward(dec_saves, encoded, dec_weights, True, d_final)
    dec_shards = reduce_grads(dec_grads)
    enc_weights = fetch_again(layer_plan[0])
    d_source, unused_grad, enc_grads = layer_backward(
        enc_saves, None, enc_weights, False, d_encoded
    )
    enc_shards = reduce_grads(enc_grads)
    gradients = tuple(
        (
            jnp.concatenate([enc_part, dec_part], axis=0)
            for enc_part, dec_part in zip(enc_shards, dec_shards)
        )
    )
    d_embedded = jnp.stack([d_source, d_decoded]).astype(jnp.bfloat16)
    d_all = lax.all_gather(d_embedded, "mp", axis=2, tiled=True)
    segment_ids = jnp.where(inside, local_ids, vocab_part).reshape(-1)
    lookup_grad = jax.ops.segment_sum(
        d_all.reshape(-1, d_all.shape[-1]).astype(jnp.float32),
        segment_ids,
        num_segments=vocab_part + 1,
    )[:vocab_part]
    grad_table = lax.psum_scatter(
        (head_table + lookup_grad).astype(jnp.bfloat16), "dp", scatter_dimension=1, tiled=True
    ).astype(jnp.float32)
    gradients = (gradients[0], gradients[1], gradients[2], gradients[3], grad_table, gradients[4])

    def own_rows(values):
        return lax.dynamic_slice_in_dim(values, first_row, row_count, axis=1)

    loss_part = jnp.sum((own_rows(log_norm) - own_rows(picked)) * own_rows(scored))
    squares = sum((jnp.sum(gradient * gradient) for gradient in gradients))
    loss_sum, squares = lax.psum((loss_part, squares), ("dp", "mp"))
    grad_norm = jnp.sqrt(squares)
    factor = jnp.minimum(1.0, CLIP / grad_norm)
    weights = (attn_in, attn_out, ff_in, ff_out, table, gains)
    moments = (attn_in_mom, attn_out_mom, ff_in_mom, ff_out_mom, table_mom, gains_mom)
    averages = (attn_in_avg, attn_out_avg, ff_in_avg, ff_out_avg, table_avg, gains_avg)
    results = [
        update(weight, gradient, moment, average, rate, factor)
        for weight, gradient, moment, average, rate in zip(
            weights, gradients, moments, averages, step_rates()
        )
    ]
    return (
        loss_sum,
        scored_count,
        grad_norm,
        results[0][0],
        results[1][0],
        results[2][0],
        results[3][0],
        results[4][0],
        results[5][0],
        results[0][1],
        results[1][1],
        results[2][1],
        results[3][1],
        results[4][1],
        results[5][1],
        results[0][2],
        results[1][2],
        results[2][2],
        results[3][2],
        results[4][2],
        results[5][2],
    )


def solution(mesh):
    in_specs = (
        P("dp", None),
        P("dp", None),
        P(),
        P(None, ("dp", "mp"), None),
        P(None, ("dp", "mp"), None),
        P(None, ("dp", "mp"), None),
        P(None, ("dp", "mp"), None),
        P("mp", "dp"),
        P(None, ("dp", "mp")),
        P(None, ("dp", "mp"), None),
        P(None, ("dp", "mp"), None),
        P(None, ("dp", "mp"), None),
        P(None, ("dp", "mp"), None),
        P("mp", "dp"),
        P(None, ("dp", "mp")),
        P(None, ("dp", "mp"), None),
        P(None, ("dp", "mp"), None),
        P(None, ("dp", "mp"), None),
        P(None, ("dp", "mp"), None),
        P("mp", "dp"),
        P(None, ("dp", "mp")),
    )
    out_specs = (
        P(),
        P(),
        P(),
        P(None, ("dp", "mp"), None),
        P(None, ("dp", "mp"), None),
        P(None, ("dp", "mp"), None),
        P(None, ("dp", "mp"), None),
        P("mp", "dp"),
        P(None, ("dp", "mp")),
        P(None, ("dp", "mp"), None),
        P(None, ("dp", "mp"), None),
        P(None, ("dp", "mp"), None),
        P(None, ("dp", "mp"), None),
        P("mp", "dp"),
        P(None, ("dp", "mp")),
        P(None, ("dp", "mp"), None),
        P(None, ("dp", "mp"), None),
        P(None, ("dp", "mp"), None),
        P(None, ("dp", "mp"), None),
        P("mp", "dp"),
        P(None, ("dp", "mp")),
    )
    return jax.shard_map(
        on_device, mesh=mesh, in_specs=in_specs, out_specs=out_specs, check_vma=False
    )
```

profile of v0, /device:TPU:0, one launch (start us, length us, event | category | flops | bytes accessed | tf_op | source)
XLA Modules:
  0.0 3559.2 jit_solution(5392820286642862115)
XLA Ops:
  12.6 88.2 %all-gather.23.cloned.1.call-done = bf16[4016,1024]{1,0:T(8,128)(2,1)} async-done(((bf16[4016,256]{1,0:T(8,128)(2,1)}), bf16[4016,1024]{1,0:T(8,128)(2,1)}) %all-gather.23.cloned.1.call-update) | async-done | bytes 8224784 | tf_op jit(solution)/shard_map/all_gather | solution.py:328
  100.7 25.2 gather_fusion
  135.9 41.7 %all-gather.4 = bf16[32,32,3]{1,2,0:T(4,128)(2,1)S(1)} all-gather(bf16[1,32,3]{1,2,0:T(4,128)(2,1)S(1)} %slice_bitcast_fusion.53), channel_id=1, replica_groups=mesh['dp'=4,'mp'=8] {'dp','mp'}, dimensions={0}, use_global_device_ids=true | all-gather | bytes 6336 | tf_op jit(solution)/shard_map/all_gather | solution.py:353
  177.7 38.0 %all-gather.3 = bf16[32,32,4]{1,2,0:T(4,128)(2,1)S(1)} all-gather(bf16[1,32,4]{1,2,0:T(4,128)(2,1)S(1)} %slice_bitcast_fusion.54), channel_id=1, replica_groups=mesh['dp'=4,'mp'=8] {'dp','mp'}, dimensions={0}, use_global_device_ids=true | all-gather | bytes 8448 | tf_op jit(solution)/shard_map/all_gather | solution.py:353
  217.0 15.0 reduce-scatter.21.cloned.1.call-done
  236.3 16.2 all-gather.31.cloned.1.call-done
  261.4 71.0 %all-gather.25.cloned.1.call-done = bf16[2,1024,2048]{2,1,0:T(8,128)(2,1)} async-done(((bf16[2,32,2048]{2,1,0:T(8,128)(2,1)}), bf16[2,1024,2048]{2,1,0:T(8,128)(2,1)}) %all-gather.25.cloned.1.call-update) | async-done | bytes 8388624 | tf_op jit(solution)/shard_map/all_gather | solution.py:353
  344.7 35.0 all-gather.33.cloned.1.call-done
  419.3 19.5 all-gather.35.cloned.1.call-done
  442.0 90.0 %all-gather.37.cloned.1.call-done = bf16[1,1024,5632]{2,1,0:T(8,128)(2,1)} async-done(((bf16[1,32,5632]{2,1,0:T(8,128)(2,1)}), bf16[1,1024,5632]{2,1,0:T(8,128)(2,1)}) %all-gather.37.cloned.1.call-update) | async-done | bytes 11534352 | tf_op jit(solution)/shard_map/all_gather | solution.py:353
  542.7 59.2 %all-gather.39.cloned.1.call-done = bf16[1,2816,1024]{2,1,0:T(8,128)(2,1)} async-done(((bf16[1,88,1024]{2,1,0:T(8,128)(2,1)}), bf16[1,2816,1024]{2,1,0:T(8,128)(2,1)}) %all-gather.39.cloned.1.call-update) | async-done | bytes 5767184 | tf_op jit(solution)/shard_map/all_gather | solution.py:353
  613.6 35.7 %all-gather.27.cloned.1.call-done = bf16[2,1024,1024]{2,1,0:T(8,128)(2,1)} async-done(((bf16[2,128,1024]{2,1,0:T(8,128)(2,1)}), bf16[2,1024,1024]{2,1,0:T(8,128)(2,1)}) %all-gather.27.cloned.1.call-update) | async-done | bytes 4194320 | tf_op jit(solution)/shard_map/all_gather | solution.py:74
  691.4 22.2 all-gather.29.cloned.1.call-done
  718.7 42.5 %all-gather.41.cloned.1.call-done = bf16[2,1024,1024]{2,1,0:T(8,128)(2,1)} async-done(((bf16[2,128,1024]{2,1,0:T(8,128)(2,1)}), bf16[2,1024,1024]{2,1,0:T(8,128)(2,1)}) %all-gather.41.cloned.1.call-update) | async-done | bytes 4194320 | tf_op jit(solution)/shard_map/all_gather | solution.py:74
  800.8 53.5 %all-gather.43.cloned.1.call-done = bf16[1,1024,5632]{2,1,0:T(8,128)(2,1)} async-done(((bf16[1,32,5632]{2,1,0:T(8,128)(2,1)}), bf16[1,1024,5632]{2,1,0:T(8,128)(2,1)}) %all-gather.43.cloned.1.call-update) | async-done | bytes 11534352 | tf_op jit(solution)/shard_map/all_gather | solution.py:353
  864.0 60.0 %all-gather.45.cloned.1.call-done = bf16[1,2816,1024]{2,1,0:T(8,128)(2,1)} async-done(((bf16[1,88,1024]{2,1,0:T(8,128)(2,1)}), bf16[1,2816,1024]{2,1,0:T(8,128)(2,1)}) %all-gather.45.cloned.1.call-update) | async-done | bytes 5767184 | tf_op jit(solution)/shard_map/all_gather | solution.py:353
  932.0 44.4 %all-gather.47.cloned.1.call-done = bf16[2,1024,1024]{2,1,0:T(8,128)(2,1)} async-done(((bf16[2,128,1024]{2,1,0:T(8,128)(2,1)}), bf16[2,1024,1024]{2,1,0:T(8,128)(2,1)}) %all-gather.47.cloned.1.call-update) | async-done | bytes 4194320 | tf_op jit(solution)/shard_map/all_gather | solution.py:365
  976.4 34.9 while.48
  1011.3 14.0 all-gather.5
  1025.3 14.0 all-gather.7
  1039.3 14.0 all-gather.6
  1054.2 98.5 %while.49 = (s32[]{:T(128)}, f32[4016,1024]{1,0:T(8,128)}, bf16[2,1024,1024]{2,1,0:T(8,128)(2,1)}, bf16[2,1024,1024]{2,1,0:T(8,128)(2,1)}, bf16[4016,1024]{1,0:T...) while((s32[]{:T(128)}, f32[4016,1024]{1,0:T(8,128)}, ...), condition=%wide.region_25.26_spmd.clone, body=%wide.region_24.25_spmd.clone.sunk | while | flops 25308663808 | bytes 148934256 | solution.py:411
  1056.0 17.4 multiply_convert_fusion.21
  1084.7 17.7 select_add_fusion.2
  1103.8 17.4 multiply_convert_fusion.21
  1132.5 20.1 select_add_fusion.2
  1153.5 48.2 %reduce-scatter.23.cloned.1.call-done = bf16[2,128,1024]{2,1,0:T(8,128)(2,1)} async-done(((bf16[2,1024,1024]{2,1,0:T(8,128)(2,1)}), bf16[2,128,1024]{2,1,0:T(8,128)(2,1)}) %reduce-scatter.23.cloned.1.call-update) | async-done | bytes 524304 | tf_op jit(solution)/shard_map/reduce_scatter | solution.py:416
  1236.5 13.4 fusion.24
  1311.6 12.4 fusion.18
  1324.0 12.6 fusion.20
  1401.3 11.9 fusion.23
  1445.1 28.8 reduce-scatter.25.cloned.1.call-done
  1517.1 25.5 copy.235
  1568.6 21.0 copy.225
  1605.9 42.2 %scatter_custom_fusion = f32[4017,1024]{1,0:T(8,128)} fusion(s32[4096]{0:T(1024)S(1)} %bitcast.737, bf16[4096,1024]{1,0:T(8,128)(2,1)} %bitcast.644, f32[]{:T(128)} %constant.89.clone.1), kind=kCustom, calls=%fused_computation.33 | custom fusion | flops 8388608 | bytes 24842244 | tf_op jit(solution)/shard_map/scatter-add | solution.py:436
  1648.1 15.0 fusion.31
  1690.0 138.6 %all-reduce.9.cloned.1.call-done = f32[2,1024,2048]{2,0,1:T(2,128)} async-done(((f32[2,1024,2048]{2,0,1:T(2,128)}), f32[2,1024,2048]{2,0,1:T(2,128)}) %all-reduce.9.cloned.1.call-update) | async-done | bytes 16777232
  1829.7 143.9 %reduce-scatter.29.cloned.1.call-done = f32[1,32,1024]{2,1,0:T(8,128)} async-done(((f32[1,1024,1024]{2,1,0:T(8,128)}), f32[1,32,1024]{2,1,0:T(8,128)}) %reduce-scatter.29.cloned.1.call-update) | async-done | bytes 131088 | tf_op jit(solution)/shard_map/reduce_scatter | solution.py:359
  1974.5 149.4 %reduce-scatter.31.cloned.1.call-done = f32[2,32,1024]{2,1,0:T(8,128)} async-done(((f32[2,1024,1024]{2,1,0:T(8,128)}), f32[2,32,1024]{2,1,0:T(8,128)}) %reduce-scatter.31.cloned.1.call-update) | async-done | bytes 262160 | tf_op jit(solution)/shard_map/reduce_scatter | solution.py:359
  2125.6 133.2 %reduce-scatter.45.cloned.1.call-done = f32[32,3]{1,0:T(8,128)} async-done(((f32[1024,3]{1,0:T(8,128)}), f32[32,3]{1,0:T(8,128)}) %reduce-scatter.45.cloned.1.call-update) | async-done | bytes 400
  2259.6 132.1 %reduce-scatter.47.cloned.1.call-done = f32[32,4]{1,0:T(8,128)} async-done(((f32[1024,4]{1,0:T(8,128)}), f32[32,4]{1,0:T(8,128)}) %reduce-scatter.47.cloned.1.call-update) | async-done | bytes 528
  2393.1 179.0 %all-reduce.7.cloned.1.call-done = f32[1,1024,2048]{2,0,1:T(1,128)} async-done(((f32[1,1024,2048]{2,0,1:T(1,128)}), f32[1,1024,2048]{2,0,1:T(1,128)}) %all-reduce.7.cloned.1.call-update) | async-done | bytes 8388624
  2575.5 159.0 %reduce-scatter.37.cloned.1.call-done = f32[1,88,1024]{2,1,0:T(8,128)} async-done(((f32[1,2816,1024]{2,1,0:T(8,128)}), f32[1,88,1024]{2,1,0:T(8,128)}) %reduce-scatter.37.cloned.1.call-update) | async-done | bytes 360464 | tf_op jit(solution)/shard_map/reduce_scatter | solution.py:359
  2735.6 159.0 %reduce-scatter.39.cloned.1.call-done = f32[1,88,1024]{2,1,0:T(8,128)} async-done(((f32[1,2816,1024]{2,1,0:T(8,128)}), f32[1,88,1024]{2,1,0:T(8,128)}) %reduce-scatter.39.cloned.1.call-update) | async-done | bytes 360464 | tf_op jit(solution)/shard_map/reduce_scatter | solution.py:359
  2896.3 85.4 %reduce-scatter.41.cloned.1.call-done = bf16[4016,256]{1,0:T(8,128)(2,1)} async-done(((bf16[4016,1024]{1,0:T(8,128)(2,1)}), bf16[4016,256]{1,0:T(8,128)(2,1)}) %reduce-scatter.41.cloned.1.call-update) | async-done | bytes 2056208 | tf_op jit(solution)/shard_map/reduce_scatter | solution.py:441
  2985.0 250.8 %reduce-scatter.33.cloned.1.call-done = f32[1,32,5632]{2,1,0:T(8,128)} async-done(((f32[1,1024,5632]{2,1,0:T(8,128)}), f32[1,32,5632]{2,1,0:T(8,128)}) %reduce-scatter.33.cloned.1.call-update) | async-done | bytes 720912 | tf_op jit(solution)/shard_map/reduce_scatter | solution.py:359
  3237.0 249.5 %reduce-scatter.35.cloned.1.call-done = f32[1,32,5632]{2,1,0:T(8,128)} async-done(((f32[1,1024,5632]{2,1,0:T(8,128)}), f32[1,32,5632]{2,1,0:T(8,128)}) %reduce-scatter.35.cloned.1.call-update) | async-done | bytes 720912 | tf_op jit(solution)/shard_map/reduce_scatter | solution.py:359
  3491.2 37.2 %all-reduce.3 = (f32[]{:T(128)}, f32[]{:T(128)}) all-reduce(f32[]{:T(128)} %multiply_reduce_fusion.19, f32[]{:T(128)S(6)} %add.421), channel_id=1, replica_groups=mesh['dp'=4,'mp'=8] {'dp','mp'}, use_global_device_ids=true, to_apply=%region_22.23 | all-reduce | flops 2 | bytes 16 | tf_op jit(solution)/shard_map/psum | solution.py:451
  (627 shorter events, 615.1 us)
Async XLA Ops:
  8.0 92.7 %all-gather.23.cloned.1.call-start = ((), (), s32[]{:S(2)}) async-start(), calls=%async_computation.14 | async-start | bytes 10280960 | tf_op jit(solution)/shard_map/all_gather | solution.py:328
  11.8 220.2 %reduce-scatter.21.cloned.1.call-start = ((), (), s32[]{:S(2)}) async-start(), calls=%async_computation.15 | async-start | bytes 9437184 | tf_op jit(solution)/shard_map/reduce_scatter | solution.py:338
  133.2 119.3 %all-gather.31.cloned.1.call-start = ((), (), s32[]{:S(2)}) async-start(), calls=%async_computation.19 | async-start | bytes 4325376 | tf_op jit(solution)/shard_map/all_gather | solution.py:353
  135.0 197.3 %all-gather.25.cloned.1.call-start = ((), (), s32[]{:S(2)}) async-start(), calls=%async_computation.16 | async-start | bytes 8650752 | tf_op jit(solution)/shard_map/all_gather | solution.py:353
  135.8 243.9 %all-gather.33.cloned.1.call-start = ((), (), s32[]{:S(2)}) async-start(), calls=%async_computation.20 | async-start | bytes 4718592 | tf_op jit(solution)/shard_map/all_gather | solution.py:74
  216.4 315.6 %copy-start.91 = (f32[1,1024]{1,0:T(1,128)}, f32[1,1024]{1,0:T(1,128)S(1)}, u32[]{:S(2)}) copy-start(f32[1,1024]{1,0:T(1,128)S(1)} %get-tuple-element.525) | copy-start | bytes 12292
  217.0 637.3 %copy-start.94 = (f32[1,1024]{1,0:T(1,128)}, f32[1,1024]{1,0:T(1,128)S(1)}, u32[]{:S(2)}) copy-start(f32[1,1024]{1,0:T(1,128)S(1)} %get-tuple-element.521) | copy-start | bytes 12292
  233.5 480.1 %copy-start.3 = (f32[2,2,128,1024]{3,2,1,0:T(8,128)}, f32[2,2,128,1024]{3,2,1,0:T(8,128)S(1)}, u32[]{:S(2)}) copy-start(f32[2,2,128,1024]{3,2,1,0:T(8,128)S(1)} %convert_element_type.256) | copy-start | bytes 6291460
  255.8 183.0 %all-gather.35.cloned.1.call-start = ((), (), s32[]{:S(2)}) async-start(), calls=%async_computation.21 | async-start | bytes 2162688 | tf_op jit(solution)/shard_map/all_gather | solution.py:353
  258.2 273.8 %all-gather.37.cloned.1.call-start = ((), (), s32[]{:S(2)}) async-start(), calls=%async_computation.22 | async-start | bytes 11894784 | tf_op jit(solution)/shard_map/all_gather | solution.py:353
  259.3 342.5 %all-gather.39.cloned.1.call-start = ((), (), s32[]{:S(2)}) async-start(), calls=%async_computation.23 | async-start | bytes 5947392 | tf_op jit(solution)/shard_map/all_gather | solution.py:353
  261.3 78.3 %copy-start.71 = (bf16[2,128,1024]{2,1,0:T(8,128)(2,1)S(1)}, bf16[2,128,1024]{2,1,0:T(8,128)(2,1)}, u32[]{:S(2)}) copy-start(bf16[2,128,1024]{2,1,0:T(8,128)(2,1)} %get-tuple-element.515) | copy-start | bytes 1572868
  261.3 387.9 %all-gather.27.cloned.1.call-start = ((), (), s32[]{:S(2)}) async-start(), calls=%async_computation.17 | async-start | bytes 4718592 | tf_op jit(solution)/shard_map/all_gather | solution.py:74
  341.2 372.4 %all-gather.29.cloned.1.call-start = ((), (), s32[]{:S(2)}) async-start(), calls=%async_computation.18 | async-start | bytes 4325376 | tf_op jit(solution)/shard_map/all_gather | solution.py:353
  341.9 419.3 %all-gather.41.cloned.1.call-start = ((), (), s32[]{:S(2)}) async-start(), calls=%async_computation.24 | async-start | bytes 4718592 | tf_op jit(solution)/shard_map/all_gather | solution.py:74
  441.4 160.5 %copy-start.11 = (f32[2,128,1024]{2,1,0:T(8,128)}, f32[2,128,1024]{2,1,0:T(8,128)S(1)}, u32[]{:S(2)}) copy-start(f32[2,128,1024]{2,1,0:T(8,128)S(1)} %get-tuple-element.548) | copy-start | bytes 3145732
  442.0 96.1 %copy-start.114 = (f32[2,128]{1,0:T(2,128)}, f32[2,128]{1,0:T(2,128)S(1)}, u32[]{:S(2)}) copy-start(f32[2,128]{1,0:T(2,128)S(1)} %get-tuple-element.536) | copy-start | bytes 3076
  542.7 65.1 %copy-start.131 = (f32[1,1024]{1,0:T(1,128)S(1)}, f32[1,1024]{1,0:T(1,128)}, u32[]{:S(2)}) copy-start(f32[1,1024]{1,0:T(1,128)} %get-tuple-element.524) | copy-start | bytes 12292
  609.4 244.9 %all-gather.43.cloned.1.call-start = ((), (), s32[]{:S(2)}) async-start(), calls=%async_computation.25 | async-start | bytes 11894784 | tf_op jit(solution)/shard_map/all_gather | solution.py:353
  610.1 313.9 %all-gather.45.cloned.1.call-start = ((), (), s32[]{:S(2)}) async-start(), calls=%async_computation.26 | async-start | bytes 5947392 | tf_op jit(solution)/shard_map/all_gather | solution.py:353
  610.7 365.7 %all-gather.47.cloned.1.call-start = ((), (), s32[]{:S(2)}) async-start(), calls=%async_computation.27 | async-start | bytes 4718592 | tf_op jit(solution)/shard_map/all_gather | solution.py:365
  610.9 70.4 %copy-start.44 = (pred[128,1024]{0,1:T(8,128)(4,1)}, pred[128,1024]{0,1:T(8,128)(4,1)S(1)}, u32[]{:S(2)}) copy-start(pred[128,1024]{0,1:T(8,128)(4,1)S(1)} %iota_compare_fusion) | copy-start | bytes 393220
  716.3 83.1 %copy-start.17 = (f32[2,128,1024]{2,1,0:T(8,128)}, f32[2,128,1024]{2,1,0:T(8,128)S(1)}, u32[]{:S(2)}) copy-start(f32[2,128,1024]{2,1,0:T(8,128)S(1)} %get-tuple-element.552) | copy-start | bytes 3145732
  800.2 123.8 %copy-start.14 = (f32[2,128,1024]{2,1,0:T(8,128)}, f32[2,128,1024]{2,1,0:T(8,128)S(1)}, u32[]{:S(2)}) copy-start(f32[2,128,1024]{2,1,0:T(8,128)S(1)} %get-tuple-element.556) | copy-start | bytes 3145732
  863.9 64.5 %copy-start.46 = (bf16[2,128,2816]{2,1,0:T(8,128)(2,1)}, bf16[2,128,2816]{2,1,0:T(8,128)(2,1)S(1)}, u32[]{:S(2)}) copy-start(bf16[2,128,2816]{2,1,0:T(8,128)(2,1)S(1)} %multiply_convert_fusion.3) | copy-start | bytes 4325380
  863.9 65.6 %copy-start.112 = (f32[1,1024]{1,0:T(1,128)S(1)}, f32[1,1024]{1,0:T(1,128)}, u32[]{:S(2)}) copy-start(f32[1,1024]{1,0:T(1,128)} %get-tuple-element.520) | copy-start | bytes 12292
  863.9 66.7 %copy-start.160 = (s32[8]{0:T(128)S(1)}, s32[8]{0:T(128)}, u32[]{:S(2)}) copy-start(s32[8]{0:T(128)} %param.29) | copy-start | bytes 100
  864.0 112.4 %copy-start.104 = (s32[2,1024]{1,0:T(2,128)S(1)}, s32[2,1024]{1,0:T(2,128)}, u32[]{:S(2)}) copy-start(s32[2,1024]{1,0:T(2,128)} %param.28) | copy-start | bytes 24580
  930.5 271.2 %reduce-scatter.23.cloned.1.call-start = ((), (), s32[]{:S(2)}) async-start(), calls=%async_computation.28 | async-start | bytes 4718592 | tf_op jit(solution)/shard_map/reduce_scatter | solution.py:416
  976.4 77.8 %copy-start.111 = (f32[2,1024]{1,0:T(2,128)S(1)}, f32[2,1024]{1,0:T(2,128)}, u32[]{:S(2)}) copy-start(f32[2,1024]{1,0:T(2,128)} %compare_convert_fusion) | copy-start | bytes 24580
  1152.8 196.1 %reduce-scatter.43.cloned.1.call-start = ((), (), s32[]{:S(2)}) async-start(), calls=%async_computation.39 | async-start | bytes 4718592
  1286.1 147.1 %reduce-scatter.27.cloned.1.call-start = ((), (), s32[]{:S(2)}) async-start(), calls=%async_computation.30 | async-start | bytes 4718592 | tf_op jit(solution)/shard_map/reduce_scatter | solution.py:172
  1348.9 125.0 %reduce-scatter.25.cloned.1.call-start = ((), (), s32[]{:S(2)}) async-start(), calls=%async_computation.29 | async-start | bytes 4718592 | tf_op jit(solution)/shard_map/reduce_scatter | solution.py:172
  1425.7 180.2 %all-gather.49.cloned.1.call-start = ((), (), s32[]{:S(2)}) async-start(), calls=%async_computation.37 | async-start | bytes 9437184 | tf_op jit(solution)/shard_map/all_gather | solution.py:434
  1481.6 347.0 %all-reduce.9.cloned.1.call-start = ((), (), s32[]{:S(2)}) async-start(), calls=%async_computation.43 | async-start | bytes 33554432
  1542.7 430.9 %reduce-scatter.29.cloned.1.call-start = ((), (), s32[]{:S(2)}) async-start(), calls=%async_computation.31 | async-start | bytes 4325376 | tf_op jit(solution)/shard_map/reduce_scatter | solution.py:359
  1548.0 575.9 %reduce-scatter.31.cloned.1.call-start = ((), (), s32[]{:S(2)}) async-start(), calls=%async_computation.32 | async-start | bytes 8650752 | tf_op jit(solution)/shard_map/reduce_scatter | solution.py:359
  1556.1 702.7 %reduce-scatter.45.cloned.1.call-start = ((), (), s32[]{:S(2)}) async-start(), calls=%async_computation.40 | async-start | bytes 540672
  1560.9 830.8 %reduce-scatter.47.cloned.1.call-start = ((), (), s32[]{:S(2)}) async-start(), calls=%async_computation.41 | async-start | bytes 540672
  1562.1 1010.0 %all-reduce.7.cloned.1.call-start = ((), (), s32[]{:S(2)}) async-start(), calls=%async_computation.42 | async-start | bytes 16777216
  1589.6 1144.9 %reduce-scatter.37.cloned.1.call-start = ((), (), s32[]{:S(2)}) async-start(), calls=%async_computation.35 | async-start | bytes 11894784 | tf_op jit(solution)/shard_map/reduce_scatter | solution.py:359
  1597.6 1296.9 %reduce-scatter.39.cloned.1.call-start = ((), (), s32[]{:S(2)}) async-start(), calls=%async_computation.36 | async-start | bytes 11894784 | tf_op jit(solution)/shard_map/reduce_scatter | solution.py:359
  1605.1 1376.6 %reduce-scatter.41.cloned.1.call-start = ((), (), s32[]{:S(2)}) async-start(), calls=%async_computation.38 | async-start | bytes 10280960 | tf_op jit(solution)/shard_map/reduce_scatter | solution.py:441
  1663.1 1572.7 %reduce-scatter.33.cloned.1.call-start = ((), (), s32[]{:S(2)}) async-start(), calls=%async_computation.33 | async-start | bytes 23789568 | tf_op jit(solution)/shard_map/reduce_scatter | solution.py:359
  1676.0 1810.5 %reduce-scatter.35.cloned.1.call-start = ((), (), s32[]{:S(2)}) async-start(), calls=%async_computation.34 | async-start | bytes 23789568 | tf_op jit(solution)/shard_map/reduce_scatter | solution.py:359
  2575.5 953.6 %copy-start.140 = (f32[7,32]{1,0:T(8,128)S(1)}, f32[7,32]{1,0:T(8,128)}, u32[]{:S(2)}) copy-start(f32[7,32]{1,0:T(8,128)} %param.35) | copy-start | bytes 2692
  2575.5 953.6 %copy-start.156 = (f32[7,32]{1,0:T(8,128)S(1)}, f32[7,32]{1,0:T(8,128)}, u32[]{:S(2)}) copy-start(f32[7,32]{1,0:T(8,128)} %param.47) | copy-start | bytes 2692
  2575.5 953.6 %copy-start.157 = (f32[7,32]{1,0:T(8,128)S(1)}, f32[7,32]{1,0:T(8,128)}, u32[]{:S(2)}) copy-start(f32[7,32]{1,0:T(8,128)} %param.41) | copy-start | bytes 2692
  (152 other events, 1426.8 us)
Sparse Core Ops, SparseCore 0:
  11.9 88.7 all-gather.22
  133.3 98.6 reduce-scatter.20
  930.7 45.6 all-gather.46
  1152.9 48.7 reduce-scatter.22
  1286.2 48.1 reduce-scatter.42
  1349.0 48.0 reduce-scatter.26
  1425.8 48.0 reduce-scatter.24
  1481.7 80.4 all-gather.48
Sparse Core Ops, SparseCore 1:
  137.2 115.2 all-gather.30
  256.0 76.2 all-gather.24
  334.4 45.3 all-gather.32
  383.4 55.4 all-gather.34
  442.2 89.7 all-gather.36
  535.5 66.3 all-gather.38
  603.9 45.3 all-gather.26
  652.7 60.7 all-gather.28
  715.6 45.5 all-gather.40
  764.6 89.6 all-gather.42
  857.6 66.3 all-gather.44
  1542.8 285.8 all-reduce.8
  1830.7 142.8 reduce-scatter.28
  1975.9 148.0 reduce-scatter.30
  2126.7 132.0 reduce-scatter.44
  2261.7 129.9 reduce-scatter.46
  2397.4 174.6 all-reduce.6
  2574.4 160.1 reduce-scatter.36
  2736.7 157.7 reduce-scatter.38
  2897.7 83.9 reduce-scatter.40
  2983.9 251.8 reduce-scatter.32
  3238.0 248.5 reduce-scatter.34
where the time goes:
time: 3570 us; the launch traced here: 3560 us
  waiting for transfers between devices  2510 us (70%)
  matrix products  422 us (12%)
  other arithmetic  237 us (7%)
  local copies, waits for them, and re-layouts  204 us (6%)
  blocking collectives  159 us (4%)
    reduce_scatter x6, waiting for transfers between devices, reduce_grads(): lax.psum_scatter(layer_grads, ('dp', 'mp'), scatter_dimension=1, tiled=True)  1110 us
    unnamed x35, waiting for transfers between devices  585 us
    all_gather x8, waiting for transfers between devices, fetch_layer(): lax.all_gather(as_sent(owned_shards(plan)), ('dp', 'mp'), axis=1, tiled=T...  392 us
    all_gather x3, waiting for transfers between devices, project_keys(): lax.all_gather(own_rows.astype(jnp.bfloat16), 'mp', axis=1, tiled=True)  113 us
    all_gather x1, waiting for transfers between devices, on_device(): lax.all_gather(table.astype(jnp.bfloat16), 'dp', axis=1, tiled=True)  88.2 us
    reduce_scatter x1, waiting for transfers between devices, on_device(): lax.psum_scatter((head_table + lookup_grad).astype(jnp.bfloat16), 'dp', s...  85.4 us
    all_gather x2, blocking collectives, fetch_layer(): lax.all_gather(as_sent(owned_shards(plan)), ('dp', 'mp'), axis=1, tiled=T...  79.6 us
  transfers between devices with their start and end apart: 30, of which 27 were waited for; matrix products, arithmetic and copies ran while one was open for 15% of the time, Pallas kernels for 0%

commit v1 on v0

v1 whole, which is shorter than its diff:
```python
from functools import partial

import jax
import jax.numpy as jnp
from jax import lax
from jax.sharding import Mesh
from jax.sharding import PartitionSpec as P

D = 1024
HQ = 16
HK = 8
HD = 64
FF = 2816
LEN = 1024
QW = 1024
KW = 512
PARAMS = 59644928

MOMENTUM = 0.9
AVERAGE = 0.9
CLIP = 0.0002
EPS = 1e-06

BF = jnp.bfloat16
F32 = jnp.float32


def step_rates():
    base_rate = 3.5 * PARAMS**0.5 / CLIP
    return (
        base_rate * D ** (-0.5),
        base_rate * max(QW // LEN, 1) ** (-0.5),
        base_rate * D ** (-0.5),
        base_rate * FF ** (-0.5),
        base_rate * 2.0,
        base_rate * 0.3,
    )


def swap(value, axis):
    return lax.ppermute(value, axis, [(0, 1), (1, 0)])


def take_bit(value, bit, position):
    return lax.dynamic_index_in_dim(value, bit, position, keepdims=False)


def gather_blocks(block, layout, order):
    have = []
    held = block
    for axis in order:
        received = swap(held, axis)
        position = sum(layout.index(other) < layout.index(axis) for other in have)
        bit = lax.axis_index(axis)
        shape = held.shape
        joined = jnp.zeros(shape[:position] + (2,) + shape[position:], held.dtype)
        joined = lax.dynamic_update_index_in_dim(joined, held, bit, position)
        held = lax.dynamic_update_index_in_dim(joined, received, 1 - bit, position)
        have.append(axis)
    return held


def sum_blocks(terms, layout, order, last=F32):
    left = list(layout)
    held = terms
    for axis in order:
        position = left.index(axis)
        bit = lax.axis_index(axis)
        received = swap(take_bit(held, 1 - bit, position), axis)
        held = take_bit(held, bit, position).astype(F32) + received.astype(F32)
        left.remove(axis)
        if left:
            held = held.astype(terms.dtype)
    return held.astype(last)


def mm(left, right):
    return jnp.dot(left, right, preferred_element_type=F32)


def mm_nt(left, right):
    return lax.dot_general(left, right, (((1,), (1,)), ((), ())), preferred_element_type=F32)


def mm_tn(left, right):
    return lax.dot_general(left, right, (((0,), (0,)), ((), ())), preferred_element_type=F32)


def norm_forward(stream, gain_row):
    inverse = lax.rsqrt(jnp.mean(stream * stream, axis=-1, keepdims=True) + EPS)
    return stream * inverse * gain_row


def norm_backward(stream, gain_row, grad_out):
    inverse = lax.rsqrt(jnp.mean(stream * stream, axis=-1, keepdims=True) + EPS)
    scaled = grad_out * gain_row
    d_input = inverse * scaled - stream * inverse**3 * jnp.mean(
        stream * scaled, axis=-1, keepdims=True
    )
    return (d_input, jnp.sum(grad_out * stream * inverse, axis=0))


def head_split(queries, keyvals):
    rows, length = queries.shape[0], keyvals.shape[0]
    query_heads = queries.reshape(rows, HK, HQ // HK, HD)
    key_heads = keyvals[:, :KW].reshape(length, HK, HD)
    value_heads = keyvals[:, KW:].reshape(length, HK, HD)
    return (query_heads, key_heads, value_heads)


def scores_of(query_heads, key_heads, first_row):
    scores = jnp.einsum(
        "rhgd,khd->hgrk", query_heads, key_heads, preferred_element_type=F32
    ) * HD ** (-0.5)
    if first_row is not None:
        rows, length = query_heads.shape[0], key_heads.shape[0]
        allowed = (first_row + jnp.arange(rows))[:, None] >= jnp.arange(length)[None, :]
        scores = jnp.where(allowed, scores, -1000000000.0)
    return scores


def attend_forward(queries, keyvals, first_row):
    query_heads, key_heads, value_heads = head_split(queries, keyvals)
    scores = scores_of(query_heads, key_heads, first_row)
    row_max = jnp.max(scores, axis=-1, keepdims=True)
    expo_terms = jnp.exp(scores - row_max)
    row_total = jnp.sum(expo_terms, axis=-1, keepdims=True)
    attn_probs = (expo_terms / row_total).astype(BF)
    mixed = jnp.einsum("hgrk,khd->rhgd", attn_probs, value_heads, preferred_element_type=F32)
    return (mixed.reshape(queries.shape[0], QW).astype(BF), row_max + jnp.log(row_total))


def attend_backward(queries, keyvals, first_row, log_total, d_mixed):
    rows, length = queries.shape[0], keyvals.shape[0]
    query_heads, key_heads, value_heads = head_split(queries, keyvals)
    attn_probs = jnp.exp(scores_of(query_heads, key_heads, first_row) - log_total)
    d_heads = d_mixed.reshape(rows, HK, HQ // HK, HD)
    d_probs = jnp.einsum("rhgd,khd->hgrk", d_heads, value_heads, preferred_element_type=F32)
    d_scores = attn_probs * (d_probs - jnp.sum(attn_probs * d_probs, axis=-1, keepdims=True))
    d_scores = d_scores.astype(BF)
    d_queries = jnp.einsum(
        "hgrk,khd->rhgd", d_scores, key_heads, preferred_element_type=F32
    ) * HD ** (-0.5)
    d_keys = jnp.einsum(
        "hgrk,rhgd->khd", d_scores, query_heads, preferred_element_type=F32
    ) * HD ** (-0.5)
    d_values = jnp.einsum(
        "hgrk,rhgd->khd", attn_probs.astype(BF), d_heads, preferred_element_type=F32
    )
    d_keyvals = jnp.concatenate(
        [d_keys.reshape(length, KW).astype(BF), d_values.reshape(length, KW).astype(BF)], axis=-1
    )
    return (d_queries.reshape(rows, QW).astype(BF), d_keyvals)


def update(weight, gradient, moment, average, rate, factor):
    clipped = gradient * factor
    moment_new = MOMENTUM * moment + (1 - MOMENTUM) * clipped
    weight_new = weight - rate * ((1 - MOMENTUM) * clipped + MOMENTUM * moment_new)
    average_new = AVERAGE * average + (1 - AVERAGE) * weight_new
    return (weight_new, moment_new, average_new)


def on_device(
    dp_axes,
    mp_axes,
    source_ids,
    target_ids,
    prefix,
    attn_in,
    attn_out,
    ff_in,
    ff_out,
    table,
    gains,
    attn_in_mom,
    attn_out_mom,
    ff_in_mom,
    ff_out_mom,
    table_mom,
    gains_mom,
    attn_in_avg,
    attn_out_avg,
    ff_in_avg,
    ff_out_avg,
    table_avg,
    gains_avg,
):
    every = dp_axes + mp_axes
    core = mp_axes[-1]
    row_axes = mp_axes[1:]
    line = mp_axes[:-1]
    gather_orders = (
        line + dp_axes + (core,),
        line + dp_axes[::-1] + (core,),
        dp_axes + line + (core,),
    )
    sum_orders = tuple(order[::-1] for order in gather_orders)
    two_dp, two_mp, two_rows = (2,) * len(dp_axes), (2,) * len(mp_axes), (2,) * len(row_axes)

    seq_count, length = source_ids.shape
    rows = length // 2 ** len(row_axes)
    first_row = lax.axis_index(row_axes) * rows

    def whole(shard, kind):
        got = gather_blocks(shard.astype(BF), every, gather_orders[kind])
        return got.reshape((-1,) + shard.shape[1:])

    gain_all = gather_blocks(gains.astype(BF).T, every, gather_orders[0])
    gain_all = gain_all.reshape(-1, gains.shape[0]).T.astype(F32)

    a_in = [None] * 3
    a_out = [None] * 3
    gate = [None] * 2
    up = [None] * 2
    down = [None] * 2
    a_in[0] = whole(attn_in[0], 0)
    a_out[0] = whole(attn_out[0], 1)
    a_in[1] = whole(attn_in[1], 2)
    gate[0] = whole(ff_in[0, :, :FF], 0)
    up[0] = whole(ff_in[0, :, FF:], 1)
    down[0] = whole(ff_out[0], 2)
    a_out[1] = whole(attn_out[1], 0)
    a_in[2] = whole(attn_in[2], 1)
    a_out[2] = whole(attn_out[2], 2)
    gate[1] = whole(ff_in[1, :, :FF], 0)
    up[1] = whole(ff_in[1, :, FF:], 1)
    down[1] = whole(ff_out[1], 2)

    vocab_part = table.shape[0]
    offset = lax.axis_index(mp_axes) * vocab_part
    table_bf = table.astype(BF)
    decoder_ids = jnp.concatenate(
        [jnp.zeros((seq_count, 1), jnp.int32), target_ids[:, :-1]], axis=1
    )
    ids_all = gather_blocks(jnp.stack([source_ids, decoder_ids]), dp_axes, dp_axes)
    ids_all = jnp.moveaxis(ids_all, len(dp_axes), 0).reshape(2, -1)
    local_ids = ids_all - offset
    inside = (local_ids >= 0) & (local_ids < vocab_part)

    def embed(which):
        found = jnp.where(
            inside[which][:, None],
            table_bf[jnp.clip(local_ids[which], 0, vocab_part - 1)],
            jnp.zeros((), BF),
        )
        width = found.shape[-1]
        found = found.reshape(two_dp + two_mp + (rows, width))
        found = sum_blocks(found, dp_axes + mp_axes, mp_axes[::-1], BF)
        for position, axis in enumerate(dp_axes):
            bit = lax.axis_index(axis)
            received = swap(take_bit(found, 1 - bit, position), axis)
            kept = take_bit(found, bit, position)
            found = jnp.stack(
                [jnp.where(bit == 0, kept, received), jnp.where(bit == 0, received, kept)],
                axis=position,
            )
        found = found.reshape(-1, rows, width)
        return jnp.moveaxis(found, 0, 1).reshape(rows, -1).astype(F32)

    stream_e = embed(0)
    stream_d = embed(1)

    table_rows = gather_blocks(table_bf, dp_axes, dp_axes[::-1]).reshape(-1, *table.shape)
    table_rows = jnp.moveaxis(table_rows, 0, 1).reshape(vocab_part, -1)

    def spread_keys(own):
        return gather_blocks(own, row_axes, row_axes).reshape(length, -1)

    def attention_forward(stream, source, block, gain_row, start):
        normed = norm_forward(stream, gain_row).astype(BF)
        anchor = normed if source is None else source
        keyvals = spread_keys(mm(anchor, a_in[block][:, QW:]).astype(BF))
        queries = mm(normed, a_in[block][:, :QW]).astype(BF)
        mixed, log_total = attend_forward(queries, keyvals, start)
        out = stream + mm(mixed, a_out[block])
        return (out, (stream, normed, anchor, queries, keyvals, mixed, log_total))

    def ffn_forward(stream, which, gain_row):
        normed = norm_forward(stream, gain_row).astype(BF)
        gate_part = mm(normed, gate[which])
        up_part = mm(normed, up[which])
        hidden_act = (jax.nn.gelu(gate_part, approximate=True) * up_part).astype(BF)
        return (stream + mm(hidden_act, down[which]), (stream, normed, gate_part, up_part))

    stream_e, enc_attn = attention_forward(stream_e, None, 0, gain_all[0], None)
    stream_d, dec_self = attention_forward(stream_d, None, 1, gain_all[3], first_row)
    stream_e, enc_ffn = ffn_forward(stream_e, 0, gain_all[1])
    encoded = norm_forward(stream_e, gain_all[2]).astype(BF)
    stream_d, dec_cross = attention_forward(stream_d, encoded, 2, gain_all[4], None)
    stream_d, dec_ffn = ffn_forward(stream_d, 1, gain_all[5])
    hidden = norm_forward(stream_d, gain_all[6]).astype(BF)

    hidden_all = gather_blocks(hidden, mp_axes, mp_axes).reshape(-1, hidden.shape[-1])
    targets = target_ids.reshape(-1)
    vocab_ids = offset + jnp.arange(vocab_part)
    hits = vocab_ids[None, :] == targets[:, None]
    logits = mm_nt(hidden_all, table_rows) * D ** (-0.5)
    own_max = jnp.max(logits, axis=-1)
    expo = jnp.exp(logits - own_max[:, None])
    stats = jnp.stack(
        [own_max, jnp.sum(expo, axis=-1), jnp.sum(jnp.where(hits, logits, 0.0), axis=-1)]
    )
    expo = expo.astype(BF)
    for axis in mp_axes[::-1]:
        other = swap(stats, axis)
        joint = jnp.maximum(stats[0], other[0])
        stats = jnp.stack(
            [
                joint,
                stats[1] * jnp.exp(stats[0] - joint) + other[1] * jnp.exp(other[0] - joint),
                stats[2] + other[2],
            ]
        )
    log_norm = stats[0] + jnp.log(stats[1])
    prefix_group = lax.dynamic_slice_in_dim(prefix, lax.axis_index(dp_axes) * seq_count, seq_count)
    scored = (jnp.arange(length)[None, :] >= prefix_group[:, None]).astype(F32).reshape(-1)
    scored_count = jnp.sum((length - prefix).astype(F32))
    scale = jnp.exp(own_max - log_norm)
    d_logits = (
        (expo.astype(F32) * scale[:, None] - hits.astype(F32)) * (scored / scored_count)[:, None]
    ).astype(BF)
    d_final = (mm(d_logits, table_rows) * D ** (-0.5)).astype(BF)
    d_final = sum_blocks(d_final.reshape(two_mp + (rows, -1)), mp_axes, mp_axes[::-1])

    head_table = (mm_tn(d_logits, hidden_all) * D ** (-0.5)).astype(BF)
    half = vocab_part // 2
    width = table.shape[1]

    def table_sum(part, order):
        stacked = jnp.stack(jnp.split(part, 2 ** len(dp_axes), axis=1))
        return sum_blocks(stacked.reshape(two_dp + part.shape[:1] + (width,)), dp_axes, order)

    grad_table = jnp.concatenate(
        [table_sum(head_table[:half], dp_axes), table_sum(head_table[half:], dp_axes[::-1])], axis=0
    )

    def own_sum(gradient, kind):
        blocks = gradient.astype(BF).reshape((2,) * len(every) + (-1,) + gradient.shape[1:])
        return sum_blocks(blocks, every, sum_orders[kind])

    def ffn_backward(saved, which, gain_row, d_stream):
        stream, normed, gate_part, up_part = saved
        activated, gelu_pull = jax.vjp(partial(jax.nn.gelu, approximate=True), gate_part)
        hidden_act = (activated * up_part).astype(BF)
        d_branch = d_stream.astype(BF)
        d_hidden = mm_nt(d_branch, down[which])
        d_gate = gelu_pull(d_hidden * up_part)[0].astype(BF)
        d_up = (d_hidden * activated).astype(BF)
        d_normed = mm_nt(d_gate, gate[which]) + mm_nt(d_up, up[which])
        grads = (
            own_sum(mm_tn(normed, d_gate), 0),
            own_sum(mm_tn(normed, d_up), 1),
            own_sum(mm_tn(hidden_act, d_branch), 2),
        )
        d_input, grad_gain = norm_backward(stream, gain_row, d_normed)
        return (d_stream + d_input, grads, grad_gain)

    def attention_backward(saved, cross, block, gain_row, start, d_stream, kinds):
        stream, normed, anchor, queries, keyvals, mixed, log_total = saved
        d_branch = d_stream.astype(BF)
        d_mixed = mm_nt(d_branch, a_out[block]).astype(BF)
        d_queries, d_keyvals = attend_backward(queries, keyvals, start, log_total, d_mixed)
        d_keyvals = sum_blocks(
            d_keyvals.reshape(two_rows + (rows, -1)), row_axes, row_axes[::-1], BF
        )
        d_normed = mm_nt(d_queries, a_in[block][:, :QW])
        d_anchor = mm_nt(d_keyvals, a_in[block][:, QW:])
        if not cross:
            d_normed = d_normed + d_anchor
        grads = (
            own_sum(mm_tn(normed, d_queries), kinds[0]),
            own_sum(mm_tn(anchor, d_keyvals), kinds[1]),
            own_sum(mm_tn(mixed, d_branch), kinds[2]),
        )
        d_input, grad_gain = norm_backward(stream, gain_row, d_normed)
        return (d_stream + d_input, d_anchor, grads, grad_gain)

    d_y, gain6 = norm_backward(stream_d, gain_all[6], d_final)
    d_y, ffn_grads1, gain5 = ffn_backward(dec_ffn, 1, gain_all[5], d_y)
    d_y, d_encoded, attn_grads2, gain4 = attention_backward(
        dec_cross, True, 2, gain_all[4], None, d_y, (0, 1, 2)
    )
    d_y, _, attn_grads1, gain3 = attention_backward(
        dec_self, False, 1, gain_all[3], first_row, d_y, (1, 2, 0)
    )
    d_x, gain2 = norm_backward(stream_e, gain_all[2], d_encoded)
    d_x, ffn_grads0, gain1 = ffn_backward(enc_ffn, 0, gain_all[1], d_x)
    d_x, _, attn_grads0, gain0 = attention_backward(
        enc_attn, False, 0, gain_all[0], None, d_x, (0, 1, 2)
    )

    def spread_rows(d_rows):
        width = table.shape[1]
        piece = jnp.moveaxis(d_rows.astype(BF).reshape(rows, -1, width), 1, 0)
        piece = piece.reshape(two_dp + (rows, width))
        for position, axis in enumerate(dp_axes):
            bit = lax.axis_index(axis)
            received = swap(take_bit(piece, 1 - bit, position), axis)
            kept = take_bit(piece, bit, position)
            piece = jnp.stack(
                [jnp.where(bit == 0, kept, received), jnp.where(bit == 0, received, kept)],
                axis=position,
            )
        piece = piece.reshape((-1, rows, width))
        everyone = gather_blocks(piece, mp_axes, mp_axes)
        everyone = everyone.reshape((2 ** len(mp_axes), -1, rows, width))
        return jnp.moveaxis(everyone, 0, 1).reshape(-1, width)

    def look_back(which, d_rows):
        segment_ids = jnp.where(inside[which], local_ids[which], vocab_part)
        return jax.ops.segment_sum(
            spread_rows(d_rows).astype(F32), segment_ids, num_segments=vocab_part + 1
        )[:vocab_part]

    grad_table = grad_table + look_back(1, d_y) + look_back(0, d_x)

    gain_grads = jnp.stack([gain0, gain1, gain2, gain3, gain4, gain5, gain6])
    gain_blocks = jnp.moveaxis(gain_grads.reshape(gains.shape[0], -1, gains.shape[1]), 1, 0)
    grad_gains = sum_blocks(
        gain_blocks.reshape((2,) * len(every) + gains.shape), every, sum_orders[0]
    )

    attn_grads = (attn_grads0, attn_grads1, attn_grads2)
    gradients = (
        jnp.stack([jnp.concatenate([g[0], g[1]], axis=1) for g in attn_grads]),
        jnp.stack([g[2] for g in attn_grads]),
        jnp.stack([jnp.concatenate([g[0], g[1]], axis=1) for g in (ffn_grads0, ffn_grads1)]),
        jnp.stack([g[2] for g in (ffn_grads0, ffn_grads1)]),
        grad_table,
        grad_gains,
    )

    own_losses = ((log_norm - stats[2]) * scored).reshape(2 ** len(mp_axes), rows)
    loss_part = jnp.sum(take_bit(own_losses, lax.axis_index(mp_axes), 0))
    squares = sum((jnp.sum(gradient * gradient) for gradient in gradients))
    totals = jnp.stack([loss_part, squares])
    for axis in every[::-1]:
        totals = totals + swap(totals, axis)
    loss_sum = totals[0]
    grad_norm = jnp.sqrt(totals[1])
    factor = jnp.minimum(1.0, CLIP / grad_norm)
    weights = (attn_in, attn_out, ff_in, ff_out, table, gains)
    moments = (attn_in_mom, attn_out_mom, ff_in_mom, ff_out_mom, table_mom, gains_mom)
    averages = (attn_in_avg, attn_out_avg, ff_in_avg, ff_out_avg, table_avg, gains_avg)
    results = [
        update(weight, gradient, moment, average, rate, factor)
        for weight, gradient, moment, average, rate in zip(
            weights, gradients, moments, averages, step_rates()
        )
    ]
    return (loss_sum, scored_count, grad_norm) + tuple(
        results[array][kind] for kind in range(3) for array in range(6)
    )


def solution(mesh):
    dp_count, mp_count = mesh.shape["dp"], mesh.shape["mp"]
    dp_axes = tuple(f"d{k}" for k in range(dp_count.bit_length() - 1))
    mp_axes = tuple(f"m{k}" for k in range(mp_count.bit_length() - 1))
    every = dp_axes + mp_axes
    fine = Mesh(mesh.devices.reshape((2,) * len(every)), every)
    rows_split = P(None, every, None)
    params = (rows_split,) * 4 + (P(mp_axes, dp_axes), P(None, every))
    in_specs = (P(dp_axes, None), P(dp_axes, None), P()) + params * 3
    out_specs = (P(), P(), P()) + params * 3
    return jax.shard_map(
        partial(on_device, dp_axes, mp_axes),
        mesh=fine,
        in_specs=in_specs,
        out_specs=out_specs,
        check_vma=False,
    )
```

time: 3570 us -> 2130 us (0.60)
  waiting for transfers between devices: 2510 us -> 829 us
  local copies, waits for them, and re-layouts: 204 us -> 481 us
  blocking collectives: 159 us -> 0 us
  starting transfers between devices: 2.27 us -> 153 us
  matrix products: 422 us -> 308 us
  other arithmetic: 237 us -> 336 us
    reduce_scatter x11 -> x0, waiting for transfers between devices: 1290 us -> none  [the longest x6 1110 us: reduce_grads(): lax.psum_scatter(layer_grads, ('dp', 'mp'), scatter_dimension=1, tiled=True)]
    ppermute x0 -> x199, waiting for transfers between devices: none -> 829 us  [swap(): return lax.ppermute(value, axis, [(0, 1), (1, 0)])]
    all_gather x14 -> x0, waiting for transfers between devices: 637 us -> none  [the longest x8 392 us: fetch_layer(): lax.all_gather(as_sent(owned_shards(plan)), ('dp', 'mp'), axis=1, tiled=T...]
    unnamed x35 -> x0, waiting for transfers between devices: 585 us -> none
    ppermute x0 -> x199, starting transfers between devices: none -> 153 us  [swap(): return lax.ppermute(value, axis, [(0, 1), (1, 0)])]
    dynamic_update_slice x6 -> x154, local copies, waits for them, and re-layouts: 0.32 us -> 131 us  [the longest x80 79.5 us: gather_blocks(): held = lax.dynamic_update_index_in_dim(joined, received, 1 - bit, position)]
    all_gather x5 -> x0, blocking collectives: 122 us -> none  [the longest x2 79.6 us: fetch_layer(): lax.all_gather(as_sent(owned_shards(plan)), ('dp', 'mp'), axis=1, tiled=T...]
    dot_general x65 -> x66, matrix products: 422 us -> 308 us  [the longest x16 59.5 us: mm_nt(): lax.dot_general(left, right, (((1,), (1,)), ((), ())), preferred_element_...]
  transfers between devices with their start and end apart: 30 -> 199, of which waited for: 27 -> 104; matrix products, arithmetic and copies ran while one was open for 15% -> 37% of each run, Pallas kernels for 0% -> 0%
where the time goes in v1:
time: 2130 us; the launch traced here: 2120 us
  waiting for transfers between devices  829 us (39%)
  local copies, waits for them, and re-layouts  481 us (23%)
  other arithmetic  336 us (16%)
  matrix products  308 us (14%)
  starting transfers between devices  153 us (7%)
    ppermute x199, waiting for transfers between devices, swap(): return lax.ppermute(value, axis, [(0, 1), (1, 0)])  829 us
    ppermute x199, starting transfers between devices, swap(): return lax.ppermute(value, axis, [(0, 1), (1, 0)])  153 us
    scatter-add x2, other arithmetic, look_back(): jax.ops.segment_sum(spread_rows(d_rows).astype(F32), segment_ids, num_seg...  107 us
    dynamic_update_slice x80, local copies, waits for them, and re-layouts, gather_blocks(): held = lax.dynamic_update_index_in_dim(joined, received, 1 - bit, position)  79.5 us
    gather x2, local copies, waits for them, and re-layouts, embed(): table_bf[jnp.clip(local_ids[which], 0, vocab_part - 1)]  66.2 us
    unnamed x763, local copies, waits for them, and re-layouts  61.8 us
    convert_element_type x73, other arithmetic, sum_blocks(): held = held.astype(terms.dtype)  59.6 us
    dot_general x16, matrix products, mm_nt(): lax.dot_general(left, right, (((1,), (1,)), ((), ())), preferred_element_...  59.5 us
  transfers between devices with their start and end apart: 199, of which 104 were waited for; matrix products, arithmetic and copies ran while one was open for 37% of the time, Pallas kernels for 0%

profile of v1, /device:TPU:0, one launch (start us, length us, event | category | flops | bytes accessed | tf_op | source)
XLA Modules:
  0.0 2122.7 jit_solution(17382685217843722400)
XLA Ops:
  61.1 33.1 %gather_fusion.1 = bf16[8192,256]{1,0:T(8,128)(2,1)} fusion(bf16[4016,256]{1,0:T(8,128)(2,1)S(1)} %get-tuple-element.75, s32[8192]{0:T(1024)S(1)} %broadcast_clamp_fusion), kind=kCustom, calls=%fused_computation.1 | custom fusion | bytes 8421376 | tf_op jit(solution)/shard_map/gather | solution.py:244
  101.4 33.1 %gather_fusion = bf16[8192,256]{1,0:T(8,128)(2,1)} fusion(bf16[4016,256]{1,0:T(8,128)(2,1)S(1)} %get-tuple-element.75, s32[8192]{0:T(1024)S(1)} %broadcast_clamp_fusion.1), kind=kCustom, calls=%fused_computation | custom fusion | bytes 8421376 | tf_op jit(solution)/shard_map/gather | solution.py:244
  207.7 12.6 collective-permute-done.65
  283.8 8.5 collective-permute-done.75
  292.8 29.4 %collective-permute-done.53 = bf16[2,2,88,1024]{3,2,1,0:T(8,128)(2,1)S(1)} collective-permute-done((bf16[2,2,88,1024]{3,2,1,0:T(8,128)(2,1)S(1)}, bf16[2,2,88,1024]{3,2,1,0:T(8,128)(2,1)S(1)}, u32[]{:S(2)}, u32[]{:S(2)}) %collective-permute-start.53) | collective-permute-done | bytes 720928 | tf_op jit(solution)/shard_map/ppermute | solution.py:41
  389.0 22.7 %collective-permute-done.54 = bf16[2,2,2,88,1024]{4,3,2,1,0:T(8,128)(2,1)} collective-permute-done((bf16[2,2,2,88,1024]{4,3,2,1,0:T(8,128)(2,1)S(1)}, bf16[2,2,2,88,1024]{4,3,2,1,0:T(8,128)(2,1)}, u32[]{:S(2)}, u32[]{:S(2)}) %collective-permute-start.54) | collective-permute-done | bytes 1441824 | tf_op jit(solution)/shard_map/ppermute | solution.py:41
  425.2 13.0 collective-permute-done.49
  457.8 17.5 collective-permute-done.25
  475.7 24.6 %collective-permute-done.3 = bf16[2,2,2,256,256]{4,3,2,1,0:T(8,128)(2,1)S(1)} collective-permute-done((bf16[2,2,2,256,256]{4,3,2,1,0:T(8,128)(2,1)S(1)}, bf16[2,2,2,256,256]{4,3,2,1,0:T(8,128)(2,1)S(1)}, u32[]{:S(2)}, u32[]{:S(2)}) %collective-permute-start.3) | collective-permute-done | bytes 1048608 | tf_op jit(solution)/shard_map/ppermute | solution.py:41
  504.2 18.6 collective-permute-done.4
  620.7 9.1 bitcast_reduce_fusion.1
  629.8 8.8 fusion.20
  676.7 8.1 fusion.19
  713.1 8.7 fusion.21
  743.1 25.8 %collective-permute-done.83 = bf16[256,1024]{1,0:T(8,128)(2,1)S(1)} collective-permute-done((bf16[256,1024]{1,0:T(8,128)(2,1)S(1)}, bf16[256,1024]{1,0:T(8,128)(2,1)S(1)}, u32[]{:S(2)}, u32[]{:S(2)}) %collective-permute-start.83) | collective-permute-done | bytes 524320 | tf_op jit(solution)/shard_map/ppermute | solution.py:41
  769.5 24.1 %collective-permute-done.84 = bf16[2,256,1024]{2,1,0:T(8,128)(2,1)S(1)} collective-permute-done((bf16[2,256,1024]{2,1,0:T(8,128)(2,1)S(1)}, bf16[2,256,1024]{2,1,0:T(8,128)(2,1)S(1)}, u32[]{:S(2)}, u32[]{:S(2)}) %collective-permute-start.84) | collective-permute-done | bytes 1048608 | tf_op jit(solution)/shard_map/ppermute | solution.py:41
  829.1 23.9 %multiply_reduce_fusion = (f32[2048]{0:T(1024)S(1)}, f32[2048,4016]{0,1:T(8,128)}) fusion(bf16[2048,1024]{1,0:T(8,128)(2,1)} %bitcast.314, bf16[4016,1024]{0,1:T(8,128)(2,1)S(1)} %bitcast.1707), kind=kOutput, calls=%fused_computation.13 | convolution fusion | flops 16860772352 | bytes 45326336 | tf_op jit(solution)/shard_map/dot_general | solution.py:82
  853.0 15.6 fusion.5
  879.4 16.2 fusion.3
  895.7 20.7 multiply_convert_fusion
  924.4 24.0 %multiply_convert_fusion.1 = bf16[2048,1024]{1,0:T(8,128)(2,1)} fusion(bf16[2048,4016]{0,1:T(8,128)(2,1)S(1)} %fusion.3, bf16[4016,1024]{0,1:T(8,128)(2,1)} %bitcast.1706), kind=kOutput, calls=%fused_computation.58 | convolution fusion | flops 16848519168 | bytes 28868608 | tf_op jit(solution)/shard_map/dot_general | solution.py:78
  960.0 8.7 collective-permute-done.175
  977.6 28.6 %collective-permute-done.177 = bf16[2,2008,256]{2,1,0:T(8,128)(2,1)} collective-permute-done((bf16[2,2008,256]{2,1,0:T(8,128)(2,1)}, bf16[2,2008,256]{2,1,0:T(8,128)(2,1)}, u32[]{:S(2)}, u32[]{:S(2)}) %collective-permute-start.177) | collective-permute-done | bytes 2056224 | tf_op jit(solution)/shard_map/ppermute | solution.py:41
  1013.5 13.2 collective-permute-done.176
  1034.9 21.1 collective-permute-done.93
  1073.8 9.1 fusion.129
  1082.9 13.2 fusion.12
  1115.5 9.6 fusion.137
  1125.1 16.0 fusion.6
  1262.7 10.0 fusion.133
  1272.7 11.6 fusion.9
  1303.5 11.8 fusion.11
  1387.6 11.7 collective-permute-done.142
  1460.6 23.5 %collective-permute-done.181 = bf16[4,256,256]{2,1,0:T(8,128)(2,1)S(1)} collective-permute-done((bf16[4,256,256]{2,1,0:T(8,128)(2,1)S(1)}, bf16[4,256,256]{2,1,0:T(8,128)(2,1)S(1)}, u32[]{:S(2)}, u32[]{:S(2)}) %collective-permute-start.181) | collective-permute-done | bytes 524320 | tf_op jit(solution)/shard_map/ppermute | solution.py:41
  1504.6 17.8 collective-permute-done.102
  1564.2 16.9 collective-permute-done.192
  1610.3 31.6 %collective-permute-done.133 = bf16[2,32,1024]{2,1,0:T(8,128)(2,1)S(1)} collective-permute-done((bf16[2,32,1024]{2,1,0:T(8,128)(2,1)S(1)}, bf16[2,32,1024]{2,1,0:T(8,128)(2,1)S(1)}, u32[]{:S(2)}, u32[]{:S(2)}) %collective-permute-start.133) | collective-permute-done | bytes 131104 | tf_op jit(solution)/shard_map/ppermute | solution.py:41
  1690.3 17.8 collective-permute-done.186
  1717.4 24.3 %collective-permute-done.161 = bf16[2,2,2,32,2816]{4,3,1,2,0:T(8,128)(2,1)S(1)} collective-permute-done((bf16[2,2,2,32,2816]{4,3,1,2,0:T(8,128)(2,1)S(1)}, bf16[2,2,2,32,2816]{4,3,1,2,0:T(8,128)(2,1)S(1)}, u32[]{:S(2)}, u32[]{:S(2)}) %collective-permute-start.161) | collective-permute-done | bytes 1441824 | tf_op jit(solution)/shard_map/ppermute | solution.py:41
  1772.7 8.6 collective-permute-done.162
  1786.5 28.9 %collective-permute-done.106 = bf16[2,32,1024]{2,1,0:T(8,128)(2,1)S(1)} collective-permute-done((bf16[2,32,1024]{2,1,0:T(8,128)(2,1)S(1)}, bf16[2,32,1024]{2,1,0:T(8,128)(2,1)S(1)}, u32[]{:S(2)}, u32[]{:S(2)}) %collective-permute-start.106) | collective-permute-done | bytes 131104 | tf_op jit(solution)/shard_map/ppermute | solution.py:41
  1849.6 11.0 collective-permute-done.159
  1881.1 53.1 %scatter_custom_fusion = f32[4017,256]{1,0:T(8,128)} fusion(s32[8192]{0:T(1024)} %bitcast.1867, f32[8192,256]{1,0:T(8,128)} %bitcast.1705, f32[]{:T(128)} %constant.1062.clone.1), kind=kCustom, calls=%fused_computation.234 | custom fusion | flops 2097152 | bytes 4113920 | tf_op jit(solution)/shard_map/scatter-add | solution.py:412
  1942.4 26.6 %collective-permute-done.167 = bf16[2,2,88,1024]{3,2,0,1:T(8,128)(2,1)S(1)} collective-permute-done((bf16[2,2,88,1024]{3,2,0,1:T(8,128)(2,1)S(1)}, bf16[2,2,88,1024]{3,2,0,1:T(8,128)(2,1)S(1)}, u32[]{:S(2)}, u32[]{:S(2)}) %collective-permute-start.167) | collective-permute-done | bytes 720928 | tf_op jit(solution)/shard_map/ppermute | solution.py:41
  1982.7 9.8 collective-permute-done.153
  1993.6 9.3 collective-permute-done.154
  2017.3 53.6 %scatter_custom_fusion.1 = f32[4017,256]{1,0:T(8,128)} fusion(s32[8192]{0:T(1024)} %bitcast.1866, f32[8192,256]{1,0:T(8,128)} %bitcast.1704, f32[]{:T(128)} %constant.1062.clone.1), kind=kCustom, calls=%fused_computation.232 | custom fusion | flops 2097152 | bytes 4113920 | tf_op jit(solution)/shard_map/scatter-add | solution.py:412
  2108.7 11.7 multiply_add_fusion
  (1853 shorter events, 1199.9 us)
Async XLA Ops:
  2.9 51.1 %collective-permute-start = (s32[2,2,1024]{2,1,0:T(2,128)}, s32[2,2,1024]{2,1,0:T(2,128)}, u32[]{:S(2)}, u32[]{:S(2)}) collective-permute-start(s32[2,2,1024]{2,1,0:T(2,128)} %pad_add_fusion), channel_id=1, source_target_pairs={{0,16},{16,0},{1,17},{17,1},{2,18},{18,2},{3,19},{19,3},{4,20},{20... | collective-permute-start | bytes 49160 | tf_op jit(solution)/shard_map/ppermute | solution.py:41
  11.0 143.4 %collective-permute-start.29 = (bf16[32,2048]{1,0:T(8,128)(2,1)}, bf16[32,2048]{1,0:T(8,128)(2,1)}, u32[]{:S(2)}, u32[]{:S(2)}) collective-permute-start(bf16[32,2048]{1,0:T(8,128)(2,1)} %get-tuple-element.141), channel_id=1, source_target_pairs={{0,4},{4,0},{1,5},{5,1},{2,6},{6,2},{3,7},{7,3},{8,12},{12,8},{9,1... | collective-permute-start | bytes 393224 | tf_op jit(solution)/shard_map/ppermute | solution.py:41
  11.3 147.0 %collective-permute-start.56 = (bf16[32,2048]{1,0:T(8,128)(2,1)}, bf16[32,2048]{1,0:T(8,128)(2,1)}, u32[]{:S(2)}, u32[]{:S(2)}) collective-permute-start(bf16[32,2048]{1,0:T(8,128)(2,1)} %get-tuple-element.142), channel_id=1, source_target_pairs={{0,4},{4,0},{1,5},{5,1},{2,6},{6,2},{3,7},{7,3},{8,12},{12,8},{9,1... | collective-permute-start | bytes 393224 | tf_op jit(solution)/shard_map/ppermute | solution.py:41
  15.8 124.1 %collective-permute-start.36 = (bf16[32,1024]{1,0:T(8,128)(2,1)}, bf16[32,1024]{1,0:T(8,128)(2,1)}, u32[]{:S(2)}, u32[]{:S(2)}) collective-permute-start(bf16[32,1024]{1,0:T(8,128)(2,1)} %get-tuple-element.157), channel_id=1, source_target_pairs={{0,4},{4,0},{1,5},{5,1},{2,6},{6,2},{3,7},{7,3},{8,12},{12,8},{9,1... | collective-permute-start | bytes 196616 | tf_op jit(solution)/shard_map/ppermute | solution.py:41
  48.4 94.7 %collective-permute-start.63 = (bf16[32,1024]{1,0:T(8,128)(2,1)}, bf16[32,1024]{1,0:T(8,128)(2,1)}, u32[]{:S(2)}, u32[]{:S(2)}) collective-permute-start(bf16[32,1024]{1,0:T(8,128)(2,1)} %get-tuple-element.156), channel_id=1, source_target_pairs={{0,16},{16,0},{1,17},{17,1},{2,18},{18,2},{3,19},{19,3},{4,20},{20... | collective-permute-start | bytes 196616 | tf_op jit(solution)/shard_map/ppermute | solution.py:41
  58.6 318.4 %collective-permute-start.86 = (bf16[4016,256]{1,0:T(8,128)(2,1)S(1)}, bf16[4016,256]{1,0:T(8,128)(2,1)}, u32[]{:S(2)}, u32[]{:S(2)}) collective-permute-start(bf16[4016,256]{1,0:T(8,128)(2,1)S(1)} %get-tuple-element.75), channel_id=1, source_target_pairs={{0,8},{8,0},{1,9},{9,1},{2,10},{10,2},{3,11},{11,3},{4,12},{12,4},... | collective-permute-start | bytes 6168584 | tf_op jit(solution)/shard_map/ppermute | solution.py:41
  176.3 205.2 %collective-permute-start.24 = (bf16[2,2,2,2,256,256]{5,4,3,2,1,0:T(8,128)(2,1)}, bf16[2,2,2,2,256,256]{5,4,3,2,1,0:T(8,128)(2,1)}, u32[]{:S(2)}, u32[]{:S(2)}) collective-permute-start(bf16[2,2,2,2,256,256]{5,4,3,2,1,0:T(8,128)(2,1)} %dynamic-slice_bitcast_fusion), channel_id=1, source_target_pairs={{0,1},{1,0},{2,3},{3,2},{4,5},{5,4},{6,7},{7,6},{8,9},{9,8},{10,11... | collective-permute-start | bytes 6291464 | tf_op jit(solution)/shard_map/ppermute | solution.py:41
  276.8 49.7 %collective-permute-start.48 = (bf16[2,2,32,2816]{3,2,1,0:T(8,128)(2,1)S(1)}, bf16[2,2,32,2816]{3,2,1,0:T(8,128)(2,1)S(1)}, u32[]{:S(2)}, u32[]{:S(2)}) collective-permute-start(bf16[2,2,32,2816]{3,2,1,0:T(8,128)(2,1)S(1)} %bitcast_dynamic-update-slice_fusion.105), channel_id=1, source_target_pairs={{0,8},{8,0},{1,9},{9,1},{2,10},{10,2},{3,11},{11,3},{4,12},{12,4},... | collective-permute-start | bytes 2162696 | tf_op jit(solution)/shard_map/ppermute | solution.py:41
  279.0 43.2 %collective-permute-start.53 = (bf16[2,2,88,1024]{3,2,1,0:T(8,128)(2,1)S(1)}, bf16[2,2,88,1024]{3,2,1,0:T(8,128)(2,1)S(1)}, u32[]{:S(2)}, u32[]{:S(2)}) collective-permute-start(bf16[2,2,88,1024]{3,2,1,0:T(8,128)(2,1)S(1)} %bitcast_dynamic-update-slice_fusion.108), channel_id=1, source_target_pairs={{0,4},{4,0},{1,5},{5,1},{2,6},{6,2},{3,7},{7,3},{8,12},{12,8},{9,1... | collective-permute-start | bytes 2162696 | tf_op jit(solution)/shard_map/ppermute | solution.py:41
  292.3 43.0 %collective-permute-start.80 = (bf16[2,2,88,1024]{3,2,1,0:T(8,128)(2,1)S(1)}, bf16[2,2,88,1024]{3,2,1,0:T(8,128)(2,1)S(1)}, u32[]{:S(2)}, u32[]{:S(2)}) collective-permute-start(bf16[2,2,88,1024]{3,2,1,0:T(8,128)(2,1)S(1)} %bitcast_dynamic-update-slice_fusion.98), channel_id=1, source_target_pairs={{0,4},{4,0},{1,5},{5,1},{2,6},{6,2},{3,7},{7,3},{8,12},{12,8},{9,1... | collective-permute-start | bytes 2162696 | tf_op jit(solution)/shard_map/ppermute | solution.py:41
  371.3 46.9 %collective-permute-start.44 = (bf16[2,2,2,32,2816]{4,3,2,1,0:T(8,128)(2,1)S(1)}, bf16[2,2,2,32,2816]{4,3,2,1,0:T(8,128)(2,1)}, u32[]{:S(2)}, u32[]{:S(2)}) collective-permute-start(bf16[2,2,2,32,2816]{4,3,2,1,0:T(8,128)(2,1)S(1)} %bitcast_dynamic-update-slice_fusion.72), channel_id=1, source_target_pairs={{0,8},{8,0},{1,9},{9,1},{2,10},{10,2},{3,11},{11,3},{4,12},{12,4},... | collective-permute-start | bytes 4325384 | tf_op jit(solution)/shard_map/ppermute | solution.py:41
  373.5 48.3 %collective-permute-start.76 = (bf16[2,2,2,32,2816]{4,3,2,1,0:T(8,128)(2,1)S(1)}, bf16[2,2,2,32,2816]{4,3,2,1,0:T(8,128)(2,1)S(1)}, u32[]{:S(2)}, u32[]{:S(2)}) collective-permute-start(bf16[2,2,2,32,2816]{4,3,2,1,0:T(8,128)(2,1)S(1)} %bitcast_dynamic-update-slice_fusion.65), channel_id=1, source_target_pairs={{0,16},{16,0},{1,17},{17,1},{2,18},{18,2},{3,19},{19,3},{4,20},{20... | collective-permute-start | bytes 4325384 | tf_op jit(solution)/shard_map/ppermute | solution.py:41
  381.5 56.7 %collective-permute-start.49 = (bf16[2,2,2,32,2816]{4,3,2,1,0:T(8,128)(2,1)S(1)}, bf16[2,2,2,32,2816]{4,3,2,1,0:T(8,128)(2,1)}, u32[]{:S(2)}, u32[]{:S(2)}) collective-permute-start(bf16[2,2,2,32,2816]{4,3,2,1,0:T(8,128)(2,1)S(1)} %bitcast_dynamic-update-slice_fusion.70), channel_id=1, source_target_pairs={{0,16},{16,0},{1,17},{17,1},{2,18},{18,2},{3,19},{19,3},{4,20},{20... | collective-permute-start | bytes 4325384 | tf_op jit(solution)/shard_map/ppermute | solution.py:41
  385.1 62.5 %collective-permute-start.81 = (bf16[2,2,2,88,1024]{4,3,2,1,0:T(8,128)(2,1)S(1)}, bf16[2,2,2,88,1024]{4,3,2,1,0:T(8,128)(2,1)S(1)}, u32[]{:S(2)}, u32[]{:S(2)}) collective-permute-start(bf16[2,2,2,88,1024]{4,3,2,1,0:T(8,128)(2,1)S(1)} %bitcast_dynamic-update-slice_fusion.62), channel_id=1, source_target_pairs={{0,2},{2,0},{1,3},{3,1},{4,6},{6,4},{5,7},{7,5},{8,10},{10,8},{9,1... | collective-permute-start | bytes 4325384 | tf_op jit(solution)/shard_map/ppermute | solution.py:41
  418.1 122.2 %collective-permute-start.33 = (bf16[2,2,2,2,32,2048]{5,4,3,2,1,0:T(8,128)(2,1)S(1)}, bf16[2,2,2,2,32,2048]{5,4,3,2,1,0:T(8,128)(2,1)}, u32[]{:S(2)}, u32[]{:S(2)}) collective-permute-start(bf16[2,2,2,2,32,2048]{5,4,3,2,1,0:T(8,128)(2,1)S(1)} %bitcast_dynamic-update-slice_fusion.51), channel_id=1, source_target_pairs={{0,1},{1,0},{2,3},{3,2},{4,5},{5,4},{6,7},{7,6},{8,9},{9,8},{10,11... | collective-permute-start | bytes 6291464 | tf_op jit(solution)/shard_map/ppermute | solution.py:41
  421.8 119.0 %collective-permute-start.60 = (bf16[2,2,2,2,32,2048]{5,4,3,2,1,0:T(8,128)(2,1)S(1)}, bf16[2,2,2,2,32,2048]{5,4,3,2,1,0:T(8,128)(2,1)}, u32[]{:S(2)}, u32[]{:S(2)}) collective-permute-start(bf16[2,2,2,2,32,2048]{5,4,3,2,1,0:T(8,128)(2,1)S(1)} %bitcast_dynamic-update-slice_fusion.58), channel_id=1, source_target_pairs={{0,1},{1,0},{2,3},{3,2},{4,5},{5,4},{6,7},{7,6},{8,9},{9,8},{10,11... | collective-permute-start | bytes 6291464 | tf_op jit(solution)/shard_map/ppermute | solution.py:41
  438.2 106.0 %collective-permute-start.16 = (bf16[2,2,2,2,32,2048]{5,4,3,2,1,0:T(8,128)(2,1)S(1)}, bf16[2,2,2,2,32,2048]{5,4,3,2,1,0:T(8,128)(2,1)S(1)}, u32[]{:S(2)}, u32[]{:S(2)}) collective-permute-start(bf16[2,2,2,2,32,2048]{5,4,3,2,1,0:T(8,128)(2,1)S(1)} %bitcast_dynamic-update-slice_fusion.61), channel_id=1, source_target_pairs={{0,1},{1,0},{2,3},{3,2},{4,5},{5,4},{6,7},{7,6},{8,9},{9,8},{10,11... | collective-permute-start | bytes 6291464 | tf_op jit(solution)/shard_map/ppermute | solution.py:41
  448.4 51.9 %collective-permute-start.3 = (bf16[2,2,2,256,256]{4,3,2,1,0:T(8,128)(2,1)S(1)}, bf16[2,2,2,256,256]{4,3,2,1,0:T(8,128)(2,1)S(1)}, u32[]{:S(2)}, u32[]{:S(2)}) collective-permute-start(bf16[2,2,2,256,256]{4,3,2,1,0:T(8,128)(2,1)S(1)} %copy-done.234), channel_id=1, source_target_pairs={{0,2},{2,0},{1,3},{3,1},{4,6},{6,4},{5,7},{7,5},{8,10},{10,8},{9,1... | collective-permute-start | bytes 3145736 | tf_op jit(solution)/shard_map/ppermute | solution.py:41
  503.9 81.2 %collective-permute-start.45 = (bf16[2,2,2,2,32,2816]{5,4,3,2,1,0:T(8,128)(2,1)}, bf16[2,2,2,2,32,2816]{5,4,3,2,1,0:T(8,128)(2,1)}, u32[]{:S(2)}, u32[]{:S(2)}) collective-permute-start(bf16[2,2,2,2,32,2816]{5,4,3,2,1,0:T(8,128)(2,1)} %bitcast_dynamic-update-slice_fusion.37), channel_id=1, source_target_pairs={{0,1},{1,0},{2,3},{3,2},{4,5},{5,4},{6,7},{7,6},{8,9},{9,8},{10,11... | collective-permute-start | bytes 8650760 | tf_op jit(solution)/shard_map/ppermute | solution.py:41
  540.2 60.6 %collective-permute-start.55 = (bf16[2,2,2,2,88,1024]{5,4,3,2,1,0:T(8,128)(2,1)}, bf16[2,2,2,2,88,1024]{5,4,3,2,1,0:T(8,128)(2,1)}, u32[]{:S(2)}, u32[]{:S(2)}) collective-permute-start(bf16[2,2,2,2,88,1024]{5,4,3,2,1,0:T(8,128)(2,1)} %bitcast_dynamic-update-slice_fusion.34), channel_id=1, source_target_pairs={{0,1},{1,0},{2,3},{3,2},{4,5},{5,4},{6,7},{7,6},{8,9},{9,8},{10,11... | collective-permute-start | bytes 8650760 | tf_op jit(solution)/shard_map/ppermute | solution.py:41
  540.3 60.5 %collective-permute-start.82 = (bf16[2,2,2,2,88,1024]{5,4,3,2,1,0:T(8,128)(2,1)}, bf16[2,2,2,2,88,1024]{5,4,3,2,1,0:T(8,128)(2,1)}, u32[]{:S(2)}, u32[]{:S(2)}) collective-permute-start(bf16[2,2,2,2,88,1024]{5,4,3,2,1,0:T(8,128)(2,1)} %bitcast_dynamic-update-slice_fusion.26), channel_id=1, source_target_pairs={{0,1},{1,0},{2,3},{3,2},{4,5},{5,4},{6,7},{7,6},{8,9},{9,8},{10,11... | collective-permute-start | bytes 8650760 | tf_op jit(solution)/shard_map/ppermute | solution.py:41
  540.9 54.7 %collective-permute-start.72 = (bf16[2,2,2,2,32,2816]{5,4,3,2,1,0:T(8,128)(2,1)}, bf16[2,2,2,2,32,2816]{5,4,3,2,1,0:T(8,128)(2,1)}, u32[]{:S(2)}, u32[]{:S(2)}) collective-permute-start(bf16[2,2,2,2,32,2816]{5,4,3,2,1,0:T(8,128)(2,1)} %bitcast_dynamic-update-slice_fusion.28), channel_id=1, source_target_pairs={{0,1},{1,0},{2,3},{3,2},{4,5},{5,4},{6,7},{7,6},{8,9},{9,8},{10,11... | collective-permute-start | bytes 8650760 | tf_op jit(solution)/shard_map/ppermute | solution.py:41
  595.6 214.7 %collective-permute-start.87 = (bf16[2,4016,256]{2,1,0:T(8,128)(2,1)}, bf16[2,4016,256]{2,1,0:T(8,128)(2,1)}, u32[]{:S(2)}, u32[]{:S(2)}) collective-permute-start(bf16[2,4016,256]{2,1,0:T(8,128)(2,1)} %bitcast_dynamic-update-slice_fusion.24), channel_id=1, source_target_pairs={{0,16},{16,0},{1,17},{17,1},{2,18},{18,2},{3,19},{19,3},{4,20},{20... | collective-permute-start | bytes 12337160 | tf_op jit(solution)/shard_map/ppermute | solution.py:41
  600.8 59.2 %collective-permute-start.18 = (bf16[2,256,1024]{2,1,0:T(8,128)(2,1)}, bf16[2,256,1024]{2,1,0:T(8,128)(2,1)}, u32[]{:S(2)}, u32[]{:S(2)}) collective-permute-start(bf16[2,256,1024]{2,1,0:T(8,128)(2,1)} %bitcast_dynamic-update-slice_fusion.95), channel_id=1, source_target_pairs={{0,1},{1,0},{2,3},{3,2},{4,5},{5,4},{6,7},{7,6},{8,9},{9,8},{10,11... | collective-permute-start | bytes 3145736 | tf_op jit(solution)/shard_map/ppermute | solution.py:41
  923.8 44.9 %collective-permute-start.175 = (bf16[2,2008,256]{2,1,0:T(8,128)(2,1)}, bf16[2,2008,256]{2,1,0:T(8,128)(2,1)}, u32[]{:S(2)}, u32[]{:S(2)}) collective-permute-start(bf16[2,2008,256]{2,1,0:T(8,128)(2,1)} %dynamic-slice_bitcast_fusion.3), channel_id=1, source_target_pairs={{0,16},{16,0},{1,17},{17,1},{2,18},{18,2},{3,19},{19,3},{4,20},{20... | collective-permute-start | bytes 6168584 | tf_op jit(solution)/shard_map/ppermute | solution.py:41
  958.2 48.0 %collective-permute-start.177 = (bf16[2,2008,256]{2,1,0:T(8,128)(2,1)}, bf16[2,2008,256]{2,1,0:T(8,128)(2,1)}, u32[]{:S(2)}, u32[]{:S(2)}) collective-permute-start(bf16[2,2008,256]{2,1,0:T(8,128)(2,1)} %dynamic-slice_bitcast_fusion.2), channel_id=1, source_target_pairs={{0,8},{8,0},{1,9},{9,1},{2,10},{10,2},{3,11},{11,3},{4,12},{12,4},... | collective-permute-start | bytes 6168584 | tf_op jit(solution)/shard_map/ppermute | solution.py:41
  972.6 54.1 %collective-permute-start.176 = (bf16[2008,256]{1,0:T(8,128)(2,1)}, bf16[2008,256]{1,0:T(8,128)(2,1)}, u32[]{:S(2)}, u32[]{:S(2)}) collective-permute-start(bf16[2008,256]{1,0:T(8,128)(2,1)} %dynamic-slice_bitcast_fusion.14), channel_id=1, source_target_pairs={{0,8},{8,0},{1,9},{9,1},{2,10},{10,2},{3,11},{11,3},{4,12},{12,4},... | collective-permute-start | bytes 3084296 | tf_op jit(solution)/shard_map/ppermute | solution.py:41
  976.4 53.5 %collective-permute-start.92 = (bf16[2,256,1024]{2,1,0:T(8,128)(2,1)S(1)}, bf16[2,256,1024]{2,1,0:T(8,128)(2,1)}, u32[]{:S(2)}, u32[]{:S(2)}) collective-permute-start(bf16[2,256,1024]{2,1,0:T(8,128)(2,1)S(1)} %dynamic-slice_bitcast_fusion.10), channel_id=1, source_target_pairs={{0,2},{2,0},{1,3},{3,1},{4,6},{6,4},{5,7},{7,5},{8,10},{10,8},{9,1... | collective-permute-start | bytes 3145736 | tf_op jit(solution)/shard_map/ppermute | solution.py:41
  1210.3 283.9 %collective-permute-start.170 = (bf16[2,2,2,2,88,1024]{5,4,0,1,2,3:T(8,128)(2,1)}, bf16[2,2,2,2,88,1024]{5,4,0,1,2,3:T(8,128)(2,1)}, u32[]{:S(2)}, u32[]{:S(2)}) collective-permute-start(bf16[2,2,2,2,88,1024]{5,4,0,1,2,3:T(8,128)(2,1)} %bitcast.1610), channel_id=1, source_target_pairs={{0,1},{1,0},{2,3},{3,2},{4,5},{5,4},{6,7},{7,6},{8,9},{9,8},{10,11... | collective-permute-start | bytes 8650760 | tf_op jit(solution)/shard_map/ppermute | solution.py:41
  1231.6 103.0 %collective-permute-start.114 = (bf16[256,1024]{1,0:T(8,128)(2,1)}, bf16[256,1024]{1,0:T(8,128)(2,1)}, u32[]{:S(2)}, u32[]{:S(2)}) collective-permute-start(bf16[256,1024]{1,0:T(8,128)(2,1)} %dynamic-slice_bitcast_fusion.27), channel_id=1, source_target_pairs={{0,2},{2,0},{1,3},{3,1},{4,6},{6,4},{5,7},{7,5},{8,10},{10,8},{9,1... | collective-permute-start | bytes 1572872 | tf_op jit(solution)/shard_map/ppermute | solution.py:41
  1235.0 116.7 %collective-permute-start.136 = (bf16[2,2,2,32,1024]{4,3,1,2,0:T(8,128)(2,1)}, bf16[2,2,2,32,1024]{4,3,1,2,0:T(8,128)(2,1)}, u32[]{:S(2)}, u32[]{:S(2)}) collective-permute-start(bf16[2,2,2,32,1024]{4,3,1,2,0:T(8,128)(2,1)} %dynamic-slice_bitcast_fusion.22), channel_id=1, source_target_pairs={{0,8},{8,0},{1,9},{9,1},{2,10},{10,2},{3,11},{11,3},{4,12},{12,4},... | collective-permute-start | bytes 1572872 | tf_op jit(solution)/shard_map/ppermute | solution.py:41
  1237.3 119.4 %collective-permute-start.141 = (bf16[2,2,2,32,1024]{4,3,0,1,2:T(8,128)(2,1)}, bf16[2,2,2,32,1024]{4,3,0,1,2:T(8,128)(2,1)}, u32[]{:S(2)}, u32[]{:S(2)}) collective-permute-start(bf16[2,2,2,32,1024]{4,3,0,1,2:T(8,128)(2,1)} %dynamic-slice_bitcast_fusion.21), channel_id=1, source_target_pairs={{0,2},{2,0},{1,3},{3,1},{4,6},{6,4},{5,7},{7,5},{8,10},{10,8},{9,1... | collective-permute-start | bytes 1572872 | tf_op jit(solution)/shard_map/ppermute | solution.py:41
  1244.1 125.5 %collective-permute-start.109 = (bf16[2,2,2,32,1024]{4,3,1,2,0:T(8,128)(2,1)}, bf16[2,2,2,32,1024]{4,3,1,2,0:T(8,128)(2,1)}, u32[]{:S(2)}, u32[]{:S(2)}) collective-permute-start(bf16[2,2,2,32,1024]{4,3,1,2,0:T(8,128)(2,1)} %dynamic-slice_bitcast_fusion.28), channel_id=1, source_target_pairs={{0,16},{16,0},{1,17},{17,1},{2,18},{18,2},{3,19},{19,3},{4,20},{20... | collective-permute-start | bytes 1572872 | tf_op jit(solution)/shard_map/ppermute | solution.py:41
  1351.7 100.8 %collective-permute-start.101 = (bf16[2,256,1024]{2,1,0:T(8,128)(2,1)}, bf16[2,256,1024]{2,1,0:T(8,128)(2,1)}, u32[]{:S(2)}, u32[]{:S(2)}) collective-permute-start(bf16[2,256,1024]{2,1,0:T(8,128)(2,1)} %fusion.175), channel_id=1, source_target_pairs={{0,1},{1,0},{2,3},{3,2},{4,5},{5,4},{6,7},{7,6},{8,9},{9,8},{10,11... | collective-permute-start | bytes 3145736 | tf_op jit(solution)/shard_map/ppermute | solution.py:41
  1369.6 85.0 %collective-permute-start.130 = (bf16[2,2,2,2,32,1024]{5,4,0,1,2,3:T(8,128)(2,1)}, bf16[2,2,2,2,32,1024]{5,4,0,1,2,3:T(8,128)(2,1)}, u32[]{:S(2)}, u32[]{:S(2)}) collective-permute-start(bf16[2,2,2,2,32,1024]{5,4,0,1,2,3:T(8,128)(2,1)} %bitcast.1619), channel_id=1, source_target_pairs={{0,1},{1,0},{2,3},{3,2},{4,5},{5,4},{6,7},{7,6},{8,9},{9,8},{10,11... | collective-permute-start | bytes 3145736 | tf_op jit(solution)/shard_map/ppermute | solution.py:41
  1400.1 49.8 %collective-permute-start.180 = (bf16[2,256,256]{2,1,0:T(8,128)(2,1)S(1)}, bf16[2,256,256]{2,1,0:T(8,128)(2,1)S(1)}, u32[]{:S(2)}, u32[]{:S(2)}) collective-permute-start(bf16[2,256,256]{2,1,0:T(8,128)(2,1)S(1)} %fusion.225), channel_id=1, source_target_pairs={{0,8},{8,0},{1,9},{9,1},{2,10},{10,2},{3,11},{11,3},{4,12},{12,4},... | collective-permute-start | bytes 786440 | tf_op jit(solution)/shard_map/ppermute | solution.py:41
  1454.6 45.1 %collective-permute-start.160 = (bf16[2,2,2,2,32,2816]{5,4,2,3,1,0:T(8,128)(2,1)S(1)}, bf16[2,2,2,2,32,2816]{5,4,2,3,1,0:T(8,128)(2,1)S(1)}, u32[]{:S(2)}, u32[]{:S(2)}) collective-permute-start(bf16[2,2,2,2,32,2816]{5,4,2,3,1,0:T(8,128)(2,1)S(1)} %bitcast.1771), channel_id=1, source_target_pairs={{0,1},{1,0},{2,3},{3,2},{4,5},{5,4},{6,7},{7,6},{8,9},{9,8},{10,11... | collective-permute-start | bytes 8650760 | tf_op jit(solution)/shard_map/ppermute | solution.py:41
  1484.1 265.0 %collective-permute-start.165 = (bf16[2,2,2,2,88,1024]{5,4,0,1,2,3:T(8,128)(2,1)}, bf16[2,2,2,2,88,1024]{5,4,0,1,2,3:T(8,128)(2,1)}, u32[]{:S(2)}, u32[]{:S(2)}) collective-permute-start(bf16[2,2,2,2,88,1024]{5,4,0,1,2,3:T(8,128)(2,1)} %bitcast.1611), channel_id=1, source_target_pairs={{0,1},{1,0},{2,3},{3,2},{4,5},{5,4},{6,7},{7,6},{8,9},{9,8},{10,11... | collective-permute-start | bytes 8650760 | tf_op jit(solution)/shard_map/ppermute | solution.py:41
  1485.0 197.3 %collective-permute-start.182 = (bf16[2,4,256,256]{3,2,1,0:T(8,128)(2,1)}, bf16[2,4,256,256]{3,2,1,0:T(8,128)(2,1)}, u32[]{:S(2)}, u32[]{:S(2)}) collective-permute-start(bf16[2,4,256,256]{3,2,1,0:T(8,128)(2,1)} %bitcast_dynamic-update-slice_fusion.80), channel_id=1, source_target_pairs={{0,2},{2,0},{1,3},{3,1},{4,6},{6,4},{5,7},{7,5},{8,10},{10,8},{9,1... | collective-permute-start | bytes 3145736 | tf_op jit(solution)/shard_map/ppermute | solution.py:41
  1536.5 177.7 %collective-permute-start.171 = (bf16[2,2,2,88,1024]{4,3,0,1,2:T(8,128)(2,1)}, bf16[2,2,2,88,1024]{4,3,0,1,2:T(8,128)(2,1)}, u32[]{:S(2)}, u32[]{:S(2)}) collective-permute-start(bf16[2,2,2,88,1024]{4,3,0,1,2:T(8,128)(2,1)} %dynamic-slice_bitcast_fusion.4), channel_id=1, source_target_pairs={{0,2},{2,0},{1,3},{3,1},{4,6},{6,4},{5,7},{7,5},{8,10},{10,8},{9,1... | collective-permute-start | bytes 4325384 | tf_op jit(solution)/shard_map/ppermute | solution.py:41
  1601.1 115.4 %collective-permute-start.156 = (bf16[2,2,2,32,2816]{4,3,1,2,0:T(8,128)(2,1)S(1)}, bf16[2,2,2,32,2816]{4,3,1,2,0:T(8,128)(2,1)S(1)}, u32[]{:S(2)}, u32[]{:S(2)}) collective-permute-start(bf16[2,2,2,32,2816]{4,3,1,2,0:T(8,128)(2,1)S(1)} %copy-done.219), channel_id=1, source_target_pairs={{0,8},{8,0},{1,9},{9,1},{2,10},{10,2},{3,11},{11,3},{4,12},{12,4},... | collective-permute-start | bytes 4325384 | tf_op jit(solution)/shard_map/ppermute | solution.py:41
  1689.4 52.8 %collective-permute-start.145 = (bf16[2,2,2,2,32,2816]{5,4,2,3,0,1:T(8,128)(2,1)S(1)}, bf16[2,2,2,2,32,2816]{5,4,2,3,0,1:T(8,128)(2,1)S(1)}, u32[]{:S(2)}, u32[]{:S(2)}) collective-permute-start(bf16[2,2,2,2,32,2816]{5,4,2,3,0,1:T(8,128)(2,1)S(1)} %bitcast.1770), channel_id=1, source_target_pairs={{0,1},{1,0},{2,3},{3,2},{4,5},{5,4},{6,7},{7,6},{8,9},{9,8},{10,11... | collective-permute-start | bytes 8650760 | tf_op jit(solution)/shard_map/ppermute | solution.py:41
  1716.6 157.5 %collective-permute-start.183 = (bf16[2,2,4,256,256]{4,3,2,1,0:T(8,128)(2,1)}, bf16[2,2,4,256,256]{4,3,2,1,0:T(8,128)(2,1)}, u32[]{:S(2)}, u32[]{:S(2)}) collective-permute-start(bf16[2,2,4,256,256]{4,3,2,1,0:T(8,128)(2,1)} %bitcast_dynamic-update-slice_fusion.57), channel_id=1, source_target_pairs={{0,1},{1,0},{2,3},{3,2},{4,5},{5,4},{6,7},{7,6},{8,9},{9,8},{10,11... | collective-permute-start | bytes 6291464 | tf_op jit(solution)/shard_map/ppermute | solution.py:41
  1741.7 83.7 %collective-permute-start.187 = (bf16[2,4,256,256]{3,2,1,0:T(8,128)(2,1)}, bf16[2,4,256,256]{3,2,1,0:T(8,128)(2,1)}, u32[]{:S(2)}, u32[]{:S(2)}) collective-permute-start(bf16[2,4,256,256]{3,2,1,0:T(8,128)(2,1)} %bitcast_dynamic-update-slice_fusion.78), channel_id=1, source_target_pairs={{0,2},{2,0},{1,3},{3,1},{4,6},{6,4},{5,7},{7,5},{8,10},{10,8},{9,1... | collective-permute-start | bytes 3145736 | tf_op jit(solution)/shard_map/ppermute | solution.py:41
  1770.8 163.4 %collective-permute-start.166 = (bf16[2,2,2,88,1024]{4,3,0,1,2:T(8,128)(2,1)}, bf16[2,2,2,88,1024]{4,3,0,1,2:T(8,128)(2,1)}, u32[]{:S(2)}, u32[]{:S(2)}) collective-permute-start(bf16[2,2,2,88,1024]{4,3,0,1,2:T(8,128)(2,1)} %dynamic-slice_bitcast_fusion.5), channel_id=1, source_target_pairs={{0,2},{2,0},{1,3},{3,1},{4,6},{6,4},{5,7},{7,5},{8,10},{10,8},{9,1... | collective-permute-start | bytes 4325384 | tf_op jit(solution)/shard_map/ppermute | solution.py:41
  1781.3 155.6 %collective-permute-start.146 = (bf16[2,2,2,32,2816]{4,3,1,2,0:T(8,128)(2,1)}, bf16[2,2,2,32,2816]{4,3,1,2,0:T(8,128)(2,1)}, u32[]{:S(2)}, u32[]{:S(2)}) collective-permute-start(bf16[2,2,2,32,2816]{4,3,1,2,0:T(8,128)(2,1)} %dynamic-slice_bitcast_fusion.9), channel_id=1, source_target_pairs={{0,8},{8,0},{1,9},{9,1},{2,10},{10,2},{3,11},{11,3},{4,12},{12,4},... | collective-permute-start | bytes 4325384 | tf_op jit(solution)/shard_map/ppermute | solution.py:41
  1821.1 118.4 %collective-permute-start.151 = (bf16[2,2,2,32,2816]{4,3,1,2,0:T(8,128)(2,1)}, bf16[2,2,2,32,2816]{4,3,1,2,0:T(8,128)(2,1)}, u32[]{:S(2)}, u32[]{:S(2)}) collective-permute-start(bf16[2,2,2,32,2816]{4,3,1,2,0:T(8,128)(2,1)} %dynamic-slice_bitcast_fusion.8), channel_id=1, source_target_pairs={{0,16},{16,0},{1,17},{17,1},{2,18},{18,2},{3,19},{19,3},{4,20},{20... | collective-permute-start | bytes 4325384 | tf_op jit(solution)/shard_map/ppermute | solution.py:41
  1873.3 133.7 %collective-permute-start.188 = (bf16[2,2,4,256,256]{4,3,2,1,0:T(8,128)(2,1)}, bf16[2,2,4,256,256]{4,3,2,1,0:T(8,128)(2,1)}, u32[]{:S(2)}, u32[]{:S(2)}) collective-permute-start(bf16[2,2,4,256,256]{4,3,2,1,0:T(8,128)(2,1)} %bitcast_dynamic-update-slice_fusion.38), channel_id=1, source_target_pairs={{0,1},{1,0},{2,3},{3,2},{4,5},{5,4},{6,7},{7,6},{8,9},{9,8},{10,11... | collective-permute-start | bytes 6291464 | tf_op jit(solution)/shard_map/ppermute | solution.py:41
  (524 other events, 7631.3 us)

commit v2 on v1

--- a/solution.py
+++ b/solution.py
@@ -3,6 +3,8 @@
 import jax
 import jax.numpy as jnp
 from jax import lax
+from jax.experimental import pallas as pl
+from jax.experimental.pallas import tpu as pltpu
 from jax.sharding import Mesh
 from jax.sharding import PartitionSpec as P
 
@@ -23,6 +25,9 @@
 
 BF = jnp.bfloat16
 F32 = jnp.float32
+MESH = pl.DeviceIdType.MESH
+CHUNK = 256
+LANES = 3
 
 
 def step_rates():
@@ -72,6 +77,200 @@
         if left:
             held = held.astype(terms.dtype)
     return held.astype(last)
+
+
+def greet(axes):
+    barrier = pltpu.get_barrier_semaphore()
+    for axis in axes:
+        pl.semaphore_signal(
+            barrier, inc=1, device_id={axis: 1 - lax.axis_index(axis)}, device_id_type=MESH
+        )
+    pl.semaphore_wait(barrier, len(axes))
+
+
+def gather_kernel(layout, units, lanes, count, *refs):
+    ins, outs = refs[:count], refs[count : 2 * count]
+    own_sem, send_sem, recv_sem = refs[2 * count :]
+    bits = {axis: lax.axis_index(axis) for axis in layout}
+    depth = len(layout)
+
+    def region(unit, have):
+        tensor, start, size, _ = units[unit]
+        blocks = tuple(pl.ds(0, 2) if axis in have else bits[axis] for axis in layout)
+        return outs[tensor].at[blocks + (slice(None), pl.ds(start, size))]
+
+    own = [
+        pltpu.make_async_copy(
+            ins[k], outs[k].at[tuple(bits[axis] for axis in layout)], own_sem.at[k]
+        )
+        for k in range(count)
+    ]
+    for copy in own:
+        copy.start()
+    greet(layout)
+    for copy in own:
+        copy.wait()
+    copies = {}
+    groups = -(-len(units) // lanes)
+    for turn in range(groups + depth - 1):
+        for step in reversed(range(depth)):
+            first = (turn - step) * lanes
+            for unit in range(max(first, 0), min(first + lanes, len(units))):
+                order = units[unit][3]
+                if step:
+                    copies[unit, step - 1].wait_recv()
+                source = region(unit, order[:step])
+                copy = pltpu.make_async_remote_copy(
+                    src_ref=source,
+                    dst_ref=source,
+                    send_sem=send_sem.at[unit, step],
+                    recv_sem=recv_sem.at[unit, step],
+                    device_id={order[step]: 1 - bits[order[step]]},
+                    device_id_type=MESH,
+                )
+                copy.start()
+                copies[unit, step] = copy
+    for unit in range(len(units)):
+        copies[unit, depth - 1].wait_recv()
+    for copy in copies.values():
+        copy.wait_send()
+
+
+def gather_all(shards, layout, orders):
+    units = []
+    for tensor, shard in enumerate(shards):
+        columns = shard.shape[1]
+        pieces = max(1, columns // 1024)
+        step = columns // pieces // 128 * 128
+        starts = [step * piece for piece in range(pieces)] + [columns]
+        for piece in range(pieces):
+            order = orders[len(units) % len(orders)]
+            units.append((tensor, starts[piece], starts[piece + 1] - starts[piece], order))
+    count = len(shards)
+    semaphores = pltpu.SemaphoreType.DMA((len(units), len(layout)))
+    return pl.pallas_call(
+        partial(gather_kernel, layout, tuple(units), LANES, count),
+        out_shape=[
+            jax.ShapeDtypeStruct((2,) * len(layout) + shard.shape, shard.dtype) for shard in shards
+        ],
+        in_specs=[pl.BlockSpec(memory_space=pl.ANY)] * count,
+        out_specs=[pl.BlockSpec(memory_space=pl.ANY)] * count,
+        scratch_shapes=[pltpu.SemaphoreType.DMA((count,)), semaphores, semaphores],
+        compiler_params=pltpu.CompilerParams(collective_id=0, has_side_effects=True),
+        name="gather_weights",
+    )(*shards)
+
+
+def grad_kernel(layout, orders, bounds, chunks, *refs):
+    x_ref, y_ref, out_ref = refs[:3]
+    depth = len(layout)
+    lanes = len(orders)
+    scratch = refs[3:]
+    sends, recvs, helds = (
+        [scratch[kind * lanes * depth + lane * depth :][:depth] for lane in range(lanes)]
+        for kind in range(3)
+    )
+    send_sem, recv_sem = scratch[3 * lanes * depth :]
+    bits = {axis: lax.axis_index(axis) for axis in layout}
+    groups = out_ref.shape[0] // lanes
+    greet(layout)
+
+    def exchange(lane, step, group):
+        axis = orders[lane][step]
+        slot = lax.rem(group, 2)
+        return pltpu.make_async_remote_copy(
+            src_ref=sends[lane][step],
+            dst_ref=recvs[lane][step].at[slot],
+            send_sem=send_sem.at[lane, step],
+            recv_sem=recv_sem.at[lane, step, slot],
+            device_id={axis: 1 - bits[axis]},
+            device_id_type=MESH,
+        )
+
+    def first(lane, group):
+        chunk = jnp.minimum(group * lanes + lane, chunks - 1)
+        which = sum((chunk >= bound).astype(jnp.int32) for bound in bounds) if bounds else 0
+        columns = y_ref[:, pl.ds(pl.multiple_of(chunk * CHUNK, CHUNK), CHUNK)]
+        bit = bits[orders[lane][0]]
+        given = jnp.dot(x_ref[which, 1 - bit], columns, preferred_element_type=F32)
+        sends[lane][0][...] = given.astype(BF).reshape(sends[lane][0].shape)
+        exchange(lane, 0, group).start()
+        kept = jnp.dot(x_ref[which, bit], columns, preferred_element_type=F32)
+        helds[lane][0][...] = kept.reshape(helds[lane][0].shape)
+
+    def later(lane, step, group):
+        order = orders[lane]
+        slot = lax.rem(group, 2)
+        exchange(lane, step - 1, group).wait()
+        held, received = helds[lane][step - 1], recvs[lane][step - 1]
+        if step == depth:
+            out_ref[group * lanes + lane] = held[...] + received[slot].astype(F32)
+            return
+        position = [axis for axis in layout if axis not in order[:step]].index(order[step])
+        bit = bits[order[step]]
+
+        def total(choice):
+            index = (slice(None),) * position + (choice,)
+            return held[index] + received[(slot,) + index].astype(F32)
+
+        sends[lane][step][...] = total(1 - bit).astype(BF)
+        exchange(lane, step, group).start()
+        helds[lane][step][...] = total(bit)
+
+    @pl.loop(0, groups + depth)
+    def _(turn):
+        for step in reversed(range(depth + 1)):
+            group = turn - step
+
+            @pl.when((group >= 0) & (group < groups))
+            def _():
+                for lane in range(lanes):
+                    if step:
+                        later(lane, step, group)
+                    else:
+                        first(lane, group)
+
+
+def grad_sums(lefts, rights, layout, orders, spans, collective):
+    depth, lanes = len(layout), len(orders)
+    tokens, width = lefts[0].shape
+    rows = width // 2**depth
+    padded = -(-rows // 16) * 16
+    blocks = jnp.stack(lefts).transpose(0, 2, 1).reshape(len(lefts), -1, 2, rows, tokens)
+    blocks = jnp.pad(blocks, ((0, 0),) * 3 + ((0, padded - rows), (0, 0)))
+    x = blocks.swapaxes(1, 2).reshape(len(lefts), 2, -1, tokens)
+    y = jnp.concatenate(rights, axis=1)
+    chunks = y.shape[1] // CHUNK
+    groups = -(-chunks // lanes)
+    bounds, passed = [], 0
+    for span in spans[:-1]:
+        passed += span // CHUNK
+        bounds.append(passed)
+    send_shapes, recv_shapes, held_shapes = [], [], []
+    for _ in range(lanes):
+        for step in range(depth):
+            shape = (2,) * (depth - 1 - step) + (padded, CHUNK)
+            send_shapes.append(pltpu.VMEM(shape, BF))
+            recv_shapes.append(pltpu.VMEM((2,) + shape, BF))
+            held_shapes.append(pltpu.VMEM(shape, F32))
+    out = pl.pallas_call(
+        partial(grad_kernel, layout, orders, tuple(bounds), chunks),
+        out_shape=jax.ShapeDtypeStruct((groups * lanes, padded, CHUNK), F32),
+        in_specs=[pl.BlockSpec(memory_space=pltpu.VMEM)] * 2,
+        out_specs=pl.BlockSpec(memory_space=pltpu.VMEM),
+        scratch_shapes=send_shapes
+        + recv_shapes
+        + held_shapes
+        + [
+            pltpu.SemaphoreType.DMA((lanes, depth)),
+            pltpu.SemaphoreType.DMA((lanes, depth, 2)),
+        ],
+        compiler_params=pltpu.CompilerParams(
+            collective_id=collective, has_side_effects=True, vmem_limit_bytes=56 * 1024 * 1024
+        ),
+        name="sum_gradients",
+    )(x, y)
+    return out[:chunks, :rows].transpose(1, 0, 2).reshape(rows, -1)
 
 
 def mm(left, right):
@@ -196,36 +395,30 @@
         dp_axes + line + (core,),
     )
     sum_orders = tuple(order[::-1] for order in gather_orders)
+    last = (line[-1], core)
+    three = (gather_orders[0], gather_orders[1], line[:-1] + dp_axes[::-1] + last)
+    six_orders = three + three[:2] + (line[:-1] + dp_axes + last,)
     two_dp, two_mp, two_rows = (2,) * len(dp_axes), (2,) * len(mp_axes), (2,) * len(row_axes)
 
     seq_count, length = source_ids.shape
     rows = length // 2 ** len(row_axes)
     first_row = lax.axis_index(row_axes) * rows
 
-    def whole(shard, kind):
-        got = gather_blocks(shard.astype(BF), every, gather_orders[kind])
-        return got.reshape((-1,) + shard.shape[1:])
-
+    shards = [attn_in[0], attn_out[0], ff_in[0], ff_out[0]]
+    shards += [attn_in[1], attn_out[1], attn_in[2], attn_out[2], ff_in[1], ff_out[1]]
+    shards = [shard.astype(BF) for shard in shards]
+    in_kernels = attn_in.shape[1] % 16 == 0
+    if in_kernels:
+        full = gather_all(shards, every, six_orders)
+    else:
+        full = [
+            gather_blocks(shard, every, gather_orders[k % 3]) for k, shard in enumerate(shards)
+        ]
+    full = [got.reshape((-1,) + shard.shape[1:]) for got, shard in zip(full, shards)]
+    a_in, a_out = (full[0], full[4], full[6]), (full[1], full[5], full[7])
+    f_in, f_out = (full[2], full[8]), (full[3], full[9])
     gain_all = gather_blocks(gains.astype(BF).T, every, gather_orders[0])
     gain_all = gain_all.reshape(-1, gains.shape[0]).T.astype(F32)
-
-    a_in = [None] * 3
-    a_out = [None] * 3
-    gate = [None] * 2
-    up = [None] * 2
-    down = [None] * 2
-    a_in[0] = whole(attn_in[0], 0)
-    a_out[0] = whole(attn_out[0], 1)
-    a_in[1] = whole(attn_in[1], 2)
-    gate[0] = whole(ff_in[0, :, :FF], 0)
-    up[0] = whole(ff_in[0, :, FF:], 1)
-    down[0] = whole(ff_out[0], 2)
-    a_out[1] = whole(attn_out[1], 0)
-    a_in[2] = whole(attn_in[2], 1)
-    a_out[2] = whole(attn_out[2], 2)
-    gate[1] = whole(ff_in[1, :, :FF], 0)
-    up[1] = whole(ff_in[1, :, FF:], 1)
-    down[1] = whole(ff_out[1], 2)
 
     vocab_part = table.shape[0]
     offset = lax.axis_index(mp_axes) * vocab_part
@@ -278,10 +471,9 @@
 
     def ffn_forward(stream, which, gain_row):
         normed = norm_forward(stream, gain_row).astype(BF)
-        gate_part = mm(normed, gate[which])
-        up_part = mm(normed, up[which])
-        hidden_act = (jax.nn.gelu(gate_part, approximate=True) * up_part).astype(BF)
-        return (stream + mm(hidden_act, down[which]), (stream, normed, gate_part, up_part))
+        both = mm(normed, f_in[which])
+        hidden_act = (jax.nn.gelu(both[:, :FF], approximate=True) * both[:, FF:]).astype(BF)
+        return (stream + mm(hidden_act, f_out[which]), (stream, normed, both, hidden_act))
 
     stream_e, enc_attn = attention_forward(stream_e, None, 0, gain_all[0], None)
     stream_d, dec_self = attention_forward(stream_d, None, 1, gain_all[3], first_row)
@@ -335,28 +527,20 @@
         [table_sum(head_table[:half], dp_axes), table_sum(head_table[half:], dp_axes[::-1])], axis=0
     )
 
-    def own_sum(gradient, kind):
-        blocks = gradient.astype(BF).reshape((2,) * len(every) + (-1,) + gradient.shape[1:])
-        return sum_blocks(blocks, every, sum_orders[kind])
-
     def ffn_backward(saved, which, gain_row, d_stream):
-        stream, normed, gate_part, up_part = saved
-        activated, gelu_pull = jax.vjp(partial(jax.nn.gelu, approximate=True), gate_part)
-        hidden_act = (activated * up_part).astype(BF)
+        stream, normed, both, hidden_act = saved
+        up_part = both[:, FF:]
+        activated, gelu_pull = jax.vjp(partial(jax.nn.gelu, approximate=True), both[:, :FF])
         d_branch = d_stream.astype(BF)
-        d_hidden = mm_nt(d_branch, down[which])
-        d_gate = gelu_pull(d_hidden * up_part)[0].astype(BF)
-        d_up = (d_hidden * activated).astype(BF)
-        d_normed = mm_nt(d_gate, gate[which]) + mm_nt(d_up, up[which])
-        grads = (
-            own_sum(mm_tn(normed, d_gate), 0),
-            own_sum(mm_tn(normed, d_up), 1),
-            own_sum(mm_tn(hidden_act, d_branch), 2),
-        )
+        d_hidden = mm_nt(d_branch, f_out[which])
+        d_both = jnp.concatenate(
+            [gelu_pull(d_hidden * up_part)[0].astype(BF), (d_hidden * activated).astype(BF)], axis=1
+        )
+        d_normed = mm_nt(d_both, f_in[which])
         d_input, grad_gain = norm_backward(stream, gain_row, d_normed)
-        return (d_stream + d_input, grads, grad_gain)
-
-    def attention_backward(saved, cross, block, gain_row, start, d_stream, kinds):
+        return (d_stream + d_input, (normed, d_both, hidden_act, d_branch), grad_gain)
+
+    def attention_backward(saved, cross, block, gain_row, start, d_stream):
         stream, normed, anchor, queries, keyvals, mixed, log_total = saved
         d_branch = d_stream.astype(BF)
         d_mixed = mm_nt(d_branch, a_out[block]).astype(BF)
@@ -368,26 +552,22 @@
         d_anchor = mm_nt(d_keyvals, a_in[block][:, QW:])
         if not cross:
             d_normed = d_normed + d_anchor
-        grads = (
-            own_sum(mm_tn(normed, d_queries), kinds[0]),
-            own_sum(mm_tn(anchor, d_keyvals), kinds[1]),
-            own_sum(mm_tn(mixed, d_branch), kinds[2]),
-        )
+        factors = (normed, anchor, d_queries, d_keyvals, mixed, d_branch)
         d_input, grad_gain = norm_backward(stream, gain_row, d_normed)
-        return (d_stream + d_input, d_anchor, grads, grad_gain)
+        return (d_stream + d_input, d_anchor, factors, grad_gain)
 
     d_y, gain6 = norm_backward(stream_d, gain_all[6], d_final)
-    d_y, ffn_grads1, gain5 = ffn_backward(dec_ffn, 1, gain_all[5], d_y)
-    d_y, d_encoded, attn_grads2, gain4 = attention_backward(
-        dec_cross, True, 2, gain_all[4], None, d_y, (0, 1, 2)
-    )
-    d_y, _, attn_grads1, gain3 = attention_backward(
-        dec_self, False, 1, gain_all[3], first_row, d_y, (1, 2, 0)
+    d_y, ffn_factors1, gain5 = ffn_backward(dec_ffn, 1, gain_all[5], d_y)
+    d_y, d_encoded, attn_factors2, gain4 = attention_backward(
+        dec_cross, True, 2, gain_all[4], None, d_y
+    )
+    d_y, _, attn_factors1, gain3 = attention_backward(
+        dec_self, False, 1, gain_all[3], first_row, d_y
     )
     d_x, gain2 = norm_backward(stream_e, gain_all[2], d_encoded)
-    d_x, ffn_grads0, gain1 = ffn_backward(enc_ffn, 0, gain_all[1], d_x)
-    d_x, _, attn_grads0, gain0 = attention_backward(
-        enc_attn, False, 0, gain_all[0], None, d_x, (0, 1, 2)
+    d_x, ffn_factors0, gain1 = ffn_backward(enc_ffn, 0, gain_all[1], d_x)
+    d_x, _, attn_factors0, gain0 = attention_backward(
+        enc_attn, False, 0, gain_all[0], None, d_x
     )
 
     def spread_rows(d_rows):
@@ -421,12 +601,48 @@
         gain_blocks.reshape((2,) * len(every) + gains.shape), every, sum_orders[0]
     )
 
-    attn_grads = (attn_grads0, attn_grads1, attn_grads2)
+    lefts, rights = [], []
+    for normed, anchor, d_queries, d_keyvals, mixed, d_branch in (
+        attn_factors0,
+        attn_factors1,
+        attn_factors2,
+    ):
+        if anchor is normed:
+            lefts += [normed, mixed]
+            rights += [jnp.concatenate([d_queries, d_keyvals], axis=1), d_branch]
+        else:
+            lefts += [normed, anchor, mixed]
+            rights += [d_queries, d_keyvals, d_branch]
+    wide_lefts, wide_rights = [], []
+    for normed, d_both, hidden_act, d_branch in (ffn_factors0, ffn_factors1):
+        lefts.append(normed)
+        rights.append(d_both)
+        wide_lefts.append(hidden_act)
+        wide_rights.append(d_branch)
+    spans = [right.shape[1] for right in rights]
+    wide_spans = [right.shape[1] for right in wide_rights]
+    if in_kernels:
+        back_orders = tuple(order[::-1] for order in three)
+        own = grad_sums(lefts, rights, every, back_orders, spans, 1)
+        wide = grad_sums(wide_lefts, wide_rights, every, back_orders, wide_spans, 2)
+    else:
+
+        def own_sum(left, right, kind):
+            product = mm_tn(left, right).astype(BF)
+            blocks = product.reshape((2,) * len(every) + (-1,) + product.shape[1:])
+            return sum_blocks(blocks, every, sum_orders[kind % 3])
+
+        pairs = list(enumerate(zip(lefts, rights)))
+        own = jnp.concatenate([own_sum(*pair, k) for k, pair in pairs], axis=1)
+        pairs = list(enumerate(zip(wide_lefts, wide_rights)))
+        wide = jnp.concatenate([own_sum(*pair, k) for k, pair in pairs], axis=1)
+    ends = (attn_in.shape[2], attn_in.shape[2] + attn_out.shape[2])
+    ffn_from = 3 * ends[1]
     gradients = (
-        jnp.stack([jnp.concatenate([g[0], g[1]], axis=1) for g in attn_grads]),
-        jnp.stack([g[2] for g in attn_grads]),
-        jnp.stack([jnp.concatenate([g[0], g[1]], axis=1) for g in (ffn_grads0, ffn_grads1)]),
-        jnp.stack([g[2] for g in (ffn_grads0, ffn_grads1)]),
+        jnp.stack([own[:, ends[1] * k : ends[1] * k + ends[0]] for k in range(3)]),
+        jnp.stack([own[:, ends[1] * k + ends[0] : ends[1] * (k + 1)] for k in range(3)]),
+        jnp.stack([own[:, ffn_from + 2 * FF * k : ffn_from + 2 * FF * (k + 1)] for k in range(2)]),
+        jnp.stack(jnp.split(wide, 2, axis=1)),
         grad_table,
         grad_gains,
     )

time: 2130 us -> 1880 us (0.88)
  Pallas kernels: 0 us -> 549 us
  waiting for transfers between devices: 829 us -> 303 us
  local copies, waits for them, and re-layouts: 481 us -> 342 us
  starting transfers between devices: 153 us -> 68 us
  matrix products: 308 us -> 275 us
    pallas_call x0 -> x3, Pallas kernels: none -> 549 us  [the longest x2 279 us: grad_sums(): pl.pallas_call(partial(grad_kernel, layout, orders, tuple(bounds), chunks...]
    ppermute x199 -> x64, waiting for transfers between devices: 829 us -> 303 us  [swap(): return lax.ppermute(value, axis, [(0, 1), (1, 0)])]
    ppermute x199 -> x64, starting transfers between devices: 153 us -> 68 us  [swap(): return lax.ppermute(value, axis, [(0, 1), (1, 0)])]
    dynamic_update_slice x80 -> x24, local copies, waits for them, and re-layouts: 79.5 us -> 29.4 us  [gather_blocks(): held = lax.dynamic_update_index_in_dim(joined, received, 1 - bit, position)]
    dynamic_slice x39 -> x9, local copies, waits for them, and re-layouts: 47.7 us -> 4.95 us  [take_bit(): return lax.dynamic_index_in_dim(value, bit, position, keepdims=False)]
    convert_element_type x73 -> x13, other arithmetic: 59.6 us -> 21.8 us  [sum_blocks(): held = held.astype(terms.dtype)]
    dynamic_update_slice x74 -> x18, local copies, waits for them, and re-layouts: 51.6 us -> 15.3 us  [gather_blocks(): joined = lax.dynamic_update_index_in_dim(joined, held, bit, position)]
    dot_general x16 -> x1, matrix products: 58 us -> 22.4 us  [mm_tn(): lax.dot_general(left, right, (((0,), (0,)), ((), ())), preferred_element_...]
  transfers between devices with their start and end apart: 199 -> 64, of which waited for: 104 -> 33; matrix products, arithmetic and copies ran while one was open for 37% -> 34% of each run, Pallas kernels for 0% -> 29%
where the time goes in v2:
time: 1880 us; the launch traced here: 1870 us
  Pallas kernels  549 us (29%)
  local copies, waits for them, and re-layouts  342 us (18%)
  other arithmetic  324 us (17%)
  waiting for transfers between devices  303 us (16%)
  matrix products  275 us (15%)
  starting transfers between devices  68 us (4%)
    ppermute x64, waiting for transfers between devices, swap(): return lax.ppermute(value, axis, [(0, 1), (1, 0)])  303 us
    pallas_call x2, Pallas kernels, grad_sums(): pl.pallas_call(partial(grad_kernel, layout, orders, tuple(bounds), chunks...  279 us
    pallas_call x1, Pallas kernels, gather_all(): pl.pallas_call(partial(gather_kernel, layout, tuple(units), LANES, count)...  270 us
    scatter-add x2, other arithmetic, look_back(): jax.ops.segment_sum(spread_rows(d_rows).astype(F32), segment_ids, num_seg...  104 us
    dot_general x14, matrix products, mm_nt(): lax.dot_general(left, right, (((1,), (1,)), ((), ())), preferred_element_...  69.5 us
    ppermute x64, starting transfers between devices, swap(): return lax.ppermute(value, axis, [(0, 1), (1, 0)])  68 us
    unnamed x470, local copies, waits for them, and re-layouts  66.4 us
    gather x2, local copies, waits for them, and re-layouts, embed(): table_bf[jnp.clip(local_ids[which], 0, vocab_part - 1)]  65.9 us
  transfers between devices with their start and end apart: 64, of which 33 were waited for; matrix products, arithmetic and copies ran while one was open for 34% of the time, Pallas kernels for 29%

profile of v2, /device:TPU:0, one launch (start us, length us, event | category | flops | bytes accessed | tf_op | source)
XLA Modules:
  0.0 1873.5 jit_solution(6114109913918321624)
XLA Ops:
  23.9 36.9 %collective-permute-done.1 = s32[2,2,2,1024]{3,2,1,0:T(2,128)S(1)} collective-permute-done((s32[2,2,2,1024]{3,2,1,0:T(2,128)S(1)}, s32[2,2,2,1024]{3,2,1,0:T(2,128)S(1)}, u32[]{:S(2)}, u32[]{:S(2)}) %collective-permute-start.1) | collective-permute-done | bytes 32800 | tf_op jit(solution)/shard_map/ppermute | solution.py:46
  61.3 33.0 %gather_fusion = bf16[8192,256]{1,0:T(8,128)(2,1)} fusion(bf16[4016,256]{1,0:T(8,128)(2,1)S(1)} %get-tuple-element.93, s32[8192]{0:T(1024)S(1)} %broadcast_clamp_fusion.1), kind=kCustom, calls=%fused_computation | custom fusion | bytes 8421376 | tf_op jit(solution)/shard_map/gather | solution.py:437
  101.3 33.0 %gather_fusion.1 = bf16[8192,256]{1,0:T(8,128)(2,1)} fusion(bf16[4016,256]{1,0:T(8,128)(2,1)S(1)} %get-tuple-element.93, s32[8192]{0:T(1024)S(1)} %broadcast_clamp_fusion), kind=kCustom, calls=%fused_computation.1 | custom fusion | bytes 8421376 | tf_op jit(solution)/shard_map/gather | solution.py:437
  156.8 270.2 %gather_weights.1 = (bf16[2,2,2,2,2,32,2048]{6,5,4,3,2,1,0:T(8,128)(2,1)}, bf16[2,2,2,2,2,32,1024]{6,5,4,3,2,1,0:T(8,128)(2,1)}, bf16[2,2,2,2,2,32,5632]{6,5,4,3...) custom-call(bf16[32,2048]{1,0:T(8,128)(2,1)} %get-tuple-element.146., ...), custom_call_target="tpu_custom_call" | custom-call | tf_op jit(solution)/shard_map/gather_weights/pallas_call | solution.py:151
  451.9 10.4 collective-permute-done.3
  468.7 27.2 %collective-permute-done.15 = bf16[2,2,2,256,256]{4,3,2,1,0:T(8,128)(2,1)} collective-permute-done((bf16[2,2,2,256,256]{4,3,2,1,0:T(8,128)(2,1)}, bf16[2,2,2,256,256]{4,3,2,1,0:T(8,128)(2,1)}, u32[]{:S(2)}, u32[]{:S(2)}) %collective-permute-start.15) | collective-permute-done | bytes 1048608 | tf_op jit(solution)/shard_map/ppermute | solution.py:46
  502.5 20.9 %collective-permute-done.16 = bf16[2,2,256,256]{3,2,1,0:T(8,128)(2,1)S(1)} collective-permute-done((bf16[2,2,256,256]{3,2,1,0:T(8,128)(2,1)S(1)}, bf16[2,2,256,256]{3,2,1,0:T(8,128)(2,1)S(1)}, u32[]{:S(2)}, u32[]{:S(2)}) %collective-permute-start.16) | collective-permute-done | bytes 524320 | tf_op jit(solution)/shard_map/ppermute | solution.py:46
  524.1 18.5 collective-permute-done.5
  600.1 8.3 bitcast_reduce_fusion.1
  608.4 8.6 fusion.20
  617.1 8.2 fusion.149
  637.9 7.2 fusion.245
  645.1 8.1 fusion.19
  653.3 7.7 fusion.150
  684.0 8.3 bitcast_reduce_fusion
  692.4 8.7 fusion.21
  701.1 8.0 fusion.148
  714.3 6.9 multiply_reduce_fusion.17
  728.3 21.6 %collective-permute-done.23 = bf16[256,1024]{1,0:T(8,128)(2,1)S(1)} collective-permute-done((bf16[256,1024]{1,0:T(8,128)(2,1)S(1)}, bf16[256,1024]{1,0:T(8,128)(2,1)S(1)}, u32[]{:S(2)}, u32[]{:S(2)}) %collective-permute-start.23) | collective-permute-done | bytes 524320 | tf_op jit(solution)/shard_map/ppermute | solution.py:46
  753.8 21.4 %collective-permute-done.24 = bf16[2,256,1024]{2,1,0:T(8,128)(2,1)S(1)} collective-permute-done((bf16[2,256,1024]{2,1,0:T(8,128)(2,1)S(1)}, bf16[2,256,1024]{2,1,0:T(8,128)(2,1)S(1)}, u32[]{:S(2)}, u32[]{:S(2)}) %collective-permute-start.24) | collective-permute-done | bytes 1048608 | tf_op jit(solution)/shard_map/ppermute | solution.py:46
  802.9 24.1 %multiply_reduce_fusion = (f32[2048]{0:T(1024)S(1)}, f32[2048,4016]{0,1:T(8,128)}) fusion(bf16[2048,1024]{1,0:T(8,128)(2,1)} %bitcast.143, bf16[4016,1024]{0,1:T(8,128)(2,1)S(1)} %bitcast.909), kind=kOutput, calls=%fused_computation.13 | convolution fusion | flops 16860772352 | bytes 45326336 | tf_op jit(solution)/shard_map/dot_general | solution.py:281
  827.1 15.6 fusion.5
  854.9 16.4 fusion.3
  871.4 22.4 %multiply_convert_fusion = bf16[4016,1024]{1,0:T(8,128)(2,1)} fusion(bf16[2048,4016]{0,1:T(8,128)(2,1)S(1)} %fusion.3, bf16[2048,1024]{1,0:T(8,128)(2,1)} %bitcast.143), kind=kOutput, calls=%fused_computation.45 | convolution fusion | flops 16852549632 | bytes 28868608 | tf_op jit(solution)/shard_map/dot_general | solution.py:285
  904.4 20.4 %multiply_convert_fusion.1 = bf16[2048,1024]{1,0:T(8,128)(2,1)S(1)} fusion(bf16[2048,4016]{0,1:T(8,128)(2,1)} %copy-done.17, bf16[4016,1024]{0,1:T(8,128)(2,1)S(1)} %bitcast.912), kind=kOutput, calls=%fused_computation.58 | convolution fusion | flops 16848519168 | bytes 28868608 | tf_op jit(solution)/shard_map/dot_general | solution.py:277
  937.7 6.7 copy.463
  959.7 22.0 %collective-permute-done.42 = bf16[2,2008,256]{2,1,0:T(8,128)(2,1)} collective-permute-done((bf16[2,2008,256]{2,1,0:T(8,128)(2,1)}, bf16[2,2008,256]{2,1,0:T(8,128)(2,1)}, u32[]{:S(2)}, u32[]{:S(2)}) %collective-permute-start.42) | collective-permute-done | bytes 2056224 | tf_op jit(solution)/shard_map/ppermute | solution.py:46
  989.1 13.1 collective-permute-done.41
  1010.8 19.6 %collective-permute-done.33 = bf16[256,1024]{1,0:T(8,128)(2,1)S(1)} collective-permute-done((bf16[256,1024]{1,0:T(8,128)(2,1)S(1)}, bf16[256,1024]{1,0:T(8,128)(2,1)S(1)}, u32[]{:S(2)}, u32[]{:S(2)}) %collective-permute-start.33) | collective-permute-done | bytes 524320 | tf_op jit(solution)/shard_map/ppermute | solution.py:46
  1038.2 8.3 multiply_reduce_fusion.4
  1049.8 8.6 fusion.110
  1058.4 14.0 fusion.12
  1072.4 7.9 fusion.14
  1090.2 11.5 fusion.6
  1101.6 9.4 fusion.118
  1131.2 11.7 fusion.8
  1192.1 7.8 multiply_reduce_fusion.8
  1205.1 12.0 fusion.9
  1217.2 8.5 fusion.114
  1233.0 11.8 fusion.11
  1276.1 71.2 %sum_gradients.3 = f32[9,96,256]{2,1,0:T(8,128)} custom-call(bf16[2,2,1536,256]{3,2,1,0:T(8,128)(2,1)} %bitcast.866, bf16[256,2048]{1,0:T(8,128)(2,1)} %pad_maximum_fusion.3.refs_1_), custom_call_target="tpu_custom_call" | custom-call | tf_op jit(solution)/shard_map/sum_gradients/pallas_call | solution.py:256
  1371.1 15.7 collective-permute-done.46
  1403.9 207.8 %sum_gradients.2 = f32[81,32,256]{2,1,0:T(8,128)} custom-call(bf16[9,2,512,256]{3,2,1,0:T(8,128)(2,1)} %bitcast.853, bf16[256,20480]{1,0:T(8,128)(2,1)} %constant_dynamic-update-slice_fusion.3.refs_1_), custom_call_target="tpu_custom_call" | custom-call | tf_op jit(solution)/shard_map/sum_gradients/pallas_call | solution.py:256
  1645.3 12.5 collective-permute-done.51
  1665.8 14.4 collective-permute-done.52
  1702.7 50.7 %scatter_custom_fusion = f32[4017,256]{1,0:T(8,128)} fusion(s32[8192]{0:T(1024)} %bitcast.1022, f32[8192,256]{1,0:T(8,128)} %bitcast.906, f32[]{:T(128)} %constant.411.clone.1), kind=kCustom, calls=%fused_computation.167 | custom fusion | flops 2097152 | bytes 4113920 | tf_op jit(solution)/shard_map/scatter-add | solution.py:592
  1763.5 53.2 %scatter_custom_fusion.1 = f32[4017,256]{1,0:T(8,128)} fusion(s32[8192]{0:T(1024)} %bitcast.1021, f32[8192,256]{1,0:T(8,128)} %bitcast.905, f32[]{:T(128)} %constant.411.clone.1), kind=kCustom, calls=%fused_computation.165 | custom fusion | flops 2097152 | bytes 4113920 | tf_op jit(solution)/shard_map/scatter-add | solution.py:592
  1859.5 11.7 multiply_add_fusion
  (955 shorter events, 580.2 us)
Async XLA Ops:
  2.1 21.1 %collective-permute-start = (s32[2,2,1024]{2,1,0:T(2,128)S(1)}, s32[2,2,1024]{2,1,0:T(2,128)S(1)}, u32[]{:S(2)}, u32[]{:S(2)}) collective-permute-start(s32[2,2,1024]{2,1,0:T(2,128)S(1)} %pad_add_fusion), channel_id=1, source_target_pairs={{0,16},{16,0},{1,17},{17,1},{2,18},{18,2},{3,19},{19,3},{4,20},{20... | collective-permute-start | bytes 49160 | tf_op jit(solution)/shard_map/ppermute | solution.py:46
  6.4 136.5 %collective-permute-start.7 = (bf16[32,7]{0,1:T(8,128)(2,1)}, bf16[32,7]{0,1:T(8,128)(2,1)S(1)}, u32[]{:S(2)}, u32[]{:S(2)}) collective-permute-start(bf16[32,7]{0,1:T(8,128)(2,1)} %get-tuple-element.187), channel_id=1, source_target_pairs={{0,4},{4,0},{1,5},{5,1},{2,6},{6,2},{3,7},{7,3},{8,12},{12,8},{9,1... | collective-permute-start | bytes 1352 | tf_op jit(solution)/shard_map/ppermute | solution.py:46
  14.2 428.0 %collective-permute-start.26 = (bf16[4016,256]{1,0:T(8,128)(2,1)S(1)}, bf16[4016,256]{1,0:T(8,128)(2,1)}, u32[]{:S(2)}, u32[]{:S(2)}) collective-permute-start(bf16[4016,256]{1,0:T(8,128)(2,1)S(1)} %get-tuple-element.93), channel_id=1, source_target_pairs={{0,8},{8,0},{1,9},{9,1},{2,10},{10,2},{3,11},{11,3},{4,12},{12,4},... | collective-permute-start | bytes 6168584 | tf_op jit(solution)/shard_map/ppermute | solution.py:46
  23.2 37.6 %collective-permute-start.1 = (s32[2,2,2,1024]{3,2,1,0:T(2,128)S(1)}, s32[2,2,2,1024]{3,2,1,0:T(2,128)S(1)}, u32[]{:S(2)}, u32[]{:S(2)}) collective-permute-start(s32[2,2,2,1024]{3,2,1,0:T(2,128)S(1)} %constant_dynamic-update-slice_fusion.25), channel_id=1, source_target_pairs={{0,8},{8,0},{1,9},{9,1},{2,10},{10,2},{3,11},{11,3},{4,12},{12,4},... | collective-permute-start | bytes 98312 | tf_op jit(solution)/shard_map/ppermute | solution.py:46
  101.3 331.5 %collective-permute-start.2 = (bf16[2,2,2,2,256,256]{5,4,3,2,1,0:T(8,128)(2,1)}, bf16[2,2,2,2,256,256]{5,4,3,2,1,0:T(8,128)(2,1)}, u32[]{:S(2)}, u32[]{:S(2)}) collective-permute-start(bf16[2,2,2,2,256,256]{5,4,3,2,1,0:T(8,128)(2,1)} %dynamic-slice_bitcast_fusion.1), channel_id=1, source_target_pairs={{0,1},{1,0},{2,3},{3,2},{4,5},{5,4},{6,7},{7,6},{8,9},{9,8},{10,11... | collective-permute-start | bytes 6291464 | tf_op jit(solution)/shard_map/ppermute | solution.py:46
  141.4 296.8 %collective-permute-start.14 = (bf16[2,2,2,2,256,256]{5,4,3,2,1,0:T(8,128)(2,1)}, bf16[2,2,2,2,256,256]{5,4,3,2,1,0:T(8,128)(2,1)}, u32[]{:S(2)}, u32[]{:S(2)}) collective-permute-start(bf16[2,2,2,2,256,256]{5,4,3,2,1,0:T(8,128)(2,1)} %dynamic-slice_bitcast_fusion), channel_id=1, source_target_pairs={{0,1},{1,0},{2,3},{3,2},{4,5},{5,4},{6,7},{7,6},{8,9},{9,8},{10,11... | collective-permute-start | bytes 6291464 | tf_op jit(solution)/shard_map/ppermute | solution.py:46
  154.2 274.8 %collective-permute-start.11 = (bf16[2,2,2,2,32,7]{4,3,5,2,1,0:T(2,128)(2,1)S(1)}, bf16[2,2,2,2,32,7]{4,3,5,2,1,0:T(2,128)(2,1)S(1)}, u32[]{:S(2)}, u32[]{:S(2)}) collective-permute-start(bf16[2,2,2,2,32,7]{4,3,5,2,1,0:T(2,128)(2,1)S(1)} %constant_dynamic-update-slice_fusion.19), channel_id=1, source_target_pairs={{0,1},{1,0},{2,3},{3,2},{4,5},{5,4},{6,7},{7,6},{8,9},{9,8},{10,11... | collective-permute-start | bytes 21512 | tf_op jit(solution)/shard_map/ppermute | solution.py:46
  435.9 26.4 %collective-permute-start.3 = (bf16[2,2,2,256,256]{4,3,2,1,0:T(8,128)(2,1)S(1)}, bf16[2,2,2,256,256]{4,3,2,1,0:T(8,128)(2,1)}, u32[]{:S(2)}, u32[]{:S(2)}) collective-permute-start(bf16[2,2,2,256,256]{4,3,2,1,0:T(8,128)(2,1)S(1)} %dynamic-slice_bitcast_fusion.6), channel_id=1, source_target_pairs={{0,2},{2,0},{1,3},{3,1},{4,6},{6,4},{5,7},{7,5},{8,10},{10,8},{9,1... | collective-permute-start | bytes 3145736 | tf_op jit(solution)/shard_map/ppermute | solution.py:46
  441.6 54.3 %collective-permute-start.15 = (bf16[2,2,2,256,256]{4,3,2,1,0:T(8,128)(2,1)}, bf16[2,2,2,256,256]{4,3,2,1,0:T(8,128)(2,1)}, u32[]{:S(2)}, u32[]{:S(2)}) collective-permute-start(bf16[2,2,2,256,256]{4,3,2,1,0:T(8,128)(2,1)} %dynamic-slice_bitcast_fusion.5), channel_id=1, source_target_pairs={{0,2},{2,0},{1,3},{3,1},{4,6},{6,4},{5,7},{7,5},{8,10},{10,8},{9,1... | collective-permute-start | bytes 3145736 | tf_op jit(solution)/shard_map/ppermute | solution.py:46
  445.2 331.6 %collective-permute-start.27 = (bf16[2,4016,256]{2,1,0:T(8,128)(2,1)}, bf16[2,4016,256]{2,1,0:T(8,128)(2,1)}, u32[]{:S(2)}, u32[]{:S(2)}) collective-permute-start(bf16[2,4016,256]{2,1,0:T(8,128)(2,1)} %bitcast_dynamic-update-slice_fusion.6), channel_id=1, source_target_pairs={{0,16},{16,0},{1,17},{17,1},{2,18},{18,2},{3,19},{19,3},{4,20},{20... | collective-permute-start | bytes 12337160 | tf_op jit(solution)/shard_map/ppermute | solution.py:46
  463.8 37.7 %collective-permute-start.4 = (bf16[2,2,256,256]{3,2,1,0:T(8,128)(2,1)S(1)}, bf16[2,2,256,256]{3,2,1,0:T(8,128)(2,1)S(1)}, u32[]{:S(2)}, u32[]{:S(2)}) collective-permute-start(bf16[2,2,256,256]{3,2,1,0:T(8,128)(2,1)S(1)} %dynamic-slice_bitcast_fusion.14), channel_id=1, source_target_pairs={{0,4},{4,0},{1,5},{5,1},{2,6},{6,2},{3,7},{7,3},{8,12},{12,8},{9,1... | collective-permute-start | bytes 1572872 | tf_op jit(solution)/shard_map/ppermute | solution.py:46
  497.4 26.0 %collective-permute-start.16 = (bf16[2,2,256,256]{3,2,1,0:T(8,128)(2,1)S(1)}, bf16[2,2,256,256]{3,2,1,0:T(8,128)(2,1)S(1)}, u32[]{:S(2)}, u32[]{:S(2)}) collective-permute-start(bf16[2,2,256,256]{3,2,1,0:T(8,128)(2,1)S(1)} %dynamic-slice_bitcast_fusion.13), channel_id=1, source_target_pairs={{0,4},{4,0},{1,5},{5,1},{2,6},{6,2},{3,7},{7,3},{8,12},{12,8},{9,1... | collective-permute-start | bytes 1572872 | tf_op jit(solution)/shard_map/ppermute | solution.py:46
  501.8 40.9 %collective-permute-start.5 = (bf16[2,256,256]{2,1,0:T(8,128)(2,1)S(1)}, bf16[2,256,256]{2,1,0:T(8,128)(2,1)S(1)}, u32[]{:S(2)}, u32[]{:S(2)}) collective-permute-start(bf16[2,256,256]{2,1,0:T(8,128)(2,1)S(1)} %dynamic-slice_bitcast_fusion.18), channel_id=1, source_target_pairs={{0,16},{16,0},{1,17},{17,1},{2,18},{18,2},{3,19},{19,3},{4,20},{20... | collective-permute-start | bytes 786440 | tf_op jit(solution)/shard_map/ppermute | solution.py:46
  523.6 24.0 %collective-permute-start.17 = (bf16[2,256,256]{2,1,0:T(8,128)(2,1)S(1)}, bf16[2,256,256]{2,1,0:T(8,128)(2,1)S(1)}, u32[]{:S(2)}, u32[]{:S(2)}) collective-permute-start(bf16[2,256,256]{2,1,0:T(8,128)(2,1)S(1)} %dynamic-slice_bitcast_fusion.17), channel_id=1, source_target_pairs={{0,16},{16,0},{1,17},{17,1},{2,18},{18,2},{3,19},{19,3},{4,20},{20... | collective-permute-start | bytes 786440 | tf_op jit(solution)/shard_map/ppermute | solution.py:46
  542.7 7.1 collective-permute-start.6
  547.7 7.7 collective-permute-start.18
  558.2 17.7 collective-permute-start.12
  562.9 19.3 %collective-permute-start.19 = (bf16[256,1024]{1,0:T(8,128)(2,1)}, bf16[256,1024]{1,0:T(8,128)(2,1)}, u32[]{:S(2)}, u32[]{:S(2)}) collective-permute-start(bf16[256,1024]{1,0:T(8,128)(2,1)} %get-tuple-element.206), channel_id=1, source_target_pairs={{0,2},{2,0},{1,3},{3,1},{4,6},{6,4},{5,7},{7,5},{8,10},{10,8},{9,1... | collective-permute-start | bytes 1572872 | tf_op jit(solution)/shard_map/ppermute | solution.py:46
  577.0 8.9 collective-permute-start.13
  584.0 6.5 collective-permute-start.20
  637.3 25.1 %collective-permute-start.21 = (bf16[256,1024]{1,0:T(8,128)(2,1)S(1)}, bf16[256,1024]{1,0:T(8,128)(2,1)S(1)}, u32[]{:S(2)}, u32[]{:S(2)}) collective-permute-start(bf16[256,1024]{1,0:T(8,128)(2,1)S(1)} %get-tuple-element.220), channel_id=1, source_target_pairs={{0,2},{2,0},{1,3},{3,1},{4,6},{6,4},{5,7},{7,5},{8,10},{10,8},{9,1... | collective-permute-start | bytes 1572872 | tf_op jit(solution)/shard_map/ppermute | solution.py:46
  663.3 13.8 collective-permute-start.22
  722.0 27.9 %collective-permute-start.23 = (bf16[256,1024]{1,0:T(8,128)(2,1)S(1)}, bf16[256,1024]{1,0:T(8,128)(2,1)S(1)}, u32[]{:S(2)}, u32[]{:S(2)}) collective-permute-start(bf16[256,1024]{1,0:T(8,128)(2,1)S(1)} %get-tuple-element.95), channel_id=1, source_target_pairs={{0,4},{4,0},{1,5},{5,1},{2,6},{6,2},{3,7},{7,3},{8,12},{12,8},{9,1... | collective-permute-start | bytes 1572872 | tf_op jit(solution)/shard_map/ppermute | solution.py:46
  750.0 25.1 %collective-permute-start.24 = (bf16[2,256,1024]{2,1,0:T(8,128)(2,1)S(1)}, bf16[2,256,1024]{2,1,0:T(8,128)(2,1)S(1)}, u32[]{:S(2)}, u32[]{:S(2)}) collective-permute-start(bf16[2,256,1024]{2,1,0:T(8,128)(2,1)S(1)} %bitcast_dynamic-update-slice_fusion.28), channel_id=1, source_target_pairs={{0,2},{2,0},{1,3},{3,1},{4,6},{6,4},{5,7},{7,5},{8,10},{10,8},{9,1... | collective-permute-start | bytes 3145736 | tf_op jit(solution)/shard_map/ppermute | solution.py:46
  776.2 23.7 %collective-permute-start.25 = (bf16[2,2,256,1024]{3,2,1,0:T(8,128)(2,1)}, bf16[2,2,256,1024]{3,2,1,0:T(8,128)(2,1)}, u32[]{:S(2)}, u32[]{:S(2)}) collective-permute-start(bf16[2,2,256,1024]{3,2,1,0:T(8,128)(2,1)} %bitcast_dynamic-update-slice_fusion.19), channel_id=1, source_target_pairs={{0,1},{1,0},{2,3},{3,2},{4,5},{5,4},{6,7},{7,6},{8,9},{9,8},{10,11... | collective-permute-start | bytes 6291464 | tf_op jit(solution)/shard_map/ppermute | solution.py:46
  848.3 6.5 collective-permute-start.30
  903.7 46.7 %collective-permute-start.40 = (bf16[2,2008,256]{2,1,0:T(8,128)(2,1)}, bf16[2,2008,256]{2,1,0:T(8,128)(2,1)}, u32[]{:S(2)}, u32[]{:S(2)}) collective-permute-start(bf16[2,2008,256]{2,1,0:T(8,128)(2,1)} %dynamic-slice_bitcast_fusion.3), channel_id=1, source_target_pairs={{0,16},{16,0},{1,17},{17,1},{2,18},{18,2},{3,19},{19,3},{4,20},{20... | collective-permute-start | bytes 6168584 | tf_op jit(solution)/shard_map/ppermute | solution.py:46
  928.0 27.0 %collective-permute-start.31 = (bf16[2,2,256,1024]{3,2,0,1:T(8,128)(2,1)}, bf16[2,2,256,1024]{3,2,0,1:T(8,128)(2,1)}, u32[]{:S(2)}, u32[]{:S(2)}) collective-permute-start(bf16[2,2,256,1024]{3,2,0,1:T(8,128)(2,1)} %bitcast.826), channel_id=1, source_target_pairs={{0,1},{1,0},{2,3},{3,2},{4,5},{5,4},{6,7},{7,6},{8,9},{9,8},{10,11... | collective-permute-start | bytes 6291464 | tf_op jit(solution)/shard_map/ppermute | solution.py:46
  933.8 48.0 %collective-permute-start.42 = (bf16[2,2008,256]{2,1,0:T(8,128)(2,1)}, bf16[2,2008,256]{2,1,0:T(8,128)(2,1)}, u32[]{:S(2)}, u32[]{:S(2)}) collective-permute-start(bf16[2,2008,256]{2,1,0:T(8,128)(2,1)} %dynamic-slice_bitcast_fusion.2), channel_id=1, source_target_pairs={{0,8},{8,0},{1,9},{9,1},{2,10},{10,2},{3,11},{11,3},{4,12},{12,4},... | collective-permute-start | bytes 6168584 | tf_op jit(solution)/shard_map/ppermute | solution.py:46
  954.4 47.8 %collective-permute-start.41 = (bf16[2008,256]{1,0:T(8,128)(2,1)}, bf16[2008,256]{1,0:T(8,128)(2,1)}, u32[]{:S(2)}, u32[]{:S(2)}) collective-permute-start(bf16[2008,256]{1,0:T(8,128)(2,1)} %dynamic-slice_bitcast_fusion.8), channel_id=1, source_target_pairs={{0,8},{8,0},{1,9},{9,1},{2,10},{10,2},{3,11},{11,3},{4,12},{12,4},... | collective-permute-start | bytes 3084296 | tf_op jit(solution)/shard_map/ppermute | solution.py:46
  957.9 47.4 %collective-permute-start.32 = (bf16[2,256,1024]{2,1,0:T(8,128)(2,1)S(1)}, bf16[2,256,1024]{2,1,0:T(8,128)(2,1)S(1)}, u32[]{:S(2)}, u32[]{:S(2)}) collective-permute-start(bf16[2,256,1024]{2,1,0:T(8,128)(2,1)S(1)} %dynamic-slice_bitcast_fusion.4), channel_id=1, source_target_pairs={{0,2},{2,0},{1,3},{3,1},{4,6},{6,4},{5,7},{7,5},{8,10},{10,8},{9,1... | collective-permute-start | bytes 3145736 | tf_op jit(solution)/shard_map/ppermute | solution.py:46
  985.5 22.6 %collective-permute-start.43 = (bf16[2008,256]{1,0:T(8,128)(2,1)}, bf16[2008,256]{1,0:T(8,128)(2,1)}, u32[]{:S(2)}, u32[]{:S(2)}) collective-permute-start(bf16[2008,256]{1,0:T(8,128)(2,1)} %dynamic-slice_bitcast_fusion.7), channel_id=1, source_target_pairs={{0,16},{16,0},{1,17},{17,1},{2,18},{18,2},{3,19},{19,3},{4,20},{20... | collective-permute-start | bytes 3084296 | tf_op jit(solution)/shard_map/ppermute | solution.py:46
  1005.9 24.5 %collective-permute-start.33 = (bf16[256,1024]{1,0:T(8,128)(2,1)S(1)}, bf16[256,1024]{1,0:T(8,128)(2,1)S(1)}, u32[]{:S(2)}, u32[]{:S(2)}) collective-permute-start(bf16[256,1024]{1,0:T(8,128)(2,1)S(1)} %dynamic-slice_bitcast_fusion.12), channel_id=1, source_target_pairs={{0,4},{4,0},{1,5},{5,1},{2,6},{6,2},{3,7},{7,3},{8,12},{12,8},{9,1... | collective-permute-start | bytes 1572872 | tf_op jit(solution)/shard_map/ppermute | solution.py:46
  1124.9 39.4 %collective-permute-start.34 = (bf16[2,256,1024]{2,1,0:T(8,128)(2,1)}, bf16[2,256,1024]{2,1,0:T(8,128)(2,1)}, u32[]{:S(2)}, u32[]{:S(2)}) collective-permute-start(bf16[2,256,1024]{2,1,0:T(8,128)(2,1)} %fusion.160), channel_id=1, source_target_pairs={{0,1},{1,0},{2,3},{3,2},{4,5},{5,4},{6,7},{7,6},{8,9},{9,8},{10,11... | collective-permute-start | bytes 3145736 | tf_op jit(solution)/shard_map/ppermute | solution.py:46
  1158.7 17.1 collective-permute-start.38
  1168.0 14.7 collective-permute-start.35
  1178.6 88.0 %collective-permute-start.39 = (bf16[256,1024]{1,0:T(8,128)(2,1)}, bf16[256,1024]{1,0:T(8,128)(2,1)}, u32[]{:S(2)}, u32[]{:S(2)}) collective-permute-start(bf16[256,1024]{1,0:T(8,128)(2,1)} %dynamic-slice_bitcast_fusion.9), channel_id=1, source_target_pairs={{0,2},{2,0},{1,3},{3,1},{4,6},{6,4},{5,7},{7,5},{8,10},{10,8},{9,1... | collective-permute-start | bytes 1572872 | tf_op jit(solution)/shard_map/ppermute | solution.py:46
  1260.4 109.0 %collective-permute-start.36 = (bf16[2,256,1024]{2,1,0:T(8,128)(2,1)}, bf16[2,256,1024]{2,1,0:T(8,128)(2,1)}, u32[]{:S(2)}, u32[]{:S(2)}) collective-permute-start(bf16[2,256,1024]{2,1,0:T(8,128)(2,1)} %fusion.156), channel_id=1, source_target_pairs={{0,1},{1,0},{2,3},{3,2},{4,5},{5,4},{6,7},{7,6},{8,9},{9,8},{10,11... | collective-permute-start | bytes 3145736 | tf_op jit(solution)/shard_map/ppermute | solution.py:46
  1274.7 82.4 %collective-permute-start.44 = (bf16[2,256,256]{2,1,0:T(8,128)(2,1)}, bf16[2,256,256]{2,1,0:T(8,128)(2,1)}, u32[]{:S(2)}, u32[]{:S(2)}) collective-permute-start(bf16[2,256,256]{2,1,0:T(8,128)(2,1)} %dynamic-slice_bitcast_fusion.16), channel_id=1, source_target_pairs={{0,16},{16,0},{1,17},{17,1},{2,18},{18,2},{3,19},{19,3},{4,20},{20... | collective-permute-start | bytes 786440 | tf_op jit(solution)/shard_map/ppermute | solution.py:46
  1364.8 21.9 %collective-permute-start.46 = (bf16[4,256,256]{2,1,0:T(8,128)(2,1)S(1)}, bf16[4,256,256]{2,1,0:T(8,128)(2,1)S(1)}, u32[]{:S(2)}, u32[]{:S(2)}) collective-permute-start(bf16[4,256,256]{2,1,0:T(8,128)(2,1)S(1)} %bitcast.949), channel_id=1, source_target_pairs={{0,4},{4,0},{1,5},{5,1},{2,6},{6,2},{3,7},{7,3},{8,12},{12,8},{9,1... | collective-permute-start | bytes 1572872 | tf_op jit(solution)/shard_map/ppermute | solution.py:46
  1371.0 18.3 collective-permute-start.37
  1387.6 270.4 %collective-permute-start.47 = (bf16[2,4,256,256]{3,2,1,0:T(8,128)(2,1)}, bf16[2,4,256,256]{3,2,1,0:T(8,128)(2,1)}, u32[]{:S(2)}, u32[]{:S(2)}) collective-permute-start(bf16[2,4,256,256]{3,2,1,0:T(8,128)(2,1)} %bitcast_dynamic-update-slice_fusion.22), channel_id=1, source_target_pairs={{0,2},{2,0},{1,3},{3,1},{4,6},{6,4},{5,7},{7,5},{8,10},{10,8},{9,1... | collective-permute-start | bytes 3145736 | tf_op jit(solution)/shard_map/ppermute | solution.py:46
  1639.3 18.4 collective-permute-start.51
  1645.1 12.8 collective-permute-start.55
  1657.8 22.4 %collective-permute-start.52 = (bf16[2,4,256,256]{3,2,1,0:T(8,128)(2,1)S(1)}, bf16[2,4,256,256]{3,2,1,0:T(8,128)(2,1)S(1)}, u32[]{:S(2)}, u32[]{:S(2)}) collective-permute-start(bf16[2,4,256,256]{3,2,1,0:T(8,128)(2,1)S(1)} %bitcast_dynamic-update-slice_fusion.20), channel_id=1, source_target_pairs={{0,2},{2,0},{1,3},{3,1},{4,6},{6,4},{5,7},{7,5},{8,10},{10,8},{9,1... | collective-permute-start | bytes 3145736 | tf_op jit(solution)/shard_map/ppermute | solution.py:46
  1659.3 34.4 %collective-permute-start.48 = (bf16[2,2,4,256,256]{4,3,2,1,0:T(8,128)(2,1)S(1)}, bf16[2,2,4,256,256]{4,3,2,1,0:T(8,128)(2,1)}, u32[]{:S(2)}, u32[]{:S(2)}) collective-permute-start(bf16[2,2,4,256,256]{4,3,2,1,0:T(8,128)(2,1)S(1)} %bitcast_dynamic-update-slice_fusion.18), channel_id=1, source_target_pairs={{0,1},{1,0},{2,3},{3,2},{4,5},{5,4},{6,7},{7,6},{8,9},{9,8},{10,11... | collective-permute-start | bytes 6291464 | tf_op jit(solution)/shard_map/ppermute | solution.py:46
  1681.2 72.1 %collective-permute-start.53 = (bf16[2,2,4,256,256]{4,3,2,1,0:T(8,128)(2,1)}, bf16[2,2,4,256,256]{4,3,2,1,0:T(8,128)(2,1)}, u32[]{:S(2)}, u32[]{:S(2)}) collective-permute-start(bf16[2,2,4,256,256]{4,3,2,1,0:T(8,128)(2,1)} %bitcast_dynamic-update-slice_fusion.8), channel_id=1, source_target_pairs={{0,1},{1,0},{2,3},{3,2},{4,5},{5,4},{6,7},{7,6},{8,9},{9,8},{10,11... | collective-permute-start | bytes 6291464 | tf_op jit(solution)/shard_map/ppermute | solution.py:46
  1825.3 7.0 collective-permute-start.59
  (237 other events, 4259.8 us)

commit v3 on v2

--- a/solution.py
+++ b/solution.py
@@ -140,8 +140,8 @@
     units = []
     for tensor, shard in enumerate(shards):
         columns = shard.shape[1]
-        pieces = max(1, columns // 1024)
-        step = columns // pieces // 128 * 128
+        step = -(-512 * 32 // shard.shape[0] // 128) * 128
+        pieces = -(-columns // step)
         starts = [step * piece for piece in range(pieces)] + [columns]
         for piece in range(pieces):
             order = orders[len(units) % len(orders)]
@@ -299,57 +299,113 @@
     return (d_input, jnp.sum(grad_out * stream * inverse, axis=0))
 
 
-def head_split(queries, keyvals):
+def nt(left, right):
+    return lax.dot_general(left, right, (((1,), (1,)), ((), ())), preferred_element_type=F32)
+
+
+def attend_kernel(causal, row_ref, q_ref, k_ref, v_ref, o_ref):
+    rows, length = q_ref.shape[0], k_ref.shape[0]
+    shape = (rows, length)
+    if causal:
+        allowed = row_ref[0] + lax.broadcasted_iota(
+            jnp.int32, shape, 0
+        ) >= lax.broadcasted_iota(jnp.int32, shape, 1)
+    for head in range(q_ref.shape[1] // HD):
+        own = pl.ds(head * HD, HD)
+        shared = pl.ds(head // (HQ // HK) * HD, HD)
+        scores = nt(q_ref[:, own], k_ref[:, shared]) * HD ** (-0.5)
+        if causal:
+            scores = jnp.where(allowed, scores, -1000000000.0)
+        expo = jnp.exp(scores - jnp.max(scores, axis=-1, keepdims=True))
+        probs = expo * (1.0 / jnp.sum(expo, axis=-1, keepdims=True))
+        mixed = jnp.dot(probs.astype(BF), v_ref[:, shared], preferred_element_type=F32)
+        o_ref[:, own] = mixed.astype(BF)
+
+
+def attend_back_kernel(causal, row_ref, q_ref, k_ref, v_ref, d_ref, dq_ref, dk_ref, dv_ref):
+    rows, length = q_ref.shape[0], k_ref.shape[0]
+    shape = (length, rows)
+    share = HQ // HK
+    if causal:
+        allowed = row_ref[0] + lax.broadcasted_iota(
+            jnp.int32, shape, 1
+        ) >= lax.broadcasted_iota(jnp.int32, shape, 0)
+    for pair in range(k_ref.shape[1] // HD):
+        shared = pl.ds(pair * HD, HD)
+        keys, values = k_ref[:, shared], v_ref[:, shared]
+        d_keys = d_values = None
+        for head in range(pair * share, (pair + 1) * share):
+            own = pl.ds(head * HD, HD)
+            queries, d_mixed = q_ref[:, own], d_ref[:, own]
+            scores = nt(keys, queries) * HD ** (-0.5)
+            if causal:
+                scores = jnp.where(allowed, scores, -1000000000.0)
+            expo = jnp.exp(scores - jnp.max(scores, axis=0, keepdims=True))
+            probs = expo * (1.0 / jnp.sum(expo, axis=0, keepdims=True))
+            d_probs = nt(values, d_mixed)
+            mean = jnp.sum(probs * d_probs, axis=0, keepdims=True)
+            d_scores = (probs * (d_probs - mean)).astype(BF)
+            key_term = jnp.dot(d_scores, queries, preferred_element_type=F32)
+            value_term = jnp.dot(probs.astype(BF), d_mixed, preferred_element_type=F32)
+            d_keys = key_term if d_keys is None else d_keys + key_term
+            d_values = value_term if d_values is None else d_values + value_term
+            d_queries = lax.dot_general(
+                keys, d_scores, (((0,), (0,)), ((), ())), preferred_element_type=F32
+            )
+            dq_ref[:, own] = (d_queries.T * HD ** (-0.5)).astype(BF)
+        dk_ref[:, shared] = (d_keys * HD ** (-0.5)).astype(BF)
+        dv_ref[:, shared] = d_values.astype(BF)
+
+
+def attend_specs(rows, length):
+    wide = 128 * (HQ // HK)
+    queries = pl.BlockSpec((rows, wide), lambda i: (0, i))
+    keys = pl.BlockSpec((length, 128), lambda i: (0, i))
+    values = pl.BlockSpec((length, 128), lambda i: (0, i + KW // 128))
+    return queries, keys, values
+
+
+def attend_forward(queries, keyvals, first_row):
     rows, length = queries.shape[0], keyvals.shape[0]
-    query_heads = queries.reshape(rows, HK, HQ // HK, HD)
-    key_heads = keyvals[:, :KW].reshape(length, HK, HD)
-    value_heads = keyvals[:, KW:].reshape(length, HK, HD)
-    return (query_heads, key_heads, value_heads)
-
-
-def scores_of(query_heads, key_heads, first_row):
-    scores = jnp.einsum(
-        "rhgd,khd->hgrk", query_heads, key_heads, preferred_element_type=F32
-    ) * HD ** (-0.5)
-    if first_row is not None:
-        rows, length = query_heads.shape[0], key_heads.shape[0]
-        allowed = (first_row + jnp.arange(rows))[:, None] >= jnp.arange(length)[None, :]
-        scores = jnp.where(allowed, scores, -1000000000.0)
-    return scores
-
-
-def attend_forward(queries, keyvals, first_row):
-    query_heads, key_heads, value_heads = head_split(queries, keyvals)
-    scores = scores_of(query_heads, key_heads, first_row)
-    row_max = jnp.max(scores, axis=-1, keepdims=True)
-    expo_terms = jnp.exp(scores - row_max)
-    row_total = jnp.sum(expo_terms, axis=-1, keepdims=True)
-    attn_probs = (expo_terms / row_total).astype(BF)
-    mixed = jnp.einsum("hgrk,khd->rhgd", attn_probs, value_heads, preferred_element_type=F32)
-    return (mixed.reshape(queries.shape[0], QW).astype(BF), row_max + jnp.log(row_total))
-
-
-def attend_backward(queries, keyvals, first_row, log_total, d_mixed):
+    by_query, by_key, by_value = attend_specs(rows, length)
+    return pl.pallas_call(
+        partial(attend_kernel, first_row is not None),
+        grid=(KW // 128,),
+        out_shape=jax.ShapeDtypeStruct(queries.shape, BF),
+        in_specs=[pl.BlockSpec(memory_space=pltpu.SMEM), by_query, by_key, by_value],
+        out_specs=by_query,
+        compiler_params=pltpu.CompilerParams(vmem_limit_bytes=56 * 1024 * 1024),
+        cost_estimate=pl.CostEstimate(
+            flops=4 * rows * length * QW,
+            bytes_accessed=4 * rows * QW + 4 * length * KW,
+            transcendentals=HQ * rows * length,
+        ),
+        name="attend",
+    )(jnp.reshape(0 if first_row is None else first_row, (1,)), queries, keyvals, keyvals)
+
+
+def attend_backward(queries, keyvals, first_row, d_mixed):
     rows, length = queries.shape[0], keyvals.shape[0]
-    query_heads, key_heads, value_heads = head_split(queries, keyvals)
-    attn_probs = jnp.exp(scores_of(query_heads, key_heads, first_row) - log_total)
-    d_heads = d_mixed.reshape(rows, HK, HQ // HK, HD)
-    d_probs = jnp.einsum("rhgd,khd->hgrk", d_heads, value_heads, preferred_element_type=F32)
-    d_scores = attn_probs * (d_probs - jnp.sum(attn_probs * d_probs, axis=-1, keepdims=True))
-    d_scores = d_scores.astype(BF)
-    d_queries = jnp.einsum(
-        "hgrk,khd->rhgd", d_scores, key_heads, preferred_element_type=F32
-    ) * HD ** (-0.5)
-    d_keys = jnp.einsum(
-        "hgrk,rhgd->khd", d_scores, query_heads, preferred_element_type=F32
-    ) * HD ** (-0.5)
-    d_values = jnp.einsum(
-        "hgrk,rhgd->khd", attn_probs.astype(BF), d_heads, preferred_element_type=F32
-    )
-    d_keyvals = jnp.concatenate(
-        [d_keys.reshape(length, KW).astype(BF), d_values.reshape(length, KW).astype(BF)], axis=-1
-    )
-    return (d_queries.reshape(rows, QW).astype(BF), d_keyvals)
+    by_query, by_key, by_value = attend_specs(rows, length)
+    d_queries, d_keys, d_values = pl.pallas_call(
+        partial(attend_back_kernel, first_row is not None),
+        grid=(KW // 128,),
+        out_shape=[
+            jax.ShapeDtypeStruct(queries.shape, BF),
+            jax.ShapeDtypeStruct((length, KW), BF),
+            jax.ShapeDtypeStruct((length, KW), BF),
+        ],
+        in_specs=[pl.BlockSpec(memory_space=pltpu.SMEM), by_query, by_key, by_value, by_query],
+        out_specs=[by_query, by_key, by_key],
+        compiler_params=pltpu.CompilerParams(vmem_limit_bytes=56 * 1024 * 1024),
+        cost_estimate=pl.CostEstimate(
+            flops=10 * rows * length * QW,
+            bytes_accessed=6 * rows * QW + 8 * length * KW,
+            transcendentals=HQ * rows * length,
+        ),
+        name="attend_back",
+    )(jnp.reshape(0 if first_row is None else first_row, (1,)), queries, keyvals, keyvals, d_mixed)
+    return (d_queries, jnp.concatenate([d_keys, d_values], axis=1))
 
 
 def update(weight, gradient, moment, average, rate, factor):
@@ -404,22 +460,6 @@
     rows = length // 2 ** len(row_axes)
     first_row = lax.axis_index(row_axes) * rows
 
-    shards = [attn_in[0], attn_out[0], ff_in[0], ff_out[0]]
-    shards += [attn_in[1], attn_out[1], attn_in[2], attn_out[2], ff_in[1], ff_out[1]]
-    shards = [shard.astype(BF) for shard in shards]
-    in_kernels = attn_in.shape[1] % 16 == 0
-    if in_kernels:
-        full = gather_all(shards, every, six_orders)
-    else:
-        full = [
-            gather_blocks(shard, every, gather_orders[k % 3]) for k, shard in enumerate(shards)
-        ]
-    full = [got.reshape((-1,) + shard.shape[1:]) for got, shard in zip(full, shards)]
-    a_in, a_out = (full[0], full[4], full[6]), (full[1], full[5], full[7])
-    f_in, f_out = (full[2], full[8]), (full[3], full[9])
-    gain_all = gather_blocks(gains.astype(BF).T, every, gather_orders[0])
-    gain_all = gain_all.reshape(-1, gains.shape[0]).T.astype(F32)
-
     vocab_part = table.shape[0]
     offset = lax.axis_index(mp_axes) * vocab_part
     table_bf = table.astype(BF)
@@ -454,6 +494,31 @@
     stream_e = embed(0)
     stream_d = embed(1)
 
+    shards = [attn_in[0], attn_out[0], ff_in[0], ff_out[0]]
+    shards += [attn_in[1], attn_out[1], attn_in[2], attn_out[2], ff_in[1], ff_out[1]]
+    shards = [shard.astype(BF) for shard in shards]
+    in_kernels = attn_in.shape[1] % 16 == 0
+    if in_kernels:
+        early = (0, 1)
+        full = [None] * len(shards)
+        for k in early:
+            full[k] = lax.all_gather(shards[k], every, axis=0, tiled=True)
+        late = [k for k in range(len(shards)) if k not in early]
+        held = lax.optimization_barrier([shards[k] for k in late] + [stream_e, stream_d])
+        stream_e, stream_d = held[-2:]
+        for k, got in zip(late, gather_all(held[:-2], every, six_orders)):
+            full[k] = got
+        full[4], table_bf = lax.optimization_barrier((full[4], table_bf))
+    else:
+        full = [
+            gather_blocks(shard, every, gather_orders[k % 3]) for k, shard in enumerate(shards)
+        ]
+    full = [got.reshape((-1,) + shard.shape[1:]) for got, shard in zip(full, shards)]
+    a_in, a_out = (full[0], full[4], full[6]), (full[1], full[5], full[7])
+    f_in, f_out = (full[2], full[8]), (full[3], full[9])
+    gain_all = gather_blocks(gains.astype(BF).T, every, gather_orders[0])
+    gain_all = gain_all.reshape(-1, gains.shape[0]).T.astype(F32)
+
     table_rows = gather_blocks(table_bf, dp_axes, dp_axes[::-1]).reshape(-1, *table.shape)
     table_rows = jnp.moveaxis(table_rows, 0, 1).reshape(vocab_part, -1)
 
@@ -465,9 +530,9 @@
         anchor = normed if source is None else source
         keyvals = spread_keys(mm(anchor, a_in[block][:, QW:]).astype(BF))
         queries = mm(normed, a_in[block][:, :QW]).astype(BF)
-        mixed, log_total = attend_forward(queries, keyvals, start)
+        mixed = attend_forward(queries, keyvals, start)
         out = stream + mm(mixed, a_out[block])
-        return (out, (stream, normed, anchor, queries, keyvals, mixed, log_total))
+        return (out, (stream, normed, anchor, queries, keyvals, mixed))
 
     def ffn_forward(stream, which, gain_row):
         normed = norm_forward(stream, gain_row).astype(BF)
@@ -541,10 +606,10 @@
         return (d_stream + d_input, (normed, d_both, hidden_act, d_branch), grad_gain)
 
     def attention_backward(saved, cross, block, gain_row, start, d_stream):
-        stream, normed, anchor, queries, keyvals, mixed, log_total = saved
+        stream, normed, anchor, queries, keyvals, mixed = saved
         d_branch = d_stream.astype(BF)
         d_mixed = mm_nt(d_branch, a_out[block]).astype(BF)
-        d_queries, d_keyvals = attend_backward(queries, keyvals, start, log_total, d_mixed)
+        d_queries, d_keyvals = attend_backward(queries, keyvals, start, d_mixed)
         d_keyvals = sum_blocks(
             d_keyvals.reshape(two_rows + (rows, -1)), row_axes, row_axes[::-1], BF
         )
@@ -558,6 +623,10 @@
 
     d_y, gain6 = norm_backward(stream_d, gain_all[6], d_final)
     d_y, ffn_factors1, gain5 = ffn_backward(dec_ffn, 1, gain_all[5], d_y)
+    if in_kernels:
+        first_sum = lax.psum_scatter(
+            mm_tn(ffn_factors1[0], ffn_factors1[1]).astype(BF), every, scatter_dimension=0, tiled=True
+        ).astype(F32)
     d_y, d_encoded, attn_factors2, gain4 = attention_backward(
         dec_cross, True, 2, gain_all[4], None, d_y
     )
@@ -588,10 +657,8 @@
         return jnp.moveaxis(everyone, 0, 1).reshape(-1, width)
 
     def look_back(which, d_rows):
-        segment_ids = jnp.where(inside[which], local_ids[which], vocab_part)
-        return jax.ops.segment_sum(
-            spread_rows(d_rows).astype(F32), segment_ids, num_segments=vocab_part + 1
-        )[:vocab_part]
+        places = (local_ids[which][None, :] == jnp.arange(vocab_part)[:, None]).astype(BF)
+        return mm(places, spread_rows(d_rows))
 
     grad_table = grad_table + look_back(1, d_y) + look_back(0, d_x)
 
@@ -615,8 +682,9 @@
             rights += [d_queries, d_keyvals, d_branch]
     wide_lefts, wide_rights = [], []
     for normed, d_both, hidden_act, d_branch in (ffn_factors0, ffn_factors1):
-        lefts.append(normed)
-        rights.append(d_both)
+        if hidden_act is ffn_factors0[2] or not in_kernels:
+            lefts.append(normed)
+            rights.append(d_both)
         wide_lefts.append(hidden_act)
         wide_rights.append(d_branch)
     spans = [right.shape[1] for right in rights]
@@ -624,6 +692,7 @@
     if in_kernels:
         back_orders = tuple(order[::-1] for order in three)
         own = grad_sums(lefts, rights, every, back_orders, spans, 1)
+        own = jnp.concatenate([own, first_sum], axis=1)
         wide = grad_sums(wide_lefts, wide_rights, every, back_orders, wide_spans, 2)
     else:
 

time: 1880 us -> 1580 us (0.84)
  other arithmetic: 324 us -> 145 us
  local copies, waits for them, and re-layouts: 342 us -> 228 us
  matrix products: 275 us -> 204 us
  Pallas kernels: 549 us -> 599 us
    dot_general x18 -> x0, matrix products: 136 us -> none  [the longest x3 37.5 us: attend_backward(): jnp.einsum('rhgd,khd->hgrk', d_heads, value_heads, preferred_element_type...]
    pallas_call x0 -> x6, Pallas kernels: none -> 104 us  [the longest x3 63.6 us: attend_backward(): pl.pallas_call(partial(attend_back_kernel, first_row is not None), grid=(...]
    scatter-add x2 -> x0, other arithmetic: 104 us -> none  [look_back(): jax.ops.segment_sum(spread_rows(d_rows).astype(F32), segment_ids, num_seg...]
    convert_element_type x26 -> x0, local copies, waits for them, and re-layouts: 59.7 us -> none  [the longest x6 19.5 us: attend_backward(): d_keys.reshape(length, KW).astype(BF)]
    dot_general x14 -> x16, matrix products: 47.1 us -> 105 us  [mm(): return jnp.dot(left, right, preferred_element_type=F32)]
    pallas_call x1, Pallas kernels: 270 us -> 225 us  [gather_all(): pl.pallas_call(partial(gather_kernel, layout, tuple(units), LANES, count)...]
    convert_element_type x5 -> x1, other arithmetic: 35.9 us -> 2.45 us  [on_device(): table_bf = table.astype(BF)]
    unnamed x470 -> x366, local copies, waits for them, and re-layouts: 66.4 us -> 37.2 us
  transfers between devices with their start and end apart: 64 -> 67, of which waited for: 33 -> 33; matrix products, arithmetic and copies ran while one was open for 34% -> 27% of each run, Pallas kernels for 29% -> 37%
where the time goes in v3:
time: 1580 us
  Pallas kernels  599 us (38%)
  waiting for transfers between devices  318 us (20%)
  local copies, waits for them, and re-layouts  228 us (14%)
  matrix products  204 us (13%)
  other arithmetic  145 us (9%)
  starting transfers between devices  59.6 us (4%)
  between operations  23.5 us (1%)
    ppermute x64, waiting for transfers between devices, swap(): return lax.ppermute(value, axis, [(0, 1), (1, 0)])  318 us
    pallas_call x2, Pallas kernels, grad_sums(): pl.pallas_call(partial(grad_kernel, layout, orders, tuple(bounds), chunks...  270 us
    pallas_call x1, Pallas kernels, gather_all(): pl.pallas_call(partial(gather_kernel, layout, tuple(units), LANES, count)...  225 us
    dot_general x16, matrix products, mm(): return jnp.dot(left, right, preferred_element_type=F32)  105 us
    dot_general x14, matrix products, mm_nt(): lax.dot_general(left, right, (((1,), (1,)), ((), ())), preferred_element_...  70.5 us
    gather x2, local copies, waits for them, and re-layouts, embed(): table_bf[jnp.clip(local_ids[which], 0, vocab_part - 1)]  66.1 us
    pallas_call x3, Pallas kernels, attend_backward(): pl.pallas_call(partial(attend_back_kernel, first_row is not None), grid=(...  63.6 us
    ppermute x64, starting transfers between devices, swap(): return lax.ppermute(value, axis, [(0, 1), (1, 0)])  59.5 us
  transfers between devices with their start and end apart: 67, of which 33 were waited for; matrix products, arithmetic and copies ran while one was open for 27% of the time, Pallas kernels for 37%

profile of v3, /device:TPU:0, one launch (start us, length us, event | category | flops | bytes accessed | tf_op | source)
XLA Modules:
  0.0 1576.5 jit_solution(5844607147857548537)
XLA Ops:
  28.3 33.1 %gather_fusion = bf16[8192,256]{1,0:T(8,128)(2,1)} fusion(bf16[4016,256]{1,0:T(8,128)(2,1)S(1)} %convert_element_type.426, s32[8192]{0:T(1024)S(1)} %broadcast_clamp_fusion.1), kind=kCustom, calls=%fused_computation | custom fusion | bytes 8421376 | tf_op jit(solution)/shard_map/gather | solution.py:477
  61.4 5.3 broadcast_select_fusion.1
  69.7 33.1 %gather_fusion.1 = bf16[8192,256]{1,0:T(8,128)(2,1)} fusion(bf16[4016,256]{1,0:T(8,128)(2,1)S(1)} %convert_element_type.426, s32[8192]{0:T(1024)S(1)} %broadcast_clamp_fusion), kind=kCustom, calls=%fused_computation.1 | custom fusion | bytes 8421376 | tf_op jit(solution)/shard_map/gather | solution.py:477
  135.0 15.6 collective-permute-done.3
  153.0 29.9 %collective-permute-done.8 = bf16[2,2,2,256,256]{4,3,2,1,0:T(8,128)(2,1)} collective-permute-done((bf16[2,2,2,256,256]{4,3,2,1,0:T(8,128)(2,1)}, bf16[2,2,2,256,256]{4,3,2,1,0:T(8,128)(2,1)}, u32[]{:S(2)}, u32[]{:S(2)}) %collective-permute-start.8) | collective-permute-done | bytes 1048608 | tf_op jit(solution)/shard_map/ppermute | solution.py:46
  187.5 20.5 %collective-permute-done.9 = bf16[2,2,256,256]{3,2,1,0:T(8,128)(2,1)S(1)} collective-permute-done((bf16[2,2,256,256]{3,2,1,0:T(8,128)(2,1)S(1)}, bf16[2,2,256,256]{3,2,1,0:T(8,128)(2,1)S(1)}, u32[]{:S(2)}, u32[]{:S(2)}) %collective-permute-start.9) | collective-permute-done | bytes 524320 | tf_op jit(solution)/shard_map/ppermute | solution.py:46
  211.6 5.0 collective-permute-done.10
  218.4 5.6 collective-permute-done.11
  226.2 224.7 %gather_weights.1 = (bf16[2,2,2,2,2,32,5632]{6,5,4,3,2,1,0:T(8,128)(2,1)}, bf16[2,2,2,2,2,88,1024]{6,5,4,3,2,1,0:T(8,128)(2,1)}, bf16[2,2,2,2,2,32,2048]{6,5,4,3...) custom-call(bf16[32,5632]{1,0:T(8,128)(2,1)} %get-tuple-element.51.r, ...), custom_call_target="tpu_custom_call" | custom-call | tf_op jit(solution)/shard_map/gather_weights/pallas_call | solution.py:151
  463.8 7.9 collective-permute-done.19
  472.5 25.9 %collective-permute-done.26 = bf16[4016,256]{1,0:T(8,128)(2,1)} collective-permute-done((bf16[4016,256]{1,0:T(8,128)(2,1)S(1)}, bf16[4016,256]{1,0:T(8,128)(2,1)}, u32[]{:S(2)}, u32[]{:S(2)}) %collective-permute-start.26) | collective-permute-done | bytes 2056224 | tf_op jit(solution)/shard_map/ppermute | solution.py:46
  502.3 6.4 copy.230
  516.1 13.6 attend.4
  540.2 6.2 fusion.166
  556.0 9.4 collective-permute-done.21
  569.5 13.7 attend.3
  590.0 13.2 attend.5
  605.8 6.2 fusion.167
  619.4 22.6 %collective-permute-done.23 = bf16[256,1024]{1,0:T(8,128)(2,1)S(1)} collective-permute-done((bf16[256,1024]{1,0:T(8,128)(2,1)S(1)}, bf16[256,1024]{1,0:T(8,128)(2,1)S(1)}, u32[]{:S(2)}, u32[]{:S(2)}) %collective-permute-start.23) | collective-permute-done | bytes 524320 | tf_op jit(solution)/shard_map/ppermute | solution.py:46
  644.5 6.6 copy.231
  651.5 15.6 collective-permute-done.24
  680.6 23.7 %multiply_reduce_fusion = (f32[2048]{0:T(1024)S(1)}, f32[2048,4016]{0,1:T(8,128)}) fusion(bf16[2048,1024]{1,0:T(8,128)(2,1)} %bitcast.114, bf16[4016,1024]{0,1:T(8,128)(2,1)S(1)} %bitcast.667), kind=kOutput, calls=%fused_computation.17 | convolution fusion | flops 16860772352 | bytes 45326336 | tf_op jit(solution)/shard_map/dot_general | solution.py:281
  704.3 17.4 %fusion.9 = (f32[2048]{0:T(1024)S(1)}, f32[2048]{0:T(1024)S(1)}) fusion(f32[2048,4016]{0,1:T(8,128)} %get-tuple-element.254, f32[2048]{0:T(1024)S(1)} %get-tuple-element.253, s32[2048]{0:T(1024)S(1)} %bitcast.733, s32[4016]{0:T(1024)S(1)} %iota_add_fusion), kind=kLoop, calls=%fused_computation.16 | loop fusion | flops 49344512 | bytes 32947904 | tf_op jit(solution)/shard_map/reduce_sum | solution.py:559
  732.6 13.3 fusion.7
  745.9 21.8 %multiply_convert_fusion = bf16[4016,1024]{1,0:T(8,128)(2,1)S(1)} fusion(bf16[2048,4016]{0,1:T(8,128)(2,1)} %fusion.7, bf16[2048,1024]{1,0:T(8,128)(2,1)} %bitcast.114), kind=kOutput, calls=%fused_computation.18 | convolution fusion | flops 16852549632 | bytes 28868608 | tf_op jit(solution)/shard_map/dot_general | solution.py:285
  776.5 20.4 %multiply_convert_fusion.1 = bf16[2048,1024]{1,0:T(8,128)(2,1)S(1)} fusion(bf16[2048,4016]{0,1:T(8,128)(2,1)} %fusion.7, bf16[4016,1024]{0,1:T(8,128)(2,1)S(1)} %bitcast.670), kind=kOutput, calls=%fused_computation.20 | convolution fusion | flops 16848519168 | bytes 28868608 | tf_op jit(solution)/shard_map/dot_general | solution.py:277
  806.2 6.4 copy.232
  835.8 16.7 %collective-permute-done.40 = bf16[2,2008,256]{2,1,0:T(8,128)(2,1)} collective-permute-done((bf16[2,2008,256]{2,1,0:T(8,128)(2,1)}, bf16[2,2008,256]{2,1,0:T(8,128)(2,1)}, u32[]{:S(2)}, u32[]{:S(2)}) %collective-permute-start.40) | collective-permute-done | bytes 2056224 | tf_op jit(solution)/shard_map/ppermute | solution.py:46
  858.9 15.2 collective-permute-done.43
  884.3 20.5 %collective-permute-done.33 = bf16[256,1024]{1,0:T(8,128)(2,1)S(1)} collective-permute-done((bf16[256,1024]{1,0:T(8,128)(2,1)S(1)}, bf16[256,1024]{1,0:T(8,128)(2,1)S(1)}, u32[]{:S(2)}, u32[]{:S(2)}) %collective-permute-start.33) | collective-permute-done | bytes 524320 | tf_op jit(solution)/shard_map/ppermute | solution.py:46
  905.7 6.3 fusion.29
  912.1 7.3 multiply_reduce_fusion.4
  922.5 21.2 %attend_back.3 = (bf16[256,1024]{1,0:T(8,128)(2,1)}, bf16[1024,512]{1,0:T(8,128)(2,1)}, bf16[1024,512]{1,0:T(8,128)(2,1)}) custom-call(s32[1]{0:T(128)} %constant.410.clone.1.row_ref, bf16[256,1024]{1,0:T(8,128)(2,1)} %fusion.84.q_ref, bf16[1024,1024]{1,0:T(8,128)(2,1)} %bitcast.699, bf16[1024,1024]{1,0:T(8,128)(2,1)} %bitcast.700, ...), custom_call_target="tpu_custom_call" | custom-call | flops 2684354560 | bytes 5767168 | tf_op jit(solution)/shard_map/attend_back/pallas_call | solution.py:390
  951.4 21.3 %attend_back.5 = (bf16[256,1024]{1,0:T(8,128)(2,1)}, bf16[1024,512]{1,0:T(8,128)(2,1)}, bf16[1024,512]{1,0:T(8,128)(2,1)}) custom-call(s32[1]{0:T(128)} %bitcast.54.row_ref, bf16[256,1024]{1,0:T(8,128)(2,1)} %fusion.78.q_ref, bf16[1024,1024]{1,0:T(8,128)(2,1)} %bitcast.695, bf16[1024,1024]{1,0:T(8,128)(2,1)} %bitcast.696, ...), custom_call_target="tpu_custom_call" | custom-call | flops 2684354560 | bytes 5767168 | tf_op jit(solution)/shard_map/attend_back/pallas_call | solution.py:390
  977.1 6.8 convolution_convert_fusion
  996.7 14.6 collective-permute-done.35
  1014.9 6.1 fusion.22
  1022.6 7.0 multiply_reduce_fusion.8
  1032.8 21.1 %attend_back.4 = (bf16[256,1024]{1,0:T(8,128)(2,1)}, bf16[1024,512]{1,0:T(8,128)(2,1)}, bf16[1024,512]{1,0:T(8,128)(2,1)}) custom-call(s32[1]{0:T(128)} %constant.410.clone.1.row_ref, bf16[256,1024]{1,0:T(8,128)(2,1)} %fusion.87.q_ref, bf16[1024,1024]{1,0:T(8,128)(2,1)} %bitcast.691, bf16[1024,1024]{1,0:T(8,128)(2,1)} %bitcast.692, ...), custom_call_target="tpu_custom_call" | custom-call | flops 2684354560 | bytes 5767168 | tf_op jit(solution)/shard_map/attend_back/pallas_call | solution.py:390
  1058.0 115.8 %sum_gradients.3 = f32[9,96,256]{2,1,0:T(8,128)} custom-call(bf16[2,2,1536,256]{3,2,1,0:T(8,128)(2,1)} %bitcast.655, bf16[256,2048]{1,0:T(8,128)(2,1)} %pad_maximum_fusion.9.refs_1_), custom_call_target="tpu_custom_call" | custom-call | tf_op jit(solution)/shard_map/sum_gradients/pallas_call | solution.py:256
  1187.8 5.4 collective-permute-done.44
  1206.9 17.7 %collective-permute-done.46 = bf16[4,256,256]{2,1,0:T(8,128)(2,1)S(1)} collective-permute-done((bf16[4,256,256]{2,1,0:T(8,128)(2,1)S(1)}, bf16[4,256,256]{2,1,0:T(8,128)(2,1)S(1)}, u32[]{:S(2)}, u32[]{:S(2)}) %collective-permute-start.46) | collective-permute-done | bytes 524320 | tf_op jit(solution)/shard_map/ppermute | solution.py:46
  1239.9 154.2 %sum_gradients.2 = f32[60,32,256]{2,1,0:T(8,128)} custom-call(bf16[8,2,512,256]{3,2,1,0:T(8,128)(2,1)} %bitcast.647, bf16[256,14848]{1,0:T(8,128)(2,1)} %constant_dynamic-update-slice_fusion.refs_1_), custom_call_target="tpu_custom_call" | custom-call | tf_op jit(solution)/shard_map/sum_gradients/pallas_call | solution.py:256
  1422.4 16.4 %collective-permute-done.51 = bf16[4,256,256]{2,1,0:T(8,128)(2,1)S(1)} collective-permute-done((bf16[4,256,256]{2,1,0:T(8,128)(2,1)S(1)}, bf16[4,256,256]{2,1,0:T(8,128)(2,1)S(1)}, u32[]{:S(2)}, u32[]{:S(2)}) %collective-permute-start.51) | collective-permute-done | bytes 524320 | tf_op jit(solution)/shard_map/ppermute | solution.py:46
  1443.8 19.0 %collective-permute-done.58 = f32[7,32]{1,0:T(8,128)S(1)} collective-permute-done((f32[7,32]{1,0:T(8,128)S(1)}, f32[7,32]{1,0:T(8,128)S(1)}, u32[]{:S(2)}, u32[]{:S(2)}) %collective-permute-start.58) | collective-permute-done | bytes 928 | tf_op jit(solution)/shard_map/ppermute | solution.py:46
  1469.7 22.4 %fusion = f32[4016,256]{1,0:T(8,128)S(1)} fusion(bf16[8192,256]{1,0:T(8,128)(2,1)S(1)} %bitcast.682, s32[8192]{0:T(1024)S(1)} %bitcast.757), kind=kOutput, calls=%fused_computation.4 | convolution fusion | flops 16877223936 | bytes 8339456 | tf_op jit(solution)/shard_map/dot_general | solution.py:277
  1494.3 27.3 %multiply_reduce_fusion.1 = (f32[]{:T(128)}, f32[4016,256]{1,0:T(8,128)}) fusion(f32[4016,256]{1,0:T(8,128)S(1)} %fusion, f32[2008,256]{1,0:T(8,128)S(1)} %copy-done.77, f32[2008,256]{1,0:T(8,128)S(1)} %copy-done.78, bf16[8192,256]{1,0:T(8,128)(2,1)S(1)} %bitcast.681, s32[8192]{0:T(1024)S(1)} %bitcast.756), kind=kOutput, calls=%fused_computation.45 | convolution fusion | flops 16882364416 | bytes 16564228 | tf_op jit(solution)/shard_map/dot_general | solution.py:277
  1556.3 11.7 multiply_add_fusion
  (805 shorter events, 376.0 us)
Async XLA Ops:
  7.2 445.5 %all-gather.5.cloned.1.call-start = ((), (), s32[]{:S(2)}) async-start(), calls=%async_computation.2 | async-start | bytes 4325376 | tf_op jit(solution)/shard_map/all_gather | solution.py:505
  9.4 527.7 %all-gather.7.cloned.1.call-start = ((), (), s32[]{:S(2)}) async-start(), calls=%async_computation.3 | async-start | bytes 2162688 | tf_op jit(solution)/shard_map/all_gather | solution.py:505
  10.1 101.3 %collective-permute-start.12 = (bf16[32,7]{0,1:T(8,128)(2,1)S(1)}, bf16[32,7]{0,1:T(8,128)(2,1)S(1)}, u32[]{:S(2)}, u32[]{:S(2)}) collective-permute-start(bf16[32,7]{0,1:T(8,128)(2,1)S(1)} %get-tuple-element.219), channel_id=1, source_target_pairs={{0,4},{4,0},{1,5},{5,1},{2,6},{6,2},{3,7},{7,3},{8,12},{12,8},{9,1... | collective-permute-start | bytes 1352 | tf_op jit(solution)/shard_map/ppermute | solution.py:46
  15.6 8.2 collective-permute-start
  18.9 1502.7 %reduce-scatter.2.cloned.1.call-start = ((), (), s32[]{:S(2)}) async-start(), calls=%async_computation.1 | async-start | bytes 11894784 | tf_op jit(solution)/shard_map/reduce_scatter | solution.py:627
  69.7 46.4 %collective-permute-start.2 = (bf16[2,2,2,2,256,256]{5,4,3,2,1,0:T(8,128)(2,1)}, bf16[2,2,2,2,256,256]{5,4,3,2,1,0:T(8,128)(2,1)}, u32[]{:S(2)}, u32[]{:S(2)}) collective-permute-start(bf16[2,2,2,2,256,256]{5,4,3,2,1,0:T(8,128)(2,1)} %dynamic-slice_bitcast_fusion.1), channel_id=1, source_target_pairs={{0,1},{1,0},{2,3},{3,2},{4,5},{5,4},{6,7},{7,6},{8,9},{9,8},{10,11... | collective-permute-start | bytes 6291464 | tf_op jit(solution)/shard_map/ppermute | solution.py:46
  110.0 10.8 collective-permute-start.7
  115.3 10.2 collective-permute-start.14
  119.3 31.3 %collective-permute-start.3 = (bf16[2,2,2,256,256]{4,3,2,1,0:T(8,128)(2,1)S(1)}, bf16[2,2,2,256,256]{4,3,2,1,0:T(8,128)(2,1)}, u32[]{:S(2)}, u32[]{:S(2)}) collective-permute-start(bf16[2,2,2,256,256]{4,3,2,1,0:T(8,128)(2,1)S(1)} %dynamic-slice_bitcast_fusion.9), channel_id=1, source_target_pairs={{0,2},{2,0},{1,3},{3,1},{4,6},{6,4},{5,7},{7,5},{8,10},{10,8},{9,1... | collective-permute-start | bytes 3145736 | tf_op jit(solution)/shard_map/ppermute | solution.py:46
  124.7 58.1 %collective-permute-start.8 = (bf16[2,2,2,256,256]{4,3,2,1,0:T(8,128)(2,1)}, bf16[2,2,2,256,256]{4,3,2,1,0:T(8,128)(2,1)}, u32[]{:S(2)}, u32[]{:S(2)}) collective-permute-start(bf16[2,2,2,256,256]{4,3,2,1,0:T(8,128)(2,1)} %dynamic-slice_bitcast_fusion.8), channel_id=1, source_target_pairs={{0,2},{2,0},{1,3},{3,1},{4,6},{6,4},{5,7},{7,5},{8,10},{10,8},{9,1... | collective-permute-start | bytes 3145736 | tf_op jit(solution)/shard_map/ppermute | solution.py:46
  152.4 33.4 %collective-permute-start.4 = (bf16[2,2,256,256]{3,2,1,0:T(8,128)(2,1)S(1)}, bf16[2,2,256,256]{3,2,1,0:T(8,128)(2,1)S(1)}, u32[]{:S(2)}, u32[]{:S(2)}) collective-permute-start(bf16[2,2,256,256]{3,2,1,0:T(8,128)(2,1)S(1)} %dynamic-slice_bitcast_fusion.17), channel_id=1, source_target_pairs={{0,4},{4,0},{1,5},{5,1},{2,6},{6,2},{3,7},{7,3},{8,12},{12,8},{9,1... | collective-permute-start | bytes 1572872 | tf_op jit(solution)/shard_map/ppermute | solution.py:46
  184.4 23.6 %collective-permute-start.9 = (bf16[2,2,256,256]{3,2,1,0:T(8,128)(2,1)S(1)}, bf16[2,2,256,256]{3,2,1,0:T(8,128)(2,1)S(1)}, u32[]{:S(2)}, u32[]{:S(2)}) collective-permute-start(bf16[2,2,256,256]{3,2,1,0:T(8,128)(2,1)S(1)} %dynamic-slice_bitcast_fusion.16), channel_id=1, source_target_pairs={{0,4},{4,0},{1,5},{5,1},{2,6},{6,2},{3,7},{7,3},{8,12},{12,8},{9,1... | collective-permute-start | bytes 1572872 | tf_op jit(solution)/shard_map/ppermute | solution.py:46
  186.0 23.8 %collective-permute-start.5 = (bf16[2,256,256]{2,1,0:T(8,128)(2,1)S(1)}, bf16[2,256,256]{2,1,0:T(8,128)(2,1)S(1)}, u32[]{:S(2)}, u32[]{:S(2)}) collective-permute-start(bf16[2,256,256]{2,1,0:T(8,128)(2,1)S(1)} %dynamic-slice_bitcast_fusion.21), channel_id=1, source_target_pairs={{0,16},{16,0},{1,17},{17,1},{2,18},{18,2},{3,19},{19,3},{4,20},{20... | collective-permute-start | bytes 786440 | tf_op jit(solution)/shard_map/ppermute | solution.py:46
  208.2 8.3 collective-permute-start.10
  209.9 8.1 collective-permute-start.6
  450.8 47.5 %collective-permute-start.26 = (bf16[4016,256]{1,0:T(8,128)(2,1)S(1)}, bf16[4016,256]{1,0:T(8,128)(2,1)}, u32[]{:S(2)}, u32[]{:S(2)}) collective-permute-start(bf16[4016,256]{1,0:T(8,128)(2,1)S(1)} %convert_element_type.426), channel_id=1, source_target_pairs={{0,8},{8,0},{1,9},{9,1},{2,10},{10,2},{3,11},{11,3},{4,12},{12,4},... | collective-permute-start | bytes 6168584 | tf_op jit(solution)/shard_map/ppermute | solution.py:46
  457.1 14.5 collective-permute-start.19
  472.5 40.9 %collective-permute-start.20 = (bf16[2,256,1024]{2,1,0:T(8,128)(2,1)}, bf16[2,256,1024]{2,1,0:T(8,128)(2,1)}, u32[]{:S(2)}, u32[]{:S(2)}) collective-permute-start(bf16[2,256,1024]{2,1,0:T(8,128)(2,1)} %bitcast_dynamic-update-slice_fusion.32), channel_id=1, source_target_pairs={{0,1},{1,0},{2,3},{3,2},{4,5},{5,4},{6,7},{7,6},{8,9},{9,8},{10,11... | collective-permute-start | bytes 3145736 | tf_op jit(solution)/shard_map/ppermute | solution.py:46
  501.4 143.2 %collective-permute-start.27 = (bf16[2,4016,256]{2,1,0:T(8,128)(2,1)}, bf16[2,4016,256]{2,1,0:T(8,128)(2,1)}, u32[]{:S(2)}, u32[]{:S(2)}) collective-permute-start(bf16[2,4016,256]{2,1,0:T(8,128)(2,1)} %bitcast_dynamic-update-slice_fusion.2), channel_id=1, source_target_pairs={{0,16},{16,0},{1,17},{17,1},{2,18},{18,2},{3,19},{19,3},{4,20},{20... | collective-permute-start | bytes 12337160 | tf_op jit(solution)/shard_map/ppermute | solution.py:46
  535.5 17.0 %collective-permute-start.17 = (bf16[256,1024]{1,0:T(8,128)(2,1)}, bf16[256,1024]{1,0:T(8,128)(2,1)}, u32[]{:S(2)}, u32[]{:S(2)}) collective-permute-start(bf16[256,1024]{1,0:T(8,128)(2,1)} %get-tuple-element.240), channel_id=1, source_target_pairs={{0,2},{2,0},{1,3},{3,1},{4,6},{6,4},{5,7},{7,5},{8,10},{10,8},{9,1... | collective-permute-start | bytes 1572872 | tf_op jit(solution)/shard_map/ppermute | solution.py:46
  551.9 13.4 collective-permute-start.21
  554.5 13.0 collective-permute-start.18
  565.4 21.9 %collective-permute-start.22 = (bf16[2,256,1024]{2,1,0:T(8,128)(2,1)S(1)}, bf16[2,256,1024]{2,1,0:T(8,128)(2,1)}, u32[]{:S(2)}, u32[]{:S(2)}) collective-permute-start(bf16[2,256,1024]{2,1,0:T(8,128)(2,1)S(1)} %bitcast_dynamic-update-slice_fusion.30), channel_id=1, source_target_pairs={{0,1},{1,0},{2,3},{3,2},{4,5},{5,4},{6,7},{7,6},{8,9},{9,8},{10,11... | collective-permute-start | bytes 3145736 | tf_op jit(solution)/shard_map/ppermute | solution.py:46
  615.5 26.5 %collective-permute-start.23 = (bf16[256,1024]{1,0:T(8,128)(2,1)S(1)}, bf16[256,1024]{1,0:T(8,128)(2,1)S(1)}, u32[]{:S(2)}, u32[]{:S(2)}) collective-permute-start(bf16[256,1024]{1,0:T(8,128)(2,1)S(1)} %get-tuple-element.131), channel_id=1, source_target_pairs={{0,4},{4,0},{1,5},{5,1},{2,6},{6,2},{3,7},{7,3},{8,12},{12,8},{9,1... | collective-permute-start | bytes 1572872 | tf_op jit(solution)/shard_map/ppermute | solution.py:46
  642.1 24.9 %collective-permute-start.24 = (bf16[2,256,1024]{2,1,0:T(8,128)(2,1)S(1)}, bf16[2,256,1024]{2,1,0:T(8,128)(2,1)}, u32[]{:S(2)}, u32[]{:S(2)}) collective-permute-start(bf16[2,256,1024]{2,1,0:T(8,128)(2,1)S(1)} %bitcast_dynamic-update-slice_fusion.28), channel_id=1, source_target_pairs={{0,2},{2,0},{1,3},{3,1},{4,6},{6,4},{5,7},{7,5},{8,10},{10,8},{9,1... | collective-permute-start | bytes 3145736 | tf_op jit(solution)/shard_map/ppermute | solution.py:46
  668.6 10.6 collective-permute-start.25
  775.0 51.5 %collective-permute-start.42 = (bf16[2,2008,256]{2,1,0:T(8,128)(2,1)}, bf16[2,2008,256]{2,1,0:T(8,128)(2,1)}, u32[]{:S(2)}, u32[]{:S(2)}) collective-permute-start(bf16[2,2008,256]{2,1,0:T(8,128)(2,1)} %dynamic-slice_bitcast_fusion.2), channel_id=1, source_target_pairs={{0,8},{8,0},{1,9},{9,1},{2,10},{10,2},{3,11},{11,3},{4,12},{12,4},... | collective-permute-start | bytes 6168584 | tf_op jit(solution)/shard_map/ppermute | solution.py:46
  800.3 31.6 %collective-permute-start.31 = (bf16[2,2,256,1024]{3,2,0,1:T(8,128)(2,1)}, bf16[2,2,256,1024]{3,2,0,1:T(8,128)(2,1)}, u32[]{:S(2)}, u32[]{:S(2)}) collective-permute-start(bf16[2,2,256,1024]{3,2,0,1:T(8,128)(2,1)} %bitcast.620), channel_id=1, source_target_pairs={{0,1},{1,0},{2,3},{3,2},{4,5},{5,4},{6,7},{7,6},{8,9},{9,8},{10,11... | collective-permute-start | bytes 6291464 | tf_op jit(solution)/shard_map/ppermute | solution.py:46
  804.6 47.9 %collective-permute-start.40 = (bf16[2,2008,256]{2,1,0:T(8,128)(2,1)}, bf16[2,2008,256]{2,1,0:T(8,128)(2,1)}, u32[]{:S(2)}, u32[]{:S(2)}) collective-permute-start(bf16[2,2008,256]{2,1,0:T(8,128)(2,1)} %dynamic-slice_bitcast_fusion.3), channel_id=1, source_target_pairs={{0,16},{16,0},{1,17},{17,1},{2,18},{18,2},{3,19},{19,3},{4,20},{20... | collective-permute-start | bytes 6168584 | tf_op jit(solution)/shard_map/ppermute | solution.py:46
  830.5 43.6 %collective-permute-start.43 = (bf16[2008,256]{1,0:T(8,128)(2,1)}, bf16[2008,256]{1,0:T(8,128)(2,1)}, u32[]{:S(2)}, u32[]{:S(2)}) collective-permute-start(bf16[2008,256]{1,0:T(8,128)(2,1)} %dynamic-slice_bitcast_fusion.10), channel_id=1, source_target_pairs={{0,16},{16,0},{1,17},{17,1},{2,18},{18,2},{3,19},{19,3},{4,20},{20... | collective-permute-start | bytes 3084296 | tf_op jit(solution)/shard_map/ppermute | solution.py:46
  834.8 42.6 %collective-permute-start.32 = (bf16[2,256,1024]{2,1,0:T(8,128)(2,1)S(1)}, bf16[2,256,1024]{2,1,0:T(8,128)(2,1)}, u32[]{:S(2)}, u32[]{:S(2)}) collective-permute-start(bf16[2,256,1024]{2,1,0:T(8,128)(2,1)S(1)} %dynamic-slice_bitcast_fusion.7), channel_id=1, source_target_pairs={{0,2},{2,0},{1,3},{3,1},{4,6},{6,4},{5,7},{7,5},{8,10},{10,8},{9,1... | collective-permute-start | bytes 3145736 | tf_op jit(solution)/shard_map/ppermute | solution.py:46
  856.2 25.1 %collective-permute-start.41 = (bf16[2008,256]{1,0:T(8,128)(2,1)}, bf16[2008,256]{1,0:T(8,128)(2,1)}, u32[]{:S(2)}, u32[]{:S(2)}) collective-permute-start(bf16[2008,256]{1,0:T(8,128)(2,1)} %dynamic-slice_bitcast_fusion.11), channel_id=1, source_target_pairs={{0,8},{8,0},{1,9},{9,1},{2,10},{10,2},{3,11},{11,3},{4,12},{12,4},... | collective-permute-start | bytes 3084296 | tf_op jit(solution)/shard_map/ppermute | solution.py:46
  879.1 25.8 %collective-permute-start.33 = (bf16[256,1024]{1,0:T(8,128)(2,1)S(1)}, bf16[256,1024]{1,0:T(8,128)(2,1)S(1)}, u32[]{:S(2)}, u32[]{:S(2)}) collective-permute-start(bf16[256,1024]{1,0:T(8,128)(2,1)S(1)} %dynamic-slice_bitcast_fusion.15), channel_id=1, source_target_pairs={{0,4},{4,0},{1,5},{5,1},{2,6},{6,2},{3,7},{7,3},{8,12},{12,8},{9,1... | collective-permute-start | bytes 1572872 | tf_op jit(solution)/shard_map/ppermute | solution.py:46
  946.7 37.2 %collective-permute-start.34 = (bf16[2,256,1024]{2,1,0:T(8,128)(2,1)}, bf16[2,256,1024]{2,1,0:T(8,128)(2,1)}, u32[]{:S(2)}, u32[]{:S(2)}) collective-permute-start(bf16[2,256,1024]{2,1,0:T(8,128)(2,1)} %dynamic-slice_bitcast_fusion.6), channel_id=1, source_target_pairs={{0,1},{1,0},{2,3},{3,2},{4,5},{5,4},{6,7},{7,6},{8,9},{9,8},{10,11... | collective-permute-start | bytes 3145736 | tf_op jit(solution)/shard_map/ppermute | solution.py:46
  977.1 14.8 collective-permute-start.38
  986.9 24.4 %collective-permute-start.35 = (bf16[256,1024]{1,0:T(8,128)(2,1)}, bf16[256,1024]{1,0:T(8,128)(2,1)}, u32[]{:S(2)}, u32[]{:S(2)}) collective-permute-start(bf16[256,1024]{1,0:T(8,128)(2,1)} %dynamic-slice_bitcast_fusion.14), channel_id=1, source_target_pairs={{0,2},{2,0},{1,3},{3,1},{4,6},{6,4},{5,7},{7,5},{8,10},{10,8},{9,1... | collective-permute-start | bytes 1572872 | tf_op jit(solution)/shard_map/ppermute | solution.py:46
  994.8 180.3 %collective-permute-start.39 = (bf16[256,1024]{1,0:T(8,128)(2,1)}, bf16[256,1024]{1,0:T(8,128)(2,1)S(1)}, u32[]{:S(2)}, u32[]{:S(2)}) collective-permute-start(bf16[256,1024]{1,0:T(8,128)(2,1)} %dynamic-slice_bitcast_fusion.12), channel_id=1, source_target_pairs={{0,2},{2,0},{1,3},{3,1},{4,6},{6,4},{5,7},{7,5},{8,10},{10,8},{9,1... | collective-permute-start | bytes 1572872 | tf_op jit(solution)/shard_map/ppermute | solution.py:46
  1056.9 146.1 %collective-permute-start.36 = (bf16[2,256,1024]{2,1,0:T(8,128)(2,1)}, bf16[2,256,1024]{2,1,0:T(8,128)(2,1)}, u32[]{:S(2)}, u32[]{:S(2)}) collective-permute-start(bf16[2,256,1024]{2,1,0:T(8,128)(2,1)} %dynamic-slice_bitcast_fusion.5), channel_id=1, source_target_pairs={{0,1},{1,0},{2,3},{3,2},{4,5},{5,4},{6,7},{7,6},{8,9},{9,8},{10,11... | collective-permute-start | bytes 3145736 | tf_op jit(solution)/shard_map/ppermute | solution.py:46
  1182.0 11.2 collective-permute-start.44
  1201.0 23.6 %collective-permute-start.46 = (bf16[4,256,256]{2,1,0:T(8,128)(2,1)S(1)}, bf16[4,256,256]{2,1,0:T(8,128)(2,1)S(1)}, u32[]{:S(2)}, u32[]{:S(2)}) collective-permute-start(bf16[4,256,256]{2,1,0:T(8,128)(2,1)S(1)} %bitcast.703), channel_id=1, source_target_pairs={{0,4},{4,0},{1,5},{5,1},{2,6},{6,2},{3,7},{7,3},{8,12},{12,8},{9,1... | collective-permute-start | bytes 1572872 | tf_op jit(solution)/shard_map/ppermute | solution.py:46
  1204.7 24.2 %collective-permute-start.37 = (bf16[256,1024]{1,0:T(8,128)(2,1)S(1)}, bf16[256,1024]{1,0:T(8,128)(2,1)S(1)}, u32[]{:S(2)}, u32[]{:S(2)}) collective-permute-start(bf16[256,1024]{1,0:T(8,128)(2,1)S(1)} %dynamic-slice_bitcast_fusion.13), channel_id=1, source_target_pairs={{0,2},{2,0},{1,3},{3,1},{4,6},{6,4},{5,7},{7,5},{8,10},{10,8},{9,1... | collective-permute-start | bytes 1572872 | tf_op jit(solution)/shard_map/ppermute | solution.py:46
  1225.4 191.8 %collective-permute-start.47 = (bf16[2,4,256,256]{3,2,1,0:T(8,128)(2,1)}, bf16[2,4,256,256]{3,2,1,0:T(8,128)(2,1)}, u32[]{:S(2)}, u32[]{:S(2)}) collective-permute-start(bf16[2,4,256,256]{3,2,1,0:T(8,128)(2,1)} %bitcast_dynamic-update-slice_fusion.18), channel_id=1, source_target_pairs={{0,2},{2,0},{1,3},{3,1},{4,6},{6,4},{5,7},{7,5},{8,10},{10,8},{9,1... | collective-permute-start | bytes 3145736 | tf_op jit(solution)/shard_map/ppermute | solution.py:46
  1417.0 21.8 %collective-permute-start.51 = (bf16[4,256,256]{2,1,0:T(8,128)(2,1)S(1)}, bf16[4,256,256]{2,1,0:T(8,128)(2,1)S(1)}, u32[]{:S(2)}, u32[]{:S(2)}) collective-permute-start(bf16[4,256,256]{2,1,0:T(8,128)(2,1)S(1)} %bitcast.701), channel_id=1, source_target_pairs={{0,4},{4,0},{1,5},{5,1},{2,6},{6,2},{3,7},{7,3},{8,12},{12,8},{9,1... | collective-permute-start | bytes 1572872 | tf_op jit(solution)/shard_map/ppermute | solution.py:46
  1418.5 49.3 %collective-permute-start.48 = (bf16[2,2,4,256,256]{4,3,2,1,0:T(8,128)(2,1)S(1)}, bf16[2,2,4,256,256]{4,3,2,1,0:T(8,128)(2,1)}, u32[]{:S(2)}, u32[]{:S(2)}) collective-permute-start(bf16[2,2,4,256,256]{4,3,2,1,0:T(8,128)(2,1)S(1)} %bitcast_dynamic-update-slice_fusion.6), channel_id=1, source_target_pairs={{0,1},{1,0},{2,3},{3,2},{4,5},{5,4},{6,7},{7,6},{8,9},{9,8},{10,11... | collective-permute-start | bytes 6291464 | tf_op jit(solution)/shard_map/ppermute | solution.py:46
  1418.6 21.0 %collective-permute-start.57 = (f32[2,7,32]{2,0,1:T(2,128)S(1)}, f32[2,7,32]{2,0,1:T(2,128)S(1)}, u32[]{:S(2)}, u32[]{:S(2)}) collective-permute-start(f32[2,7,32]{2,0,1:T(2,128)S(1)} %bitcast.767), channel_id=1, source_target_pairs={{0,2},{2,0},{1,3},{3,1},{4,6},{6,4},{5,7},{7,5},{8,10},{10,8},{9,1... | collective-permute-start | bytes 5384 | tf_op jit(solution)/shard_map/ppermute | solution.py:46
  1439.6 26.1 %collective-permute-start.52 = (bf16[2,4,256,256]{3,2,1,0:T(8,128)(2,1)}, bf16[2,4,256,256]{3,2,1,0:T(8,128)(2,1)}, u32[]{:S(2)}, u32[]{:S(2)}) collective-permute-start(bf16[2,4,256,256]{3,2,1,0:T(8,128)(2,1)} %bitcast_dynamic-update-slice_fusion.16), channel_id=1, source_target_pairs={{0,2},{2,0},{1,3},{3,1},{4,6},{6,4},{5,7},{7,5},{8,10},{10,8},{9,1... | collective-permute-start | bytes 3145736 | tf_op jit(solution)/shard_map/ppermute | solution.py:46
  1439.6 23.2 %collective-permute-start.58 = (f32[7,32]{1,0:T(8,128)S(1)}, f32[7,32]{1,0:T(8,128)S(1)}, u32[]{:S(2)}, u32[]{:S(2)}) collective-permute-start(f32[7,32]{1,0:T(8,128)S(1)} %bitcast.768), channel_id=1, source_target_pairs={{0,4},{4,0},{1,5},{5,1},{2,6},{6,2},{3,7},{7,3},{8,12},{12,8},{9,1... | collective-permute-start | bytes 2696 | tf_op jit(solution)/shard_map/ppermute | solution.py:46
  1467.0 25.2 %collective-permute-start.53 = (bf16[2,2,4,256,256]{4,3,2,1,0:T(8,128)(2,1)S(1)}, bf16[2,2,4,256,256]{4,3,2,1,0:T(8,128)(2,1)S(1)}, u32[]{:S(2)}, u32[]{:S(2)}) collective-permute-start(bf16[2,2,4,256,256]{4,3,2,1,0:T(8,128)(2,1)S(1)} %bitcast_dynamic-update-slice_fusion.4), channel_id=1, source_target_pairs={{0,1},{1,0},{2,3},{3,2},{4,5},{5,4},{6,7},{7,6},{8,9},{9,8},{10,11... | collective-permute-start | bytes 6291464 | tf_op jit(solution)/shard_map/ppermute | solution.py:46
  (192 other events, 5562.2 us)
Sparse Core Ops, SparseCore 0:
  11.6 64.8 all-gather.4
  80.1 56.0 all-gather.6
  984.0 210.4 reduce-scatter.1

commit v4 on v3

--- a/solution.py
+++ b/solution.py
@@ -28,6 +28,7 @@
 MESH = pl.DeviceIdType.MESH
 CHUNK = 256
 LANES = 3
+PREFIX_LOW = 192
 
 
 def step_rates():
@@ -65,18 +66,20 @@
     return held
 
 
-def sum_blocks(terms, layout, order, last=F32):
+def sum_blocks(terms, layout, order, last=F32, beside=None):
     left = list(layout)
     held = terms
     for axis in order:
         position = left.index(axis)
         bit = lax.axis_index(axis)
         received = swap(take_bit(held, 1 - bit, position), axis)
+        if beside is not None and axis == order[1]:
+            received, result = lax.optimization_barrier((received, beside(held)))
         held = take_bit(held, bit, position).astype(F32) + received.astype(F32)
         left.remove(axis)
         if left:
             held = held.astype(terms.dtype)
-    return held.astype(last)
+    return held.astype(last) if beside is None else (held.astype(last), result)
 
 
 def greet(axes):
@@ -233,7 +236,11 @@
 
 def grad_sums(lefts, rights, layout, orders, spans, collective):
     depth, lanes = len(layout), len(orders)
-    tokens, width = lefts[0].shape
+    tokens, width = max(left.shape[0] for left in lefts), lefts[0].shape[1]
+    lefts, rights = (
+        [jnp.pad(term, ((tokens - term.shape[0], 0), (0, 0))) for term in terms]
+        for terms in (lefts, rights)
+    )
     rows = width // 2**depth
     padded = -(-rows // 16) * 16
     blocks = jnp.stack(lefts).transpose(0, 2, 1).reshape(len(lefts), -1, 2, rows, tokens)
@@ -273,6 +280,76 @@
     return out[:chunks, :rows].transpose(1, 0, 2).reshape(rows, -1)
 
 
+def total_kernel(layout, value_ref, out_ref, send_ref, recv_ref, send_sem, recv_sem):
+    greet(layout)
+    held = value_ref[...]
+    for step, axis in enumerate(layout):
+        send_ref[step] = held
+        copy = pltpu.make_async_remote_copy(
+            src_ref=send_ref.at[step],
+            dst_ref=recv_ref.at[step],
+            send_sem=send_sem.at[step],
+            recv_sem=recv_sem.at[step],
+            device_id={axis: 1 - lax.axis_index(axis)},
+            device_id_type=MESH,
+        )
+        copy.start()
+        copy.wait()
+        held = held + recv_ref[step]
+    out_ref[...] = held
+
+
+def total_of(values, layout, collective):
+    depth = len(layout)
+    tile = jnp.broadcast_to(jnp.pad(values, (0, 8 - values.shape[0]))[:, None], (8, 128))
+    sums = pl.pallas_call(
+        partial(total_kernel, layout),
+        out_shape=jax.ShapeDtypeStruct(tile.shape, F32),
+        in_specs=[pl.BlockSpec(memory_space=pltpu.VMEM)],
+        out_specs=pl.BlockSpec(memory_space=pltpu.VMEM),
+        scratch_shapes=[pltpu.VMEM((depth, 8, 128), F32)] * 2
+        + [pltpu.SemaphoreType.DMA((depth,))] * 2,
+        compiler_params=pltpu.CompilerParams(collective_id=collective, has_side_effects=True),
+        name="sum_numbers",
+    )(tile)
+    return sums[: values.shape[0], 0]
+
+
+def rows_kernel(ids_ref, table_ref, out_ref, held_ref):
+    groups = held_ref.shape[0]
+    first = pl.program_id(0) * groups * 8
+
+    def eight(group, carry):
+        for k in range(8):
+            place = ids_ref[first + group * 8 + k]
+            held_ref[group, pl.ds(k, 1), :] = table_ref[pl.ds(place, 1), :]
+        return carry
+
+    lax.fori_loop(0, groups, eight, 0)
+    out_ref[...] = held_ref[...].reshape(out_ref.shape).astype(BF)
+
+
+def rows_of(table, places):
+    count, width = places.shape[0], table.shape[1]
+    step = 512
+    return pl.pallas_call(
+        rows_kernel,
+        grid=(count // step,),
+        out_shape=jax.ShapeDtypeStruct((count, width), BF),
+        in_specs=[
+            pl.BlockSpec(memory_space=pltpu.SMEM),
+            pl.BlockSpec(table.shape, lambda i: (0, 0)),
+        ],
+        out_specs=pl.BlockSpec((step, width), lambda i: (i, 0)),
+        scratch_shapes=[pltpu.VMEM((step // 8, 8, width), F32)],
+        compiler_params=pltpu.CompilerParams(vmem_limit_bytes=48 * 1024 * 1024),
+        cost_estimate=pl.CostEstimate(
+            flops=0, bytes_accessed=80 * count * width, transcendentals=0
+        ),
+        name="look_up",
+    )(places, table)
+
+
 def mm(left, right):
     return jnp.dot(left, right, preferred_element_type=F32)
 
@@ -303,13 +380,18 @@
     return lax.dot_general(left, right, (((1,), (1,)), ((), ())), preferred_element_type=F32)
 
 
+def allowed_keys(row_ref, shape, by_query, per_item):
+    queries = lax.broadcasted_iota(jnp.int32, shape, by_query)
+    keys = lax.broadcasted_iota(jnp.int32, shape, 1 - by_query)
+    each = shape[1 - by_query] // per_item
+    return row_ref[0] + queries * per_item >= lax.rem(keys, each) * per_item + keys // each
+
+
 def attend_kernel(causal, row_ref, q_ref, k_ref, v_ref, o_ref):
     rows, length = q_ref.shape[0], k_ref.shape[0]
     shape = (rows, length)
     if causal:
-        allowed = row_ref[0] + lax.broadcasted_iota(
-            jnp.int32, shape, 0
-        ) >= lax.broadcasted_iota(jnp.int32, shape, 1)
+        allowed = allowed_keys(row_ref, shape, 0, causal)
     for head in range(q_ref.shape[1] // HD):
         own = pl.ds(head * HD, HD)
         shared = pl.ds(head // (HQ // HK) * HD, HD)
@@ -327,9 +409,7 @@
     shape = (length, rows)
     share = HQ // HK
     if causal:
-        allowed = row_ref[0] + lax.broadcasted_iota(
-            jnp.int32, shape, 1
-        ) >= lax.broadcasted_iota(jnp.int32, shape, 0)
+        allowed = allowed_keys(row_ref, shape, 1, causal)
     for pair in range(k_ref.shape[1] // HD):
         shared = pl.ds(pair * HD, HD)
         keys, values = k_ref[:, shared], v_ref[:, shared]
@@ -365,11 +445,11 @@
     return queries, keys, values
 
 
-def attend_forward(queries, keyvals, first_row):
+def attend_forward(queries, keyvals, first_row, per_item):
     rows, length = queries.shape[0], keyvals.shape[0]
     by_query, by_key, by_value = attend_specs(rows, length)
     return pl.pallas_call(
-        partial(attend_kernel, first_row is not None),
+        partial(attend_kernel, 0 if first_row is None else per_item),
         grid=(KW // 128,),
         out_shape=jax.ShapeDtypeStruct(queries.shape, BF),
         in_specs=[pl.BlockSpec(memory_space=pltpu.SMEM), by_query, by_key, by_value],
@@ -384,11 +464,11 @@
     )(jnp.reshape(0 if first_row is None else first_row, (1,)), queries, keyvals, keyvals)
 
 
-def attend_backward(queries, keyvals, first_row, d_mixed):
+def attend_backward(queries, keyvals, first_row, per_item, d_mixed):
     rows, length = queries.shape[0], keyvals.shape[0]
     by_query, by_key, by_value = attend_specs(rows, length)
     d_queries, d_keys, d_values = pl.pallas_call(
-        partial(attend_back_kernel, first_row is not None),
+        partial(attend_back_kernel, 0 if first_row is None else per_item),
         grid=(KW // 128,),
         out_shape=[
             jax.ShapeDtypeStruct(queries.shape, BF),
@@ -458,7 +538,16 @@
 
     seq_count, length = source_ids.shape
     rows = length // 2 ** len(row_axes)
-    first_row = lax.axis_index(row_axes) * rows
+    per_item = 2 ** len(row_axes)
+    skip = PREFIX_LOW // per_item
+    first_row = lax.axis_index(row_axes)
+
+    def by_device(values):
+        return values.reshape(values.shape[:-1] + (rows, per_item)).swapaxes(-1, -2)
+
+    def with_skipped(values):
+        return jnp.pad(values, ((rows - values.shape[0], 0), (0, 0)))
+
 
     vocab_part = table.shape[0]
     offset = lax.axis_index(mp_axes) * vocab_part
@@ -466,49 +555,52 @@
     decoder_ids = jnp.concatenate(
         [jnp.zeros((seq_count, 1), jnp.int32), target_ids[:, :-1]], axis=1
     )
-    ids_all = gather_blocks(jnp.stack([source_ids, decoder_ids]), dp_axes, dp_axes)
-    ids_all = jnp.moveaxis(ids_all, len(dp_axes), 0).reshape(2, -1)
+    ids_all = by_device(gather_blocks(jnp.stack([source_ids, decoder_ids]), dp_axes, dp_axes))
+    ids_all = ids_all.reshape(-1, 2, 2 ** len(mp_axes), rows).transpose(1, 2, 0, 3).reshape(2, -1)
+    ids_all, sent_table = lax.optimization_barrier((ids_all, table_bf))
+    table_rows = lax.all_gather(sent_table, dp_axes, axis=1, tiled=True)
     local_ids = ids_all - offset
     inside = (local_ids >= 0) & (local_ids < vocab_part)
 
-    def embed(which):
-        found = jnp.where(
-            inside[which][:, None],
-            table_bf[jnp.clip(local_ids[which], 0, vocab_part - 1)],
-            jnp.zeros((), BF),
-        )
-        width = found.shape[-1]
-        found = found.reshape(two_dp + two_mp + (rows, width))
-        found = sum_blocks(found, dp_axes + mp_axes, mp_axes[::-1], BF)
+    def trade(parts):
         for position, axis in enumerate(dp_axes):
             bit = lax.axis_index(axis)
-            received = swap(take_bit(found, 1 - bit, position), axis)
-            kept = take_bit(found, bit, position)
-            found = jnp.stack(
+            received = swap(take_bit(parts, 1 - bit, position), axis)
+            kept = take_bit(parts, bit, position)
+            parts = jnp.stack(
                 [jnp.where(bit == 0, kept, received), jnp.where(bit == 0, received, kept)],
                 axis=position,
             )
-        found = found.reshape(-1, rows, width)
-        return jnp.moveaxis(found, 0, 1).reshape(rows, -1).astype(F32)
-
-    stream_e = embed(0)
-    stream_d = embed(1)
+        return parts
+
+    table_zero = jnp.pad(table, ((0, 8), (0, 0)))
+    places = jnp.where(inside, local_ids, vocab_part)
+
+    def look_up(which):
+        found = rows_of(table_zero, places[which])
+        return found.reshape(2 ** len(mp_axes), -1, found.shape[-1])
+
+    def collect(found):
+        return lax.psum_scatter(found, mp_axes, scatter_dimension=0)
+
+    def embed(mine):
+        width = mine.shape[-1]
+        parts = trade(mine.reshape(two_dp + (rows, width))).reshape(-1, rows, width)
+        return jnp.moveaxis(parts, 0, 1).reshape(rows, -1).astype(F32)
+
+    found_e = look_up(0)
+    mine_e = collect(found_e)
+    found_d = look_up(1)
+    mine_d = collect(found_d)
 
     shards = [attn_in[0], attn_out[0], ff_in[0], ff_out[0]]
     shards += [attn_in[1], attn_out[1], attn_in[2], attn_out[2], ff_in[1], ff_out[1]]
     shards = [shard.astype(BF) for shard in shards]
     in_kernels = attn_in.shape[1] % 16 == 0
     if in_kernels:
-        early = (0, 1)
-        full = [None] * len(shards)
-        for k in early:
-            full[k] = lax.all_gather(shards[k], every, axis=0, tiled=True)
-        late = [k for k in range(len(shards)) if k not in early]
-        held = lax.optimization_barrier([shards[k] for k in late] + [stream_e, stream_d])
-        stream_e, stream_d = held[-2:]
-        for k, got in zip(late, gather_all(held[:-2], every, six_orders)):
-            full[k] = got
-        full[4], table_bf = lax.optimization_barrier((full[4], table_bf))
+        *shards, found_e, found_d = lax.optimization_barrier(shards + [found_e, found_d])
+        full = list(gather_all(shards, every, six_orders))
+        full[0], mine_e, mine_d = lax.optimization_barrier((full[0], mine_e, mine_d))
     else:
         full = [
             gather_blocks(shard, every, gather_orders[k % 3]) for k, shard in enumerate(shards)
@@ -519,9 +611,6 @@
     gain_all = gather_blocks(gains.astype(BF).T, every, gather_orders[0])
     gain_all = gain_all.reshape(-1, gains.shape[0]).T.astype(F32)
 
-    table_rows = gather_blocks(table_bf, dp_axes, dp_axes[::-1]).reshape(-1, *table.shape)
-    table_rows = jnp.moveaxis(table_rows, 0, 1).reshape(vocab_part, -1)
-
     def spread_keys(own):
         return gather_blocks(own, row_axes, row_axes).reshape(length, -1)
 
@@ -529,9 +618,11 @@
         normed = norm_forward(stream, gain_row).astype(BF)
         anchor = normed if source is None else source
         keyvals = spread_keys(mm(anchor, a_in[block][:, QW:]).astype(BF))
-        queries = mm(normed, a_in[block][:, :QW]).astype(BF)
-        mixed = attend_forward(queries, keyvals, start)
-        out = stream + mm(mixed, a_out[block])
+        first = 0 if start is None else skip
+        queries = mm(normed[first:], a_in[block][:, :QW]).astype(BF)
+        position = None if start is None else start + first * per_item
+        mixed = attend_forward(queries, keyvals, position, per_item)
+        out = stream[first:] + mm(mixed, a_out[block])
         return (out, (stream, normed, anchor, queries, keyvals, mixed))
 
     def ffn_forward(stream, which, gain_row):
@@ -540,7 +631,10 @@
         hidden_act = (jax.nn.gelu(both[:, :FF], approximate=True) * both[:, FF:]).astype(BF)
         return (stream + mm(hidden_act, f_out[which]), (stream, normed, both, hidden_act))
 
+    stream_e = embed(mine_e)
     stream_e, enc_attn = attention_forward(stream_e, None, 0, gain_all[0], None)
+    stream_e, mine_d = lax.optimization_barrier((stream_e, mine_d))
+    stream_d = embed(mine_d)
     stream_d, dec_self = attention_forward(stream_d, None, 1, gain_all[3], first_row)
     stream_e, enc_ffn = ffn_forward(stream_e, 0, gain_all[1])
     encoded = norm_forward(stream_e, gain_all[2]).astype(BF)
@@ -549,7 +643,7 @@
     hidden = norm_forward(stream_d, gain_all[6]).astype(BF)
 
     hidden_all = gather_blocks(hidden, mp_axes, mp_axes).reshape(-1, hidden.shape[-1])
-    targets = target_ids.reshape(-1)
+    targets = by_device(target_ids)[..., skip:].reshape(-1)
     vocab_ids = offset + jnp.arange(vocab_part)
     hits = vocab_ids[None, :] == targets[:, None]
     logits = mm_nt(hidden_all, table_rows) * D ** (-0.5)
@@ -571,26 +665,24 @@
         )
     log_norm = stats[0] + jnp.log(stats[1])
     prefix_group = lax.dynamic_slice_in_dim(prefix, lax.axis_index(dp_axes) * seq_count, seq_count)
-    scored = (jnp.arange(length)[None, :] >= prefix_group[:, None]).astype(F32).reshape(-1)
+    positions = by_device(jnp.arange(length))[..., skip:].reshape(1, -1)
+    scored = (positions >= prefix_group[:, None]).astype(F32).reshape(-1)
     scored_count = jnp.sum((length - prefix).astype(F32))
     scale = jnp.exp(own_max - log_norm)
     d_logits = (
         (expo.astype(F32) * scale[:, None] - hits.astype(F32)) * (scored / scored_count)[:, None]
     ).astype(BF)
     d_final = (mm(d_logits, table_rows) * D ** (-0.5)).astype(BF)
-    d_final = sum_blocks(d_final.reshape(two_mp + (rows, -1)), mp_axes, mp_axes[::-1])
-
-    head_table = (mm_tn(d_logits, hidden_all) * D ** (-0.5)).astype(BF)
-    half = vocab_part // 2
-    width = table.shape[1]
-
-    def table_sum(part, order):
-        stacked = jnp.stack(jnp.split(part, 2 ** len(dp_axes), axis=1))
-        return sum_blocks(stacked.reshape(two_dp + part.shape[:1] + (width,)), dp_axes, order)
-
-    grad_table = jnp.concatenate(
-        [table_sum(head_table[:half], dp_axes), table_sum(head_table[half:], dp_axes[::-1])], axis=0
-    )
+
+    def table_term(held):
+        _, rows_all = lax.optimization_barrier((held, hidden_all))
+        return (mm_tn(d_logits, rows_all) * D ** (-0.5)).astype(BF)
+
+    d_final, head_table = sum_blocks(
+        d_final.reshape(two_mp + hidden.shape), mp_axes, mp_axes[::-1], F32, table_term
+    )
+
+    grad_table = lax.psum_scatter(head_table, dp_axes, scatter_dimension=1, tiled=True)
 
     def ffn_backward(saved, which, gain_row, d_stream):
         stream, normed, both, hidden_act = saved
@@ -609,24 +701,26 @@
         stream, normed, anchor, queries, keyvals, mixed = saved
         d_branch = d_stream.astype(BF)
         d_mixed = mm_nt(d_branch, a_out[block]).astype(BF)
-        d_queries, d_keyvals = attend_backward(queries, keyvals, start, d_mixed)
+        queries = with_skipped(queries)
+        d_queries, d_keyvals = attend_backward(
+            queries, keyvals, start, per_item, with_skipped(d_mixed)
+        )
         d_keyvals = sum_blocks(
             d_keyvals.reshape(two_rows + (rows, -1)), row_axes, row_axes[::-1], BF
         )
+        d_queries = d_queries[rows - stream.shape[0] :]
         d_normed = mm_nt(d_queries, a_in[block][:, :QW])
         d_anchor = mm_nt(d_keyvals, a_in[block][:, QW:])
         if not cross:
             d_normed = d_normed + d_anchor
-        factors = (normed, anchor, d_queries, d_keyvals, mixed, d_branch)
+        factors = (normed, anchor, with_skipped(d_queries), d_keyvals, mixed, d_branch)
         d_input, grad_gain = norm_backward(stream, gain_row, d_normed)
+        if start is not None:
+            d_stream = with_skipped(d_stream)
         return (d_stream + d_input, d_anchor, factors, grad_gain)
 
     d_y, gain6 = norm_backward(stream_d, gain_all[6], d_final)
     d_y, ffn_factors1, gain5 = ffn_backward(dec_ffn, 1, gain_all[5], d_y)
-    if in_kernels:
-        first_sum = lax.psum_scatter(
-            mm_tn(ffn_factors1[0], ffn_factors1[1]).astype(BF), every, scatter_dimension=0, tiled=True
-        ).astype(F32)
     d_y, d_encoded, attn_factors2, gain4 = attention_backward(
         dec_cross, True, 2, gain_all[4], None, d_y
     )
@@ -639,28 +733,17 @@
         enc_attn, False, 0, gain_all[0], None, d_x
     )
 
-    def spread_rows(d_rows):
+    def trade_rows(d_rows):
         width = table.shape[1]
-        piece = jnp.moveaxis(d_rows.astype(BF).reshape(rows, -1, width), 1, 0)
-        piece = piece.reshape(two_dp + (rows, width))
-        for position, axis in enumerate(dp_axes):
-            bit = lax.axis_index(axis)
-            received = swap(take_bit(piece, 1 - bit, position), axis)
-            kept = take_bit(piece, bit, position)
-            piece = jnp.stack(
-                [jnp.where(bit == 0, kept, received), jnp.where(bit == 0, received, kept)],
-                axis=position,
-            )
-        piece = piece.reshape((-1, rows, width))
-        everyone = gather_blocks(piece, mp_axes, mp_axes)
-        everyone = everyone.reshape((2 ** len(mp_axes), -1, rows, width))
-        return jnp.moveaxis(everyone, 0, 1).reshape(-1, width)
-
-    def look_back(which, d_rows):
+        parts = jnp.moveaxis(d_rows.astype(BF).reshape(rows, -1, width), 1, 0)
+        return trade(parts.reshape(two_dp + (rows, width))).reshape(-1, width)
+
+    def look_back(which, spread):
         places = (local_ids[which][None, :] == jnp.arange(vocab_part)[:, None]).astype(BF)
-        return mm(places, spread_rows(d_rows))
-
-    grad_table = grad_table + look_back(1, d_y) + look_back(0, d_x)
+        return mm(places, spread.reshape(-1, spread.shape[-1]))
+
+    traded_y, traded_x = trade_rows(d_y), trade_rows(d_x)
+    spread_y, spread_x = (lax.all_gather(traded, mp_axes) for traded in (traded_y, traded_x))
 
     gain_grads = jnp.stack([gain0, gain1, gain2, gain3, gain4, gain5, gain6])
     gain_blocks = jnp.moveaxis(gain_grads.reshape(gains.shape[0], -1, gains.shape[1]), 1, 0)
@@ -669,6 +752,12 @@
     )
 
     lefts, rights = [], []
+    if in_kernels:
+        traded_x, ffn_left, attn_left = lax.optimization_barrier(
+            (traded_x, ffn_factors0[2], attn_factors0[0])
+        )
+        attn_factors0 = (attn_left, attn_left) + attn_factors0[2:]
+        ffn_factors0 = ffn_factors0[:2] + (ffn_left,) + ffn_factors0[3:]
     for normed, anchor, d_queries, d_keyvals, mixed, d_branch in (
         attn_factors0,
         attn_factors1,
@@ -678,13 +767,12 @@
             lefts += [normed, mixed]
             rights += [jnp.concatenate([d_queries, d_keyvals], axis=1), d_branch]
         else:
-            lefts += [normed, anchor, mixed]
+            lefts += [with_skipped(normed), anchor, mixed]
             rights += [d_queries, d_keyvals, d_branch]
     wide_lefts, wide_rights = [], []
     for normed, d_both, hidden_act, d_branch in (ffn_factors0, ffn_factors1):
-        if hidden_act is ffn_factors0[2] or not in_kernels:
-            lefts.append(normed)
-            rights.append(d_both)
+        lefts.append(normed)
+        rights.append(d_both)
         wide_lefts.append(hidden_act)
         wide_rights.append(d_branch)
     spans = [right.shape[1] for right in rights]
@@ -692,8 +780,8 @@
     if in_kernels:
         back_orders = tuple(order[::-1] for order in three)
         own = grad_sums(lefts, rights, every, back_orders, spans, 1)
-        own = jnp.concatenate([own, first_sum], axis=1)
         wide = grad_sums(wide_lefts, wide_rights, every, back_orders, wide_spans, 2)
+        own, wide, spread_x, spread_y = lax.optimization_barrier((own, wide, spread_x, spread_y))
     else:
 
         def own_sum(left, right, kind):
@@ -705,6 +793,7 @@
         own = jnp.concatenate([own_sum(*pair, k) for k, pair in pairs], axis=1)
         pairs = list(enumerate(zip(wide_lefts, wide_rights)))
         wide = jnp.concatenate([own_sum(*pair, k) for k, pair in pairs], axis=1)
+    grad_table = grad_table.astype(F32) + look_back(1, spread_y) + look_back(0, spread_x)
     ends = (attn_in.shape[2], attn_in.shape[2] + attn_out.shape[2])
     ffn_from = 3 * ends[1]
     gradients = (
@@ -716,12 +805,11 @@
         grad_gains,
     )
 
-    own_losses = ((log_norm - stats[2]) * scored).reshape(2 ** len(mp_axes), rows)
+    own_losses = ((log_norm - stats[2]) * scored).reshape(2 ** len(mp_axes), -1)
     loss_part = jnp.sum(take_bit(own_losses, lax.axis_index(mp_axes), 0))
     squares = sum((jnp.sum(gradient * gradient) for gradient in gradients))
     totals = jnp.stack([loss_part, squares])
-    for axis in every[::-1]:
-        totals = totals + swap(totals, axis)
+    totals = total_of(totals, every[::-1], 3)
     loss_sum = totals[0]
     grad_norm = jnp.sqrt(totals[1])
     factor = jnp.minimum(1.0, CLIP / grad_norm)

time: 1580 us -> 1370 us (0.87)
  waiting for transfers between devices: 318 us -> 179 us
  Pallas kernels: 599 us -> 721 us
  local copies, waits for them, and re-layouts: 228 us -> 120 us
  other arithmetic: 145 us -> 95.1 us
  starting transfers between devices: 59.6 us -> 35.4 us
  matrix products: 204 us -> 185 us
    ppermute x64 -> x41, waiting for transfers between devices: 318 us -> 179 us  [swap(): return lax.ppermute(value, axis, [(0, 1), (1, 0)])]
    gather x2 -> x0, local copies, waits for them, and re-layouts: 66.1 us -> none  [embed(): table_bf[jnp.clip(local_ids[which], 0, vocab_part - 1)]]
    pallas_call x6 -> x9, Pallas kernels: 104 us -> 166 us  [the longest x3 63.2 us: attend_backward(): pl.pallas_call(partial(attend_back_kernel, 0 if first_row is None else pe...]
    pallas_call x1, Pallas kernels: 225 us -> 260 us  [gather_all(): pl.pallas_call(partial(gather_kernel, layout, tuple(units), LANES, count)...]
    pallas_call x2, Pallas kernels: 270 us -> 295 us  [grad_sums(): pl.pallas_call(partial(grad_kernel, layout, orders, tuple(bounds), chunks...]
    ppermute x64 -> x41, starting transfers between devices: 59.5 us -> 34.9 us  [swap(): return lax.ppermute(value, axis, [(0, 1), (1, 0)])]
    convert_element_type x13 -> x5, other arithmetic: 23.9 us -> 3.45 us  [sum_blocks(): held = held.astype(terms.dtype)]
    unnamed x366 -> x388, local copies, waits for them, and re-layouts: 37.2 us -> 38.8 us
  transfers between devices with their start and end apart: 67 -> 47, of which waited for: 33 -> 29; matrix products, arithmetic and copies ran while one was open for 27% -> 17% of each run, Pallas kernels for 37% -> 47%
where the time goes in v4:
time: 1370 us; the launch traced here: 1360 us
  Pallas kernels  721 us (53%)
  matrix products  185 us (14%)
  waiting for transfers between devices  179 us (13%)
  local copies, waits for them, and re-layouts  120 us (9%)
  other arithmetic  95.1 us (7%)
  starting transfers between devices  35.4 us (3%)
  between operations  25.4 us (2%)
    pallas_call x2, Pallas kernels, grad_sums(): pl.pallas_call(partial(grad_kernel, layout, orders, tuple(bounds), chunks...  295 us
    pallas_call x1, Pallas kernels, gather_all(): pl.pallas_call(partial(gather_kernel, layout, tuple(units), LANES, count)...  260 us
    ppermute x41, waiting for transfers between devices, swap(): return lax.ppermute(value, axis, [(0, 1), (1, 0)])  179 us
    dot_general x16, matrix products, mm(): return jnp.dot(left, right, preferred_element_type=F32)  98.8 us
    dot_general x14, matrix products, mm_nt(): lax.dot_general(left, right, (((1,), (1,)), ((), ())), preferred_element_...  67.3 us
    pallas_call x3, Pallas kernels, attend_backward(): pl.pallas_call(partial(attend_back_kernel, 0 if first_row is None else pe...  63.2 us
    pallas_call x2, Pallas kernels, rows_of(): pl.pallas_call(rows_kernel, grid=(count // step,), out_shape=jax.ShapeDty...  49.4 us
    unnamed x388, local copies, waits for them, and re-layouts  38.8 us
  transfers between devices with their start and end apart: 47, of which 29 were waited for; matrix products, arithmetic and copies ran while one was open for 17% of the time, Pallas kernels for 47%

profile of v4, /device:TPU:0, one launch (start us, length us, event | category | flops | bytes accessed | tf_op | source)
XLA Modules:
  0.0 1361.7 jit_solution(18147124670479446158)
XLA Ops:
  13.2 3.7 convert_element_type.369
  17.0 4.5 pad.62.table_ref
  31.4 24.7 %look_up.2 = bf16[8192,256]{1,0:T(8,128)(2,1)} custom-call(s32[8192]{0:T(1024)S(1)} %bitcast.483, f32[4024,256]{1,0:T(8,128)S(1)} %copy-done), custom_call_target="tpu_custom_call" | custom-call | bytes 167772160 | tf_op jit(solution)/shard_map/look_up/pallas_call | solution.py:335
  58.3 24.7 %look_up.3 = bf16[8192,256]{1,0:T(8,128)(2,1)} custom-call(s32[8192]{0:T(1024)S(1)} %bitcast.482, f32[4024,256]{1,0:T(8,128)S(1)} %copy-done.1), custom_call_target="tpu_custom_call" | custom-call | bytes 167772160 | tf_op jit(solution)/shard_map/look_up/pallas_call | solution.py:335
  93.7 260.4 %gather_weights.1 = (bf16[2,2,2,2,2,32,2048]{6,5,4,3,2,1,0:T(8,128)(2,1)}, bf16[2,2,2,2,2,32,1024]{6,5,4,3,2,1,0:T(8,128)(2,1)}, bf16[2,2,2,2,2,32,5632]{6,5,4,3...) custom-call(bf16[32,2048]{1,0:T(8,128)(2,1)} %get-tuple-element.67.r, ...), custom_call_target="tpu_custom_call" | custom-call | tf_op jit(solution)/shard_map/gather_weights/pallas_call | solution.py:154
  357.3 6.8 collective-permute-done.2
  378.4 11.7 collective-permute-done.9
  396.8 13.3 attend.3
  412.7 6.9 fusion.148
  425.5 5.3 collective-permute-done.11
  434.2 11.0 collective-permute-done.12
  452.6 10.2 collective-permute-done.13
  468.3 12.5 attend.4
  484.9 12.2 attend.5
  499.8 5.9 fusion.158
  509.9 22.2 %collective-permute-done.17 = bf16[208,1024]{1,0:T(8,128)(2,1)S(1)} collective-permute-done((bf16[208,1024]{1,0:T(8,128)(2,1)S(1)}, bf16[208,1024]{1,0:T(8,128)(2,1)S(1)}, u32[]{:S(2)}, u32[]{:S(2)}) %collective-permute-start.17) | collective-permute-done | bytes 426016 | tf_op jit(solution)/shard_map/ppermute | solution.py:47
  532.6 20.3 %collective-permute-done.18 = bf16[2,208,1024]{2,1,0:T(8,128)(2,1)S(1)} collective-permute-done((bf16[2,208,1024]{2,1,0:T(8,128)(2,1)S(1)}, bf16[2,208,1024]{2,1,0:T(8,128)(2,1)S(1)}, u32[]{:S(2)}, u32[]{:S(2)}) %collective-permute-start.18) | collective-permute-done | bytes 852000 | tf_op jit(solution)/shard_map/ppermute | solution.py:47
  561.6 18.7 %multiply_reduce_fusion = (f32[1664]{0:T(1024)S(1)}, f32[1664,4016]{0,1:T(8,128)S(1)}) fusion(bf16[1664,1024]{1,0:T(8,128)(2,1)} %bitcast.109, bf16[4016,1024]{1,0:T(8,128)(2,1)} %all-gather.4.cloned.1.call-done), kind=kOutput, calls=%fused_computation.15 | convolution fusion | flops 13699377152 | bytes 38369792 | tf_op jit(solution)/shard_map/dot_general | solution.py:358
  580.3 8.9 fusion.9
  596.3 4.5 collective-permute-done.22
  601.5 13.9 %fusion.7 = bf16[1664,4016]{0,1:T(8,128)(2,1)S(1)} fusion(f32[1664,4016]{0,1:T(8,128)} %copy-done.2, f32[1664]{0:T(1024)S(1)} %div.70, f32[1664]{0:T(1024)S(1)} %subtract_exponential_fusion.1, s32[1664]{0:T(1024)S(1)} %eq.31, f32[1664]{0:T(1024)S(1)} %get-tuple-element.269, s32[4016]{0:T(1024)S(1)} %iota_add_fusion), kind=kLoop, calls=%fused_computation.11 | loop fusion | flops 66826240 | bytes 40138432 | tf_op jit(solution)/shard_map/convert_element_type | solution.py:674
  615.4 17.2 %multiply_convert_fusion.1 = bf16[1664,1024]{1,0:T(8,128)(2,1)S(1)} fusion(bf16[1664,4016]{0,1:T(8,128)(2,1)S(1)} %fusion.7, bf16[4016,1024]{1,0:T(8,128)(2,1)} %all-gather.4.cloned.1.call-done), kind=kOutput, calls=%fused_computation.17 | convolution fusion | flops 13689421824 | bytes 24997888 | tf_op jit(solution)/shard_map/dot_general | solution.py:354
  633.3 3.6 collective-permute-done.23
  638.0 19.3 %multiply_convert_fusion = bf16[4016,1024]{1,0:T(8,128)(2,1)} fusion(bf16[1664,4016]{0,1:T(8,128)(2,1)S(1)} %fusion.7, bf16[1664,1024]{1,0:T(8,128)(2,1)} %bitcast.109), kind=kOutput, calls=%fused_computation.16 | convolution fusion | flops 13694238720 | bytes 24997888 | tf_op jit(solution)/shard_map/dot_general | solution.py:362
  662.4 19.1 %collective-permute-done.25 = bf16[208,1024]{1,0:T(8,128)(2,1)S(1)} collective-permute-done((bf16[208,1024]{1,0:T(8,128)(2,1)S(1)}, bf16[208,1024]{1,0:T(8,128)(2,1)S(1)}, u32[]{:S(2)}, u32[]{:S(2)}) %collective-permute-start.25) | collective-permute-done | bytes 426016 | tf_op jit(solution)/shard_map/ppermute | solution.py:47
  682.7 8.3 fusion.29
  691.1 9.3 multiply_reduce_fusion.16
  703.9 21.2 %attend_back.3 = (bf16[256,1024]{1,0:T(8,128)(2,1)}, bf16[1024,512]{1,0:T(8,128)(2,1)}, bf16[1024,512]{1,0:T(8,128)(2,1)}) custom-call(s32[1]{0:T(128)} %constant.321.clone.1.row_ref, bf16[256,1024]{1,0:T(8,128)(2,1)} %pad.67.q_ref, bf16[1024,1024]{1,0:T(8,128)(2,1)} %bitcast.535, bf16[1024,1024]{1,0:T(8,128)(2,1)} %bitcast.536, bf16[256,1024]{1,0:T(8,128)(2,1)} %pad.68.d_ref), custom_call_target="tpu_custom_call" | custom-call | flops 2684354560 | bytes 5767168 | tf_op jit(solution)/shard_map/attend_back/pallas_call | solution.py:470
  731.9 21.1 %attend_back.5 = (bf16[256,1024]{1,0:T(8,128)(2,1)}, bf16[1024,512]{1,0:T(8,128)(2,1)}, bf16[1024,512]{1,0:T(8,128)(2,1)}) custom-call(s32[1]{0:T(128)} %bitcast.141.row_ref, bf16[256,1024]{1,0:T(8,128)(2,1)} %pad.69.q_ref, bf16[1024,1024]{1,0:T(8,128)(2,1)} %bitcast.539, bf16[1024,1024]{1,0:T(8,128)(2,1)} %bitcast.540, bf16[256,1024]{1,0:T(8,128)(2,1)} %pad.70.d_ref), custom_call_target="tpu_custom_call" | custom-call | flops 2684354560 | bytes 5767168 | tf_op jit(solution)/shard_map/attend_back/pallas_call | solution.py:470
  762.4 10.6 collective-permute-done.31
  778.5 5.1 collective-permute-done.27
  789.7 4.9 collective-permute-done.35
  795.7 8.1 fusion.18
  803.8 8.2 multiply_reduce_fusion.5
  815.2 21.0 %attend_back.4 = (bf16[256,1024]{1,0:T(8,128)(2,1)}, bf16[1024,512]{1,0:T(8,128)(2,1)}, bf16[1024,512]{1,0:T(8,128)(2,1)}) custom-call(s32[1]{0:T(128)} %constant.321.clone.1.row_ref, bf16[256,1024]{1,0:T(8,128)(2,1)} %fusion.65.q_ref, bf16[1024,1024]{1,0:T(8,128)(2,1)} %bitcast.531, bf16[1024,1024]{1,0:T(8,128)(2,1)} %bitcast.532, ...), custom_call_target="tpu_custom_call" | custom-call | flops 2684354560 | bytes 5767168 | tf_op jit(solution)/shard_map/attend_back/pallas_call | solution.py:470
  842.6 12.7 collective-permute-done.29
  858.8 6.6 collective-permute-done.32
  867.1 5.1 collective-permute-done.33
  889.2 4.7 copy.258
  903.5 6.7 copy.250
  910.3 5.4 copy.251
  925.2 92.1 %sum_gradients.3 = f32[9,96,256]{2,1,0:T(8,128)} custom-call(bf16[2,2,1536,256]{3,2,1,0:T(8,128)(2,1)} %bitcast.495, bf16[256,2048]{1,0:T(8,128)(2,1)} %fusion.83.refs_1_), custom_call_target="tpu_custom_call" | custom-call | tf_op jit(solution)/shard_map/sum_gradients/pallas_call | solution.py:263
  1042.4 203.2 %sum_gradients.2 = f32[81,32,256]{2,1,0:T(8,128)} custom-call(bf16[9,2,512,256]{3,2,1,0:T(8,128)(2,1)} %bitcast.485, bf16[256,20480]{1,0:T(8,128)(2,1)} %pad_dynamic-update-slice_fusion.refs_1_), custom_call_target="tpu_custom_call" | custom-call | tf_op jit(solution)/shard_map/sum_gradients/pallas_call | solution.py:263
  1260.6 24.3 %fusion = f32[4016,256]{1,0:T(8,128)} fusion(bf16[8192,256]{1,0:T(8,128)(2,1)} %bitcast.615, s32[8192]{0:T(1024)S(1)} %bitcast.587), kind=kOutput, calls=%fused_computation.2 | convolution fusion | flops 16877223936 | bytes 8339456 | tf_op jit(solution)/shard_map/dot_general | solution.py:354
  1284.9 25.9 %multiply_reduce_fusion.1 = (f32[]{:T(128)}, f32[4016,256]{1,0:T(8,128)}) fusion(bf16[8192,256]{1,0:T(8,128)(2,1)} %bitcast.616, s32[8192]{0:T(1024)S(1)} %bitcast.586, f32[4016,256]{1,0:T(8,128)} %fusion, bf16[4016,256]{1,0:T(8,128)(2,1)} %reduce-scatter.8.cloned.1.call-done), kind=kOutput, calls=%fused_computation.25 | convolution fusion | flops 16882364416 | bytes 14508036 | tf_op jit(solution)/shard_map/dot_general | solution.py:354
  1313.7 15.0 %sum_numbers.1 = f32[8,128]{1,0:T(8,128)} custom-call(f32[8,128]{1,0:T(8,128)} %broadcast_in_dim.221.value_ref), custom_call_target="tpu_custom_call" | custom-call | tf_op jit(solution)/shard_map/sum_numbers/pallas_call | solution.py:305
  1330.7 3.5 multiply_add_fusion.6
  1340.6 11.7 multiply_add_fusion
  (744 shorter events, 240.0 us)
Async XLA Ops:
  8.0 346.1 %reduce-scatter.4.cloned.1.call-start = ((), (), s32[]{:S(2)}) async-start(), calls=%async_computation.3 | async-start | bytes 4718592 | tf_op jit(solution)/shard_map/reduce_scatter | solution.py:584
  9.5 11.9 collective-permute-start
  21.4 4.0 collective-permute-start.1
  56.1 298.0 %reduce-scatter.6.cloned.1.call-start = ((), (), s32[]{:S(2)}) async-start(), calls=%async_computation.4 | async-start | bytes 4718592 | tf_op jit(solution)/shard_map/reduce_scatter | solution.py:584
  83.1 478.5 %all-gather.4.cloned.1.call-start = ((), (), s32[]{:S(2)}) async-start(), calls=%async_computation.5 | async-start | bytes 10280960 | tf_op jit(solution)/shard_map/all_gather | solution.py:561
  83.7 5.3 collective-permute-start.4
  89.1 3.9 collective-permute-start.5
  93.1 263.1 %collective-permute-start.6 = (bf16[2,2,32,7]{2,1,3,0:T(2,128)(2,1)S(1)}, bf16[2,2,32,7]{2,1,3,0:T(2,128)(2,1)S(1)}, u32[]{:S(2)}, u32[]{:S(2)}) collective-permute-start(bf16[2,2,32,7]{2,1,3,0:T(2,128)(2,1)S(1)} %dynamic_update_slice.115), channel_id=1, source_target_pairs={{0,16},{16,0},{1,17},{17,1},{2,18},{18,2},{3,19},{19,3},{4,20},{20... | collective-permute-start | bytes 5384 | tf_op jit(solution)/shard_map/ppermute | solution.py:47
  355.1 9.0 collective-permute-start.2
  356.3 10.1 collective-permute-start.7
  365.2 8.2 collective-permute-start.3
  366.4 2.0 collective-permute-start.8
  370.4 112.9 %copy-start.130 = (f32[1,1024]{1,0:T(1,128)}, f32[1,1024]{1,0:T(1,128)S(1)}, u32[]{:S(2)}) copy-start(f32[1,1024]{1,0:T(1,128)S(1)} %get-tuple-element.224) | copy-start | bytes 12292
  377.1 12.9 collective-permute-start.9
  390.1 3.8 collective-permute-start.10
  390.2 860.7 %all-gather.8.cloned.1.call-start = ((), (), s32[]{:S(2)}) async-start(), calls=%async_computation.7 | async-start | bytes 4718592 | tf_op jit(solution)/shard_map/all_gather | solution.py:746
  422.1 8.7 collective-permute-start.11
  430.9 14.3 %collective-permute-start.12 = (bf16[2,256,256]{2,1,0:T(8,128)(2,1)S(1)}, bf16[2,256,256]{2,1,0:T(8,128)(2,1)S(1)}, u32[]{:S(2)}, u32[]{:S(2)}) collective-permute-start(bf16[2,256,256]{2,1,0:T(8,128)(2,1)S(1)} %fusion.99), channel_id=1, source_target_pairs={{0,8},{8,0},{1,9},{9,1},{2,10},{10,2},{3,11},{11,3},{4,12},{12,4},... | collective-permute-start | bytes 786440 | tf_op jit(solution)/shard_map/ppermute | solution.py:47
  433.7 17.6 %collective-permute-start.15 = (bf16[256,1024]{1,0:T(8,128)(2,1)}, bf16[256,1024]{1,0:T(8,128)(2,1)}, u32[]{:S(2)}, u32[]{:S(2)}) collective-permute-start(bf16[256,1024]{1,0:T(8,128)(2,1)} %get-tuple-element.264), channel_id=1, source_target_pairs={{0,2},{2,0},{1,3},{3,1},{4,6},{6,4},{5,7},{7,5},{8,10},{10,8},{9,1... | collective-permute-start | bytes 1572872 | tf_op jit(solution)/shard_map/ppermute | solution.py:47
  450.1 12.8 collective-permute-start.13
  452.4 13.8 %collective-permute-start.16 = (bf16[2,256,1024]{2,1,0:T(8,128)(2,1)S(1)}, bf16[2,256,1024]{2,1,0:T(8,128)(2,1)S(1)}, u32[]{:S(2)}, u32[]{:S(2)}) collective-permute-start(bf16[2,256,1024]{2,1,0:T(8,128)(2,1)S(1)} %bitcast_dynamic-update-slice_fusion.18), channel_id=1, source_target_pairs={{0,1},{1,0},{2,3},{3,2},{4,5},{5,4},{6,7},{7,6},{8,9},{9,8},{10,11... | collective-permute-start | bytes 3145736 | tf_op jit(solution)/shard_map/ppermute | solution.py:47
  464.0 2.7 collective-permute-start.14
  509.8 22.3 %collective-permute-start.17 = (bf16[208,1024]{1,0:T(8,128)(2,1)S(1)}, bf16[208,1024]{1,0:T(8,128)(2,1)S(1)}, u32[]{:S(2)}, u32[]{:S(2)}) collective-permute-start(bf16[208,1024]{1,0:T(8,128)(2,1)S(1)} %get-tuple-element.165), channel_id=1, source_target_pairs={{0,4},{4,0},{1,5},{5,1},{2,6},{6,2},{3,7},{7,3},{8,12},{12,8},{9,1... | collective-permute-start | bytes 1277960 | tf_op jit(solution)/shard_map/ppermute | solution.py:47
  532.2 20.6 %collective-permute-start.18 = (bf16[2,208,1024]{2,1,0:T(8,128)(2,1)S(1)}, bf16[2,208,1024]{2,1,0:T(8,128)(2,1)S(1)}, u32[]{:S(2)}, u32[]{:S(2)}) collective-permute-start(bf16[2,208,1024]{2,1,0:T(8,128)(2,1)S(1)} %bitcast_dynamic-update-slice_fusion.24), channel_id=1, source_target_pairs={{0,2},{2,0},{1,3},{3,1},{4,6},{6,4},{5,7},{7,5},{8,10},{10,8},{9,1... | collective-permute-start | bytes 2555912 | tf_op jit(solution)/shard_map/ppermute | solution.py:47
  552.9 7.4 collective-permute-start.19
  589.3 1.4 collective-permute-start.20
  591.4 3.9 collective-permute-start.21
  596.0 4.8 collective-permute-start.22
  633.2 3.7 collective-permute-start.23
  637.7 21.2 %collective-permute-start.24 = (bf16[2,208,1024]{2,1,0:T(8,128)(2,1)S(1)}, bf16[2,208,1024]{2,1,0:T(8,128)(2,1)}, u32[]{:S(2)}, u32[]{:S(2)}) collective-permute-start(bf16[2,208,1024]{2,1,0:T(8,128)(2,1)S(1)} %dynamic-slice_bitcast_fusion.3), channel_id=1, source_target_pairs={{0,2},{2,0},{1,3},{3,1},{4,6},{6,4},{5,7},{7,5},{8,10},{10,8},{9,1... | collective-permute-start | bytes 2555912 | tf_op jit(solution)/shard_map/ppermute | solution.py:47
  660.4 21.1 %collective-permute-start.25 = (bf16[208,1024]{1,0:T(8,128)(2,1)S(1)}, bf16[208,1024]{1,0:T(8,128)(2,1)S(1)}, u32[]{:S(2)}, u32[]{:S(2)}) collective-permute-start(bf16[208,1024]{1,0:T(8,128)(2,1)S(1)} %dynamic-slice_bitcast_fusion.7), channel_id=1, source_target_pairs={{0,4},{4,0},{1,5},{5,1},{2,6},{6,2},{3,7},{7,3},{8,12},{12,8},{9,1... | collective-permute-start | bytes 1277960 | tf_op jit(solution)/shard_map/ppermute | solution.py:47
  755.0 2.7 collective-permute-start.30
  755.6 3.7 collective-permute-start.26
  758.2 14.8 %collective-permute-start.31 = (bf16[256,1024]{1,0:T(8,128)(2,1)S(1)}, bf16[256,1024]{1,0:T(8,128)(2,1)S(1)}, u32[]{:S(2)}, u32[]{:S(2)}) collective-permute-start(bf16[256,1024]{1,0:T(8,128)(2,1)S(1)} %dynamic-slice_bitcast_fusion.4), channel_id=1, source_target_pairs={{0,2},{2,0},{1,3},{3,1},{4,6},{6,4},{5,7},{7,5},{8,10},{10,8},{9,1... | collective-permute-start | bytes 1572872 | tf_op jit(solution)/shard_map/ppermute | solution.py:47
  760.6 23.0 %collective-permute-start.27 = (bf16[256,1024]{1,0:T(8,128)(2,1)}, bf16[256,1024]{1,0:T(8,128)(2,1)}, u32[]{:S(2)}, u32[]{:S(2)}) collective-permute-start(bf16[256,1024]{1,0:T(8,128)(2,1)} %dynamic-slice_bitcast_fusion.6), channel_id=1, source_target_pairs={{0,2},{2,0},{1,3},{3,1},{4,6},{6,4},{5,7},{7,5},{8,10},{10,8},{9,1... | collective-permute-start | bytes 1572872 | tf_op jit(solution)/shard_map/ppermute | solution.py:47
  777.5 9.5 collective-permute-start.34
  787.0 7.6 collective-permute-start.35
  795.6 455.2 %all-gather.6.cloned.1.call-start = ((), (), s32[]{:S(2)}) async-start(), calls=%async_computation.6 | async-start | bytes 4718592 | tf_op jit(solution)/shard_map/all_gather | solution.py:746
  838.1 2.7 collective-permute-start.28
  841.3 14.0 %collective-permute-start.29 = (bf16[256,1024]{1,0:T(8,128)(2,1)S(1)}, bf16[256,1024]{1,0:T(8,128)(2,1)S(1)}, u32[]{:S(2)}, u32[]{:S(2)}) collective-permute-start(bf16[256,1024]{1,0:T(8,128)(2,1)S(1)} %dynamic-slice_bitcast_fusion.5), channel_id=1, source_target_pairs={{0,2},{2,0},{1,3},{3,1},{4,6},{6,4},{5,7},{7,5},{8,10},{10,8},{9,1... | collective-permute-start | bytes 1572872 | tf_op jit(solution)/shard_map/ppermute | solution.py:47
  857.9 7.6 collective-permute-start.32
  865.6 6.7 collective-permute-start.33
  873.2 411.7 %reduce-scatter.8.cloned.1.call-start = ((), (), s32[]{:S(2)}) async-start(), calls=%async_computation.8 | async-start | bytes 10280960 | tf_op jit(solution)/shard_map/reduce_scatter | solution.py:685
  1020.7 10.0 collective-permute-start.36
  1030.7 3.9 collective-permute-start.37
  1034.7 4.5 collective-permute-start.38
  1039.2 206.4 %collective-permute-start.39 = (f32[2,7,32]{2,0,1:T(2,128)S(1)}, f32[2,7,32]{2,0,1:T(2,128)S(1)}, u32[]{:S(2)}, u32[]{:S(2)}) collective-permute-start(f32[2,7,32]{2,0,1:T(2,128)S(1)} %bitcast.591), channel_id=1, source_target_pairs={{0,2},{2,0},{1,3},{3,1},{4,6},{6,4},{5,7},{7,5},{8,10},{10,8},{9,1... | collective-permute-start | bytes 5384 | tf_op jit(solution)/shard_map/ppermute | solution.py:47
  1245.7 4.6 collective-permute-start.40
  (182 other events, 1697.9 us)
Sparse Core Ops, SparseCore 0:
  56.2 50.4 reduce-scatter.3
  109.0 55.3 reduce-scatter.5
  795.7 45.2 all-gather.7
  873.3 45.0 all-gather.5
Sparse Core Ops, SparseCore 1:
  390.3 91.6 all-gather.3
  876.9 105.9 reduce-scatter.7

commit v5 on v4

--- a/solution.py
+++ b/solution.py
@@ -164,19 +164,53 @@
     )(*shards)
 
 
-def grad_kernel(layout, orders, bounds, chunks, *refs):
-    x_ref, y_ref, out_ref = refs[:3]
+def grad_kernel(layout, orders, bounds, chunks, counts, *refs):
+    lefts, rights = refs[: counts[0]], refs[counts[0] : sum(counts)]
+    out_ref = refs[sum(counts)]
+    scratch = refs[sum(counts) + 1 :]
     depth = len(layout)
     lanes = len(orders)
-    scratch = refs[3:]
     sends, recvs, helds = (
         [scratch[kind * lanes * depth + lane * depth :][:depth] for lane in range(lanes)]
         for kind in range(3)
     )
-    send_sem, recv_sem = scratch[3 * lanes * depth :]
+    given_ref, x_ref, y_ref, in_sem, send_sem, recv_sem = scratch[3 * lanes * depth :]
     bits = {axis: lax.axis_index(axis) for axis in layout}
-    groups = out_ref.shape[0] // lanes
+    groups = out_ref.shape[1] // CHUNK // lanes
+    tokens = y_ref.shape[0]
+
+    copies, passed = [], 0
+    for k, term in enumerate(lefts + rights):
+        absent = tokens - term.shape[0]
+        if k < len(lefts):
+            place = given_ref.at[k]
+        else:
+            place = y_ref.at[:, pl.ds(passed, term.shape[1])]
+            passed += term.shape[1]
+        if absent:
+            place[pl.ds(0, absent), :] = jnp.zeros((absent, term.shape[1]), BF)
+        copy = pltpu.make_async_copy(term, place.at[pl.ds(absent, term.shape[0])], in_sem.at[k])
+        copy.start()
+        copies.append(copy)
     greet(layout)
+    padded = x_ref.shape[2] * 2 // 2**depth
+
+    def turned(k):
+        copies[k].wait()
+        rows = lefts[k].shape[1] // 2**depth
+        across = given_ref[k].astype(F32).T.reshape(-1, 2, rows, tokens)
+        for bit in range(2):
+            blocks = across[:, bit]
+            if padded > rows:
+                filler = jnp.zeros((blocks.shape[0], padded - rows, tokens), F32)
+                blocks = jnp.concatenate([blocks, filler], axis=1)
+            x_ref[k, bit] = blocks.reshape(-1, tokens).astype(BF)
+    for copy in copies[len(lefts) :]:
+        copy.wait()
+    turned(0)
+    early = [k for k in range(1, len(lefts)) if bounds[k - 1] // lanes < k - 1]
+    for k in early:
+        turned(k)
 
     def exchange(lane, step, group):
         axis = orders[lane][step]
@@ -207,7 +241,10 @@
         exchange(lane, step - 1, group).wait()
         held, received = helds[lane][step - 1], recvs[lane][step - 1]
         if step == depth:
-            out_ref[group * lanes + lane] = held[...] + received[slot].astype(F32)
+            chunk = group * lanes + lane
+            out_ref[:, pl.ds(pl.multiple_of(chunk * CHUNK, CHUNK), CHUNK)] = held[
+                ...
+            ] + received[slot].astype(F32)
             return
         position = [axis for axis in layout if axis not in order[:step]].index(order[step])
         bit = bits[order[step]]
@@ -222,6 +259,9 @@
 
     @pl.loop(0, groups + depth)
     def _(turn):
+        for k in range(1, len(lefts)):
+            if k not in early:
+                pl.when(turn == k - 1)(partial(turned, k))
         for step in reversed(range(depth + 1)):
             group = turn - step
 
@@ -237,17 +277,10 @@
 def grad_sums(lefts, rights, layout, orders, spans, collective):
     depth, lanes = len(layout), len(orders)
     tokens, width = max(left.shape[0] for left in lefts), lefts[0].shape[1]
-    lefts, rights = (
-        [jnp.pad(term, ((tokens - term.shape[0], 0), (0, 0))) for term in terms]
-        for terms in (lefts, rights)
-    )
     rows = width // 2**depth
     padded = -(-rows // 16) * 16
-    blocks = jnp.stack(lefts).transpose(0, 2, 1).reshape(len(lefts), -1, 2, rows, tokens)
-    blocks = jnp.pad(blocks, ((0, 0),) * 3 + ((0, padded - rows), (0, 0)))
-    x = blocks.swapaxes(1, 2).reshape(len(lefts), 2, -1, tokens)
-    y = jnp.concatenate(rights, axis=1)
-    chunks = y.shape[1] // CHUNK
+    total = sum(right.shape[1] for right in rights)
+    chunks = total // CHUNK
     groups = -(-chunks // lanes)
     bounds, passed = [], 0
     for span in spans[:-1]:
@@ -260,15 +293,20 @@
             send_shapes.append(pltpu.VMEM(shape, BF))
             recv_shapes.append(pltpu.VMEM((2,) + shape, BF))
             held_shapes.append(pltpu.VMEM(shape, F32))
+    counts = (len(lefts), len(rights))
     out = pl.pallas_call(
-        partial(grad_kernel, layout, orders, tuple(bounds), chunks),
-        out_shape=jax.ShapeDtypeStruct((groups * lanes, padded, CHUNK), F32),
-        in_specs=[pl.BlockSpec(memory_space=pltpu.VMEM)] * 2,
+        partial(grad_kernel, layout, orders, tuple(bounds), chunks, counts),
+        out_shape=jax.ShapeDtypeStruct((padded, groups * lanes * CHUNK), F32),
+        in_specs=[pl.BlockSpec(memory_space=pl.ANY)] * sum(counts),
         out_specs=pl.BlockSpec(memory_space=pltpu.VMEM),
         scratch_shapes=send_shapes
         + recv_shapes
         + held_shapes
         + [
+            pltpu.VMEM((len(lefts), tokens, width), BF),
+            pltpu.VMEM((len(lefts), 2, 2 ** (depth - 1) * padded, tokens), BF),
+            pltpu.VMEM((tokens, total), BF),
+            pltpu.SemaphoreType.DMA((sum(counts),)),
             pltpu.SemaphoreType.DMA((lanes, depth)),
             pltpu.SemaphoreType.DMA((lanes, depth, 2)),
         ],
@@ -276,8 +314,8 @@
             collective_id=collective, has_side_effects=True, vmem_limit_bytes=56 * 1024 * 1024
         ),
         name="sum_gradients",
-    )(x, y)
-    return out[:chunks, :rows].transpose(1, 0, 2).reshape(rows, -1)
+    )(*lefts, *rights)
+    return out[:rows, :total]
 
 
 def total_kernel(layout, value_ref, out_ref, send_ref, recv_ref, send_sem, recv_sem):
@@ -557,8 +595,7 @@
     )
     ids_all = by_device(gather_blocks(jnp.stack([source_ids, decoder_ids]), dp_axes, dp_axes))
     ids_all = ids_all.reshape(-1, 2, 2 ** len(mp_axes), rows).transpose(1, 2, 0, 3).reshape(2, -1)
-    ids_all, sent_table = lax.optimization_barrier((ids_all, table_bf))
-    table_rows = lax.all_gather(sent_table, dp_axes, axis=1, tiled=True)
+    table_rows = lax.all_gather(table_bf, dp_axes, axis=1, tiled=True)
     local_ids = ids_all - offset
     inside = (local_ids >= 0) & (local_ids < vocab_part)
 
@@ -598,9 +635,18 @@
     shards = [shard.astype(BF) for shard in shards]
     in_kernels = attn_in.shape[1] % 16 == 0
     if in_kernels:
-        *shards, found_e, found_d = lax.optimization_barrier(shards + [found_e, found_d])
-        full = list(gather_all(shards, every, six_orders))
+        *shards, found_e, found_d, table_rows = lax.optimization_barrier(
+            shards + [found_e, found_d, table_rows]
+        )
+        behind = (8, 9,)
+        full = [None] * len(shards)
+        ahead = [k for k in range(len(shards)) if k not in behind]
+        for k, got in zip(ahead, gather_all([shards[k] for k in ahead], every, six_orders)):
+            full[k] = got
         full[0], mine_e, mine_d = lax.optimization_barrier((full[0], mine_e, mine_d))
+        full[0], *sent = lax.optimization_barrier([full[0]] + [shards[k] for k in behind])
+        for k, shard in zip(behind, sent):
+            full[k] = lax.all_gather(shard, every, axis=0, tiled=True)
     else:
         full = [
             gather_blocks(shard, every, gather_orders[k % 3]) for k, shard in enumerate(shards)
@@ -713,7 +759,7 @@
         d_anchor = mm_nt(d_keyvals, a_in[block][:, QW:])
         if not cross:
             d_normed = d_normed + d_anchor
-        factors = (normed, anchor, with_skipped(d_queries), d_keyvals, mixed, d_branch)
+        factors = (normed, anchor, d_queries, d_keyvals, mixed, d_branch)
         d_input, grad_gain = norm_backward(stream, gain_row, d_normed)
         if start is not None:
             d_stream = with_skipped(d_stream)
@@ -727,6 +773,7 @@
     d_y, _, attn_factors1, gain3 = attention_backward(
         dec_self, False, 1, gain_all[3], first_row, d_y
     )
+    d_encoded, grad_table = lax.optimization_barrier((d_encoded, grad_table))
     d_x, gain2 = norm_backward(stream_e, gain_all[2], d_encoded)
     d_x, ffn_factors0, gain1 = ffn_backward(enc_ffn, 0, gain_all[1], d_x)
     d_x, _, attn_factors0, gain0 = attention_backward(
@@ -751,36 +798,34 @@
         gain_blocks.reshape((2,) * len(every) + gains.shape), every, sum_orders[0]
     )
 
-    lefts, rights = [], []
     if in_kernels:
         traded_x, ffn_left, attn_left = lax.optimization_barrier(
             (traded_x, ffn_factors0[2], attn_factors0[0])
         )
         attn_factors0 = (attn_left, attn_left) + attn_factors0[2:]
         ffn_factors0 = ffn_factors0[:2] + (ffn_left,) + ffn_factors0[3:]
+    lefts, rights, spans = [], [], []
     for normed, anchor, d_queries, d_keyvals, mixed, d_branch in (
         attn_factors0,
         attn_factors1,
         attn_factors2,
     ):
-        if anchor is normed:
-            lefts += [normed, mixed]
-            rights += [jnp.concatenate([d_queries, d_keyvals], axis=1), d_branch]
-        else:
-            lefts += [with_skipped(normed), anchor, mixed]
-            rights += [d_queries, d_keyvals, d_branch]
+        lefts += [normed, mixed] if anchor is normed else [normed, anchor, mixed]
+        rights += [d_queries, d_keyvals, d_branch]
+        widths = [d_queries.shape[1], d_keyvals.shape[1]]
+        spans += ([sum(widths)] if anchor is normed else widths) + [d_branch.shape[1]]
     wide_lefts, wide_rights = [], []
     for normed, d_both, hidden_act, d_branch in (ffn_factors0, ffn_factors1):
         lefts.append(normed)
         rights.append(d_both)
+        spans.append(d_both.shape[1])
         wide_lefts.append(hidden_act)
         wide_rights.append(d_branch)
-    spans = [right.shape[1] for right in rights]
     wide_spans = [right.shape[1] for right in wide_rights]
     if in_kernels:
         back_orders = tuple(order[::-1] for order in three)
         own = grad_sums(lefts, rights, every, back_orders, spans, 1)
-        wide = grad_sums(wide_lefts, wide_rights, every, back_orders, wide_spans, 2)
+        wide = grad_sums(wide_lefts, wide_rights, every, back_orders[:2], wide_spans, 2)
         own, wide, spread_x, spread_y = lax.optimization_barrier((own, wide, spread_x, spread_y))
     else:
 
@@ -789,7 +834,10 @@
             blocks = product.reshape((2,) * len(every) + (-1,) + product.shape[1:])
             return sum_blocks(blocks, every, sum_orders[kind % 3])
 
-        pairs = list(enumerate(zip(lefts, rights)))
+        everything = jnp.concatenate([with_skipped(right) for right in rights], axis=1)
+        ends = [sum(spans[: k + 1]) for k in range(len(spans))]
+        parts = jnp.split(everything, ends[:-1], axis=1)
+        pairs = list(enumerate(zip([with_skipped(left) for left in lefts], parts)))
         own = jnp.concatenate([own_sum(*pair, k) for k, pair in pairs], axis=1)
         pairs = list(enumerate(zip(wide_lefts, wide_rights)))
         wide = jnp.concatenate([own_sum(*pair, k) for k, pair in pairs], axis=1)

time: 1370 us -> 1250 us (0.912)
  Pallas kernels: 721 us -> 628 us
  local copies, waits for them, and re-layouts: 120 us -> 76.9 us
  waiting for transfers between devices: 179 us -> 210 us
    pallas_call x1, Pallas kernels: 260 us -> 188 us  [gather_all(): pl.pallas_call(partial(gather_kernel, layout, tuple(units), LANES, count)...]
    transpose x7 -> x0, local copies, waits for them, and re-layouts: 21.6 us -> none  [the longest x2 11.4 us: grad_sums(): jnp.stack(lefts).transpose(0, 2, 1).reshape(len(lefts), -1, 2, rows, tokens)]
    all_gather x1 -> x3, waiting for transfers between devices: 0.01 us -> 20.1 us  [the longest x1 14.9 us: on_device(): table_rows = lax.all_gather(table_bf, dp_axes, axis=1, tiled=True)]
    pallas_call x2, Pallas kernels: 295 us -> 276 us  [grad_sums(): pl.pallas_call(partial(grad_kernel, layout, orders, tuple(bounds), chunks...]
    unnamed x388 -> x295, local copies, waits for them, and re-layouts: 38.8 us -> 29.3 us
  transfers between devices with their start and end apart: 47 -> 49, of which waited for: 29 -> 31; matrix products, arithmetic and copies ran while one was open for 17% -> 13% of each run, Pallas kernels for 47% -> 50%
where the time goes in v5:
time: 1250 us; the launch traced here: 1240 us
  Pallas kernels  628 us (50%)
  waiting for transfers between devices  210 us (17%)
  matrix products  180 us (14%)
  other arithmetic  81.7 us (7%)
  local copies, waits for them, and re-layouts  76.9 us (6%)
  starting transfers between devices  35.7 us (3%)
  between operations  25.6 us (2%)
    pallas_call x2, Pallas kernels, grad_sums(): pl.pallas_call(partial(grad_kernel, layout, orders, tuple(bounds), chunks...  276 us
    ppermute x41, waiting for transfers between devices, swap(): return lax.ppermute(value, axis, [(0, 1), (1, 0)])  189 us
    pallas_call x1, Pallas kernels, gather_all(): pl.pallas_call(partial(gather_kernel, layout, tuple(units), LANES, count)...  188 us
    dot_general x16, matrix products, mm(): return jnp.dot(left, right, preferred_element_type=F32)  98.3 us
    dot_general x14, matrix products, mm_nt(): lax.dot_general(left, right, (((1,), (1,)), ((), ())), preferred_element_...  64.3 us
    pallas_call x3, Pallas kernels, attend_backward(): pl.pallas_call(partial(attend_back_kernel, 0 if first_row is None else pe...  63.5 us
    pallas_call x2, Pallas kernels, rows_of(): pl.pallas_call(rows_kernel, grid=(count // step,), out_shape=jax.ShapeDty...  49.4 us
    pallas_call x3, Pallas kernels, attend_forward(): pl.pallas_call(partial(attend_kernel, 0 if first_row is None else per_ite...  37.9 us
  transfers between devices with their start and end apart: 49, of which 31 were waited for; matrix products, arithmetic and copies ran while one was open for 13% of the time, Pallas kernels for 50%

profile of v5, /device:TPU:0, one launch (start us, length us, event | category | flops | bytes accessed | tf_op | source)
XLA Modules:
  0.0 1237.7 jit_solution(683806011079157889)
XLA Ops:
  8.1 3.7 convert_element_type.332
  15.0 4.5 pad.26.table_ref
  29.0 24.7 %look_up.2 = bf16[8192,256]{1,0:T(8,128)(2,1)} custom-call(s32[8192]{0:T(1024)S(1)} %bitcast.438, f32[4024,256]{1,0:T(8,128)S(1)} %copy-done), custom_call_target="tpu_custom_call" | custom-call | bytes 167772160 | tf_op jit(solution)/shard_map/look_up/pallas_call | solution.py:373
  56.1 24.7 %look_up.3 = bf16[8192,256]{1,0:T(8,128)(2,1)} custom-call(s32[8192]{0:T(1024)S(1)} %bitcast.437, f32[4024,256]{1,0:T(8,128)S(1)} %copy-done.1), custom_call_target="tpu_custom_call" | custom-call | bytes 167772160 | tf_op jit(solution)/shard_map/look_up/pallas_call | solution.py:373
  85.9 14.9 %all-gather.6.cloned.1.call-done = bf16[4016,1024]{1,0:T(8,128)(2,1)} async-done(((bf16[4016,256]{1,0:T(8,128)(2,1)}), bf16[4016,1024]{1,0:T(8,128)(2,1)}) %all-gather.6.cloned.1.call-update) | async-done | bytes 8224784 | tf_op jit(solution)/shard_map/all_gather | solution.py:598
  100.7 188.4 %gather_weights.1 = (bf16[2,2,2,2,2,32,2048]{6,5,4,3,2,1,0:T(8,128)(2,1)}, bf16[2,2,2,2,2,32,1024]{6,5,4,3,2,1,0:T(8,128)(2,1)}, bf16[2,2,2,2,2,32,5632]{6,5,4,3...) custom-call(bf16[32,2048]{1,0:T(8,128)(2,1)} %get-tuple-element.68.r, ...), custom_call_target="tpu_custom_call" | custom-call | tf_op jit(solution)/shard_map/gather_weights/pallas_call | solution.py:154
  289.5 4.4 collective-permute-done.4
  301.6 4.9 collective-permute-done.2
  319.8 24.7 %collective-permute-done.9 = bf16[256,1024]{1,0:T(8,128)(2,1)S(1)} collective-permute-done((bf16[256,1024]{1,0:T(8,128)(2,1)S(1)}, bf16[256,1024]{1,0:T(8,128)(2,1)S(1)}, u32[]{:S(2)}, u32[]{:S(2)}) %collective-permute-start.9) | collective-permute-done | bytes 524320 | tf_op jit(solution)/shard_map/ppermute | solution.py:47
  351.4 13.5 %attend.3.refs_1_ = bf16[256,1024]{1,0:T(8,128)(2,1)} custom-call(s32[1]{0:T(128)} %constant.321.clone.1.row_ref, bf16[256,1024]{1,0:T(8,128)(2,1)} %fusion.61.q_ref, bf16[1024,1024]{1,0:T(8,128)(2,1)} %bitcast.472, bf16[1024,1024]{1,0:T(8,128)(2,1)} %bitcast.473), custom_call_target="tpu_custom_call" | custom-call | flops 1073741824 | bytes 3145728 | tf_op jit(solution)/shard_map/attend/pallas_call | solution.py:489
  369.2 6.3 fusion.142
  384.2 5.0 collective-permute-done.12
  393.8 7.6 collective-permute-done.15
  402.7 11.2 collective-permute-done.13
  421.7 12.2 attend.4.refs_3_
  437.9 12.2 attend.5.refs_6_
  452.9 5.8 fusion.143
  461.8 5.2 all-gather.10.cloned.1.call-done
  467.0 4.1 multiply_reduce_fusion.21
  473.7 19.8 %collective-permute-done.17 = bf16[208,1024]{1,0:T(8,128)(2,1)S(1)} collective-permute-done((bf16[208,1024]{1,0:T(8,128)(2,1)S(1)}, bf16[208,1024]{1,0:T(8,128)(2,1)S(1)}, u32[]{:S(2)}, u32[]{:S(2)}) %collective-permute-start.17) | collective-permute-done | bytes 426016 | tf_op jit(solution)/shard_map/ppermute | solution.py:47
  493.9 20.0 %collective-permute-done.18 = bf16[2,208,1024]{2,1,0:T(8,128)(2,1)S(1)} collective-permute-done((bf16[2,208,1024]{2,1,0:T(8,128)(2,1)S(1)}, bf16[2,208,1024]{2,1,0:T(8,128)(2,1)S(1)}, u32[]{:S(2)}, u32[]{:S(2)}) %collective-permute-start.18) | collective-permute-done | bytes 852000 | tf_op jit(solution)/shard_map/ppermute | solution.py:47
  520.5 18.8 %multiply_reduce_fusion = (f32[1664]{0:T(1024)S(1)}, f32[1664,4016]{0,1:T(8,128)S(1)}) fusion(bf16[1664,1024]{1,0:T(8,128)(2,1)} %bitcast.464, bf16[4016,1024]{1,0:T(8,128)(2,1)} %all-gather.6.cloned.1.call-done), kind=kOutput, calls=%fused_computation.15 | convolution fusion | flops 13699377152 | bytes 38369792 | tf_op jit(solution)/shard_map/dot_general | solution.py:396
  539.3 8.9 fusion.9
  559.8 13.9 %fusion.7 = bf16[1664,4016]{0,1:T(8,128)(2,1)S(1)} fusion(f32[1664,4016]{0,1:T(8,128)} %copy-done.2, f32[1664]{0:T(1024)S(1)} %div.70, f32[1664]{0:T(1024)S(1)} %subtract_exponential_fusion.1, s32[1664]{0:T(1024)S(1)} %eq.31, f32[1664]{0:T(1024)S(1)} %get-tuple-element.273, s32[4016]{0:T(1024)S(1)} %iota_add_fusion), kind=kLoop, calls=%fused_computation.11 | loop fusion | flops 66826240 | bytes 40138432 | tf_op jit(solution)/shard_map/convert_element_type | solution.py:720
  573.7 17.4 %multiply_convert_fusion.1 = bf16[1664,1024]{1,0:T(8,128)(2,1)S(1)} fusion(bf16[1664,4016]{0,1:T(8,128)(2,1)S(1)} %fusion.7, bf16[4016,1024]{1,0:T(8,128)(2,1)} %all-gather.6.cloned.1.call-done), kind=kOutput, calls=%fused_computation.17 | convolution fusion | flops 13689421824 | bytes 24997888 | tf_op jit(solution)/shard_map/dot_general | solution.py:392
  591.7 3.6 collective-permute-done.23
  597.3 17.5 %multiply_convert_fusion = bf16[4016,1024]{1,0:T(8,128)(2,1)} fusion(bf16[1664,4016]{0,1:T(8,128)(2,1)S(1)} %fusion.7, bf16[1664,1024]{1,0:T(8,128)(2,1)S(1)} %bitcast.465), kind=kOutput, calls=%fused_computation.16 | convolution fusion | flops 13694238720 | bytes 24997888 | tf_op jit(solution)/shard_map/dot_general | solution.py:400
  620.6 18.0 %collective-permute-done.25 = bf16[208,1024]{1,0:T(8,128)(2,1)S(1)} collective-permute-done((bf16[208,1024]{1,0:T(8,128)(2,1)S(1)}, bf16[208,1024]{1,0:T(8,128)(2,1)S(1)}, u32[]{:S(2)}, u32[]{:S(2)}) %collective-permute-start.25) | collective-permute-done | bytes 426016 | tf_op jit(solution)/shard_map/ppermute | solution.py:47
  639.2 8.5 fusion.26
  647.8 9.7 multiply_reduce_fusion.16
  660.9 21.1 %attend_back.3 = (bf16[256,1024]{1,0:T(8,128)(2,1)}, bf16[1024,512]{1,0:T(8,128)(2,1)}, bf16[1024,512]{1,0:T(8,128)(2,1)}) custom-call(s32[1]{0:T(128)} %constant.321.clone.1.row_ref, bf16[256,1024]{1,0:T(8,128)(2,1)} %pad.27.q_ref, bf16[1024,1024]{1,0:T(8,128)(2,1)} %bitcast.478, bf16[1024,1024]{1,0:T(8,128)(2,1)} %bitcast.479, bf16[256,1024]{1,0:T(8,128)(2,1)} %pad.28.d_ref), custom_call_target="tpu_custom_call" | custom-call | flops 2684354560 | bytes 5767168 | tf_op jit(solution)/shard_map/attend_back/pallas_call | solution.py:508
  688.2 21.2 %attend_back.5 = (bf16[256,1024]{1,0:T(8,128)(2,1)}, bf16[1024,512]{1,0:T(8,128)(2,1)}, bf16[1024,512]{1,0:T(8,128)(2,1)}) custom-call(s32[1]{0:T(128)} %bitcast.127.row_ref, bf16[256,1024]{1,0:T(8,128)(2,1)} %pad.29.q_ref, bf16[1024,1024]{1,0:T(8,128)(2,1)} %bitcast.482, bf16[1024,1024]{1,0:T(8,128)(2,1)} %bitcast.483, bf16[256,1024]{1,0:T(8,128)(2,1)} %pad.30.d_ref), custom_call_target="tpu_custom_call" | custom-call | flops 2684354560 | bytes 5767168 | tf_op jit(solution)/shard_map/attend_back/pallas_call | solution.py:508
  718.7 10.7 collective-permute-done.31
  733.7 6.3 collective-permute-done.27
  743.6 5.4 collective-permute-done.35
  750.7 9.3 fusion.19
  760.1 7.3 multiply_reduce_fusion.5
  770.8 21.1 %attend_back.4 = (bf16[256,1024]{1,0:T(8,128)(2,1)}, bf16[1024,512]{1,0:T(8,128)(2,1)}, bf16[1024,512]{1,0:T(8,128)(2,1)}) custom-call(s32[1]{0:T(128)} %constant.321.clone.1.row_ref, bf16[256,1024]{1,0:T(8,128)(2,1)} %fusion.61.q_ref, bf16[1024,1024]{1,0:T(8,128)(2,1)} %bitcast.474, bf16[1024,1024]{1,0:T(8,128)(2,1)} %bitcast.475, ...), custom_call_target="tpu_custom_call" | custom-call | flops 2684354560 | bytes 5767168 | tf_op jit(solution)/shard_map/attend_back/pallas_call | solution.py:508
  798.3 12.8 %collective-permute-done.29 = bf16[256,1024]{1,0:T(8,128)(2,1)S(1)} collective-permute-done((bf16[256,1024]{1,0:T(8,128)(2,1)S(1)}, bf16[256,1024]{1,0:T(8,128)(2,1)S(1)}, u32[]{:S(2)}, u32[]{:S(2)}) %collective-permute-start.29) | collective-permute-done | bytes 524320 | tf_op jit(solution)/shard_map/ppermute | solution.py:47
  814.8 6.1 collective-permute-done.32
  822.3 5.3 collective-permute-done.33
  851.6 73.7 %sum_gradients.3 = f32[96,2048]{1,0:T(8,128)} custom-call(bf16[256,2816]{1,0:T(8,128)(2,1)} %copy-done.27, bf16[208,2816]{1,0:T(8,128)(2,1)} %copy-done.29, bf16[256,1024]{1,0:T(8,128)(2,1)} %copy-done.58, bf16[208,1024]{1,0:T(8,128)(2,1)} %copy-done.59), custom_call_target="tpu_custom_call" | custom-call | tf_op jit(solution)/shard_map/sum_gradients/pallas_call | solution.py:297
  927.3 201.9 %sum_gradients.2 = f32[32,20736]{1,0:T(8,128)} custom-call(bf16[256,1024]{1,0:T(8,128)(2,1)} %copy-done.54, bf16[256,1024]{1,0:T(8,128)(2,1)} %attend.3.refs_1_, bf16[256,1024]{1,0:T(8,128)(2,1)} %copy-done.56, bf16[208,1024]{1,0:T(8,128)(2,1)} %attend.4.refs_3_, bf16[208,1024]{1,0:T(8,128)(2,1)} %copy-done.60, bf16[256,1024]{1,0:T(8,128)(2,1)} %copy-done.55, ...), custom_call_target="tpu_custom_call" | custom-call | tf_op jit(solution)/shard_map/sum_gradients/pallas_call | solution.py:297
  1140.3 24.9 %fusion.11 = f32[4016,256]{1,0:T(8,128)S(1)} fusion(bf16[8192,256]{1,0:T(8,128)(2,1)} %bitcast.554, s32[8192]{0:T(1024)S(1)} %bitcast.528, bf16[4016,256]{1,0:T(8,128)(2,1)S(1)} %copy-done.138), kind=kOutput, calls=%fused_computation.19 | convolution fusion | flops 16879280128 | bytes 10395648 | tf_op jit(solution)/shard_map/dot_general | solution.py:392
  1165.3 23.0 %multiply_reduce_fusion.1 = (f32[]{:T(128)}, f32[4016,256]{1,0:T(8,128)}) fusion(f32[4016,256]{1,0:T(8,128)S(1)} %fusion.11, bf16[8192,256]{1,0:T(8,128)(2,1)S(1)} %bitcast.555, s32[8192]{0:T(1024)S(1)} %bitcast.527), kind=kOutput, calls=%fused_computation.26 | convolution fusion | flops 16880308224 | bytes 12451844 | tf_op jit(solution)/shard_map/dot_general | solution.py:392
  1191.0 13.4 %sum_numbers.1 = f32[8,128]{1,0:T(8,128)} custom-call(f32[8,128]{1,0:T(8,128)} %broadcast_in_dim.221.value_ref), custom_call_target="tpu_custom_call" | custom-call | tf_op jit(solution)/shard_map/sum_numbers/pallas_call | solution.py:343
  1206.5 3.5 multiply_add_fusion.6
  1216.4 11.7 multiply_add_fusion
  (645 shorter events, 199.7 us)
Async XLA Ops:
  8.0 92.7 %all-gather.6.cloned.1.call-start = ((), (), s32[]{:S(2)}) async-start(), calls=%async_computation.3 | async-start | bytes 10280960 | tf_op jit(solution)/shard_map/all_gather | solution.py:598
  11.8 277.4 %reduce-scatter.4.cloned.1.call-start = ((), (), s32[]{:S(2)}) async-start(), calls=%async_computation.4 | async-start | bytes 4718592 | tf_op jit(solution)/shard_map/reduce_scatter | solution.py:621
  11.9 7.6 collective-permute-start
  19.5 4.0 collective-permute-start.1
  53.7 235.5 %reduce-scatter.6.cloned.1.call-start = ((), (), s32[]{:S(2)}) async-start(), calls=%async_computation.5 | async-start | bytes 4718592 | tf_op jit(solution)/shard_map/reduce_scatter | solution.py:621
  80.8 371.3 %all-gather.8.cloned.1.call-start = ((), (), s32[]{:S(2)}) async-start(), calls=%async_computation.6 | async-start | bytes 11894784 | tf_op jit(solution)/shard_map/all_gather | solution.py:649
  289.2 177.8 %all-gather.10.cloned.1.call-start = ((), (), s32[]{:S(2)}) async-start(), calls=%async_computation.7 | async-start | bytes 5947392 | tf_op jit(solution)/shard_map/all_gather | solution.py:649
  289.3 4.5 collective-permute-start.4
  293.9 3.7 collective-permute-start.5
  297.6 3.8 collective-permute-start.6
  298.7 7.8 collective-permute-start.2
  301.5 7.5 collective-permute-start.7
  307.5 7.0 collective-permute-start.3
  309.0 2.0 collective-permute-start.8
  318.3 26.2 %collective-permute-start.9 = (bf16[256,1024]{1,0:T(8,128)(2,1)S(1)}, bf16[256,1024]{1,0:T(8,128)(2,1)S(1)}, u32[]{:S(2)}, u32[]{:S(2)}) collective-permute-start(bf16[256,1024]{1,0:T(8,128)(2,1)S(1)} %get-tuple-element.260), channel_id=1, source_target_pairs={{0,2},{2,0},{1,3},{3,1},{4,6},{6,4},{5,7},{7,5},{8,10},{10,8},{9,1... | collective-permute-start | bytes 1572872 | tf_op jit(solution)/shard_map/ppermute | solution.py:47
  344.5 4.1 collective-permute-start.10
  344.6 405.4 %reduce-scatter.8.cloned.1.call-start = ((), (), s32[]{:S(2)}) async-start(), calls=%async_computation.8 | async-start | bytes 10280960 | tf_op jit(solution)/shard_map/reduce_scatter | solution.py:731
  366.7 13.9 %collective-permute-start.11 = (bf16[2,256,256]{2,1,0:T(8,128)(2,1)S(1)}, bf16[2,256,256]{2,1,0:T(8,128)(2,1)S(1)}, u32[]{:S(2)}, u32[]{:S(2)}) collective-permute-start(bf16[2,256,256]{2,1,0:T(8,128)(2,1)S(1)} %dynamic-slice_bitcast_fusion.10), channel_id=1, source_target_pairs={{0,16},{16,0},{1,17},{17,1},{2,18},{18,2},{3,19},{19,3},{4,20},{20... | collective-permute-start | bytes 786440 | tf_op jit(solution)/shard_map/ppermute | solution.py:47
  380.7 8.5 collective-permute-start.12
  384.1 17.3 %collective-permute-start.15 = (bf16[256,1024]{1,0:T(8,128)(2,1)}, bf16[256,1024]{1,0:T(8,128)(2,1)}, u32[]{:S(2)}, u32[]{:S(2)}) collective-permute-start(bf16[256,1024]{1,0:T(8,128)(2,1)} %get-tuple-element.268), channel_id=1, source_target_pairs={{0,2},{2,0},{1,3},{3,1},{4,6},{6,4},{5,7},{7,5},{8,10},{10,8},{9,1... | collective-permute-start | bytes 1572872 | tf_op jit(solution)/shard_map/ppermute | solution.py:47
  393.8 20.1 %collective-permute-start.13 = (bf16[256,1024]{1,0:T(8,128)(2,1)}, bf16[256,1024]{1,0:T(8,128)(2,1)}, u32[]{:S(2)}, u32[]{:S(2)}) collective-permute-start(bf16[256,1024]{1,0:T(8,128)(2,1)} %get-tuple-element.262), channel_id=1, source_target_pairs={{0,2},{2,0},{1,3},{3,1},{4,6},{6,4},{5,7},{7,5},{8,10},{10,8},{9,1... | collective-permute-start | bytes 1572872 | tf_op jit(solution)/shard_map/ppermute | solution.py:47
  402.5 16.9 %collective-permute-start.16 = (bf16[2,256,1024]{2,1,0:T(8,128)(2,1)S(1)}, bf16[2,256,1024]{2,1,0:T(8,128)(2,1)S(1)}, u32[]{:S(2)}, u32[]{:S(2)}) collective-permute-start(bf16[2,256,1024]{2,1,0:T(8,128)(2,1)S(1)} %bitcast_dynamic-update-slice_fusion.10), channel_id=1, source_target_pairs={{0,1},{1,0},{2,3},{3,2},{4,5},{5,4},{6,7},{7,6},{8,9},{9,8},{10,11... | collective-permute-start | bytes 3145736 | tf_op jit(solution)/shard_map/ppermute | solution.py:47
  415.0 4.4 collective-permute-start.14
  471.4 22.1 %collective-permute-start.17 = (bf16[208,1024]{1,0:T(8,128)(2,1)S(1)}, bf16[208,1024]{1,0:T(8,128)(2,1)S(1)}, u32[]{:S(2)}, u32[]{:S(2)}) collective-permute-start(bf16[208,1024]{1,0:T(8,128)(2,1)S(1)} %get-tuple-element.171), channel_id=1, source_target_pairs={{0,4},{4,0},{1,5},{5,1},{2,6},{6,2},{3,7},{7,3},{8,12},{12,8},{9,1... | collective-permute-start | bytes 1277960 | tf_op jit(solution)/shard_map/ppermute | solution.py:47
  493.5 20.4 %collective-permute-start.18 = (bf16[2,208,1024]{2,1,0:T(8,128)(2,1)S(1)}, bf16[2,208,1024]{2,1,0:T(8,128)(2,1)S(1)}, u32[]{:S(2)}, u32[]{:S(2)}) collective-permute-start(bf16[2,208,1024]{2,1,0:T(8,128)(2,1)S(1)} %bitcast_dynamic-update-slice_fusion.16), channel_id=1, source_target_pairs={{0,2},{2,0},{1,3},{3,1},{4,6},{6,4},{5,7},{7,5},{8,10},{10,8},{9,1... | collective-permute-start | bytes 2555912 | tf_op jit(solution)/shard_map/ppermute | solution.py:47
  514.0 4.5 collective-permute-start.19
  548.2 1.4 collective-permute-start.20
  550.3 3.9 collective-permute-start.21
  554.9 4.8 collective-permute-start.22
  591.6 3.7 collective-permute-start.23
  596.1 21.1 %collective-permute-start.24 = (bf16[2,208,1024]{2,1,0:T(8,128)(2,1)S(1)}, bf16[2,208,1024]{2,1,0:T(8,128)(2,1)S(1)}, u32[]{:S(2)}, u32[]{:S(2)}) collective-permute-start(bf16[2,208,1024]{2,1,0:T(8,128)(2,1)S(1)} %dynamic-slice_bitcast_fusion.3), channel_id=1, source_target_pairs={{0,2},{2,0},{1,3},{3,1},{4,6},{6,4},{5,7},{7,5},{8,10},{10,8},{9,1... | collective-permute-start | bytes 2555912 | tf_op jit(solution)/shard_map/ppermute | solution.py:47
  617.2 514.5 %all-gather.14.cloned.1.call-start = ((), (), s32[]{:S(2)}) async-start(), calls=%async_computation.10 | async-start | bytes 4718592 | tf_op jit(solution)/shard_map/all_gather | solution.py:793
  617.7 20.9 %collective-permute-start.25 = (bf16[208,1024]{1,0:T(8,128)(2,1)S(1)}, bf16[208,1024]{1,0:T(8,128)(2,1)S(1)}, u32[]{:S(2)}, u32[]{:S(2)}) collective-permute-start(bf16[208,1024]{1,0:T(8,128)(2,1)S(1)} %dynamic-slice_bitcast_fusion.7), channel_id=1, source_target_pairs={{0,4},{4,0},{1,5},{5,1},{2,6},{6,2},{3,7},{7,3},{8,12},{12,8},{9,1... | collective-permute-start | bytes 1277960 | tf_op jit(solution)/shard_map/ppermute | solution.py:47
  711.4 2.7 collective-permute-start.30
  712.0 3.8 collective-permute-start.26
  714.6 14.8 %collective-permute-start.31 = (bf16[256,1024]{1,0:T(8,128)(2,1)S(1)}, bf16[256,1024]{1,0:T(8,128)(2,1)S(1)}, u32[]{:S(2)}, u32[]{:S(2)}) collective-permute-start(bf16[256,1024]{1,0:T(8,128)(2,1)S(1)} %dynamic-slice_bitcast_fusion.4), channel_id=1, source_target_pairs={{0,2},{2,0},{1,3},{3,1},{4,6},{6,4},{5,7},{7,5},{8,10},{10,8},{9,1... | collective-permute-start | bytes 1572872 | tf_op jit(solution)/shard_map/ppermute | solution.py:47
  717.1 22.9 %collective-permute-start.27 = (bf16[256,1024]{1,0:T(8,128)(2,1)}, bf16[256,1024]{1,0:T(8,128)(2,1)}, u32[]{:S(2)}, u32[]{:S(2)}) collective-permute-start(bf16[256,1024]{1,0:T(8,128)(2,1)} %dynamic-slice_bitcast_fusion.6), channel_id=1, source_target_pairs={{0,2},{2,0},{1,3},{3,1},{4,6},{6,4},{5,7},{7,5},{8,10},{10,8},{9,1... | collective-permute-start | bytes 1572872 | tf_op jit(solution)/shard_map/ppermute | solution.py:47
  732.1 9.1 collective-permute-start.34
  741.3 7.6 collective-permute-start.35
  749.9 381.8 %all-gather.12.cloned.1.call-start = ((), (), s32[]{:S(2)}) async-start(), calls=%async_computation.9 | async-start | bytes 4718592 | tf_op jit(solution)/shard_map/all_gather | solution.py:793
  793.8 2.7 collective-permute-start.28
  797.1 14.0 %collective-permute-start.29 = (bf16[256,1024]{1,0:T(8,128)(2,1)S(1)}, bf16[256,1024]{1,0:T(8,128)(2,1)S(1)}, u32[]{:S(2)}, u32[]{:S(2)}) collective-permute-start(bf16[256,1024]{1,0:T(8,128)(2,1)S(1)} %dynamic-slice_bitcast_fusion.5), channel_id=1, source_target_pairs={{0,2},{2,0},{1,3},{3,1},{4,6},{6,4},{5,7},{7,5},{8,10},{10,8},{9,1... | collective-permute-start | bytes 1572872 | tf_op jit(solution)/shard_map/ppermute | solution.py:47
  813.3 7.6 collective-permute-start.32
  821.0 6.7 collective-permute-start.33
  834.7 3.9 collective-permute-start.37
  838.7 3.8 collective-permute-start.38
  842.5 4.5 collective-permute-start.39
  847.1 284.1 %collective-permute-start.40 = (f32[7,32]{1,0:T(8,128)S(1)}, f32[7,32]{1,0:T(8,128)S(1)}, u32[]{:S(2)}, u32[]{:S(2)}) collective-permute-start(f32[7,32]{1,0:T(8,128)S(1)} %bitcast.535), channel_id=1, source_target_pairs={{0,4},{4,0},{1,5},{5,1},{2,6},{6,2},{3,7},{7,3},{8,12},{12,8},{9,1... | collective-permute-start | bytes 2696 | tf_op jit(solution)/shard_map/ppermute | solution.py:47
  (143 other events, 1655.0 us)
Sparse Core Ops, SparseCore 0:
  11.9 88.7 all-gather.5
  289.4 104.8 all-gather.7
  397.7 69.2 all-gather.9
  617.3 85.4 reduce-scatter.7
Sparse Core Ops, SparseCore 1:
  53.8 50.1 reduce-scatter.3
  106.1 57.8 reduce-scatter.5
  750.0 46.7 all-gather.13
  828.7 46.4 all-gather.11

commit v6 on v5

--- a/solution.py
+++ b/solution.py
@@ -164,7 +164,7 @@
     )(*shards)
 
 
-def grad_kernel(layout, orders, bounds, chunks, counts, *refs):
+def grad_kernel(layout, orders, bounds, chunks, counts, chunk_width, *refs):
     lefts, rights = refs[: counts[0]], refs[counts[0] : sum(counts)]
     out_ref = refs[sum(counts)]
     scratch = refs[sum(counts) + 1 :]
@@ -176,7 +176,7 @@
     )
     given_ref, x_ref, y_ref, in_sem, send_sem, recv_sem = scratch[3 * lanes * depth :]
     bits = {axis: lax.axis_index(axis) for axis in layout}
-    groups = out_ref.shape[1] // CHUNK // lanes
+    groups = out_ref.shape[1] // chunk_width // lanes
     tokens = y_ref.shape[0]
 
     copies, passed = [], 0
@@ -227,7 +227,7 @@
     def first(lane, group):
         chunk = jnp.minimum(group * lanes + lane, chunks - 1)
         which = sum((chunk >= bound).astype(jnp.int32) for bound in bounds) if bounds else 0
-        columns = y_ref[:, pl.ds(pl.multiple_of(chunk * CHUNK, CHUNK), CHUNK)]
+        columns = y_ref[:, pl.ds(pl.multiple_of(chunk * chunk_width, chunk_width), chunk_width)]
         bit = bits[orders[lane][0]]
         given = jnp.dot(x_ref[which, 1 - bit], columns, preferred_element_type=F32)
         sends[lane][0][...] = given.astype(BF).reshape(sends[lane][0].shape)
@@ -242,7 +242,7 @@
         held, received = helds[lane][step - 1], recvs[lane][step - 1]
         if step == depth:
             chunk = group * lanes + lane
-            out_ref[:, pl.ds(pl.multiple_of(chunk * CHUNK, CHUNK), CHUNK)] = held[
+            out_ref[:, pl.ds(pl.multiple_of(chunk * chunk_width, chunk_width), chunk_width)] = held[
                 ...
             ] + received[slot].astype(F32)
             return
@@ -274,29 +274,29 @@
                         first(lane, group)
 
 
-def grad_sums(lefts, rights, layout, orders, spans, collective):
+def grad_sums(lefts, rights, layout, orders, spans, collective, chunk_width=CHUNK):
     depth, lanes = len(layout), len(orders)
     tokens, width = max(left.shape[0] for left in lefts), lefts[0].shape[1]
     rows = width // 2**depth
     padded = -(-rows // 16) * 16
     total = sum(right.shape[1] for right in rights)
-    chunks = total // CHUNK
+    chunks = total // chunk_width
     groups = -(-chunks // lanes)
     bounds, passed = [], 0
     for span in spans[:-1]:
-        passed += span // CHUNK
+        passed += span // chunk_width
         bounds.append(passed)
     send_shapes, recv_shapes, held_shapes = [], [], []
     for _ in range(lanes):
         for step in range(depth):
-            shape = (2,) * (depth - 1 - step) + (padded, CHUNK)
+            shape = (2,) * (depth - 1 - step) + (padded, chunk_width)
             send_shapes.append(pltpu.VMEM(shape, BF))
             recv_shapes.append(pltpu.VMEM((2,) + shape, BF))
             held_shapes.append(pltpu.VMEM(shape, F32))
     counts = (len(lefts), len(rights))
     out = pl.pallas_call(
-        partial(grad_kernel, layout, orders, tuple(bounds), chunks, counts),
-        out_shape=jax.ShapeDtypeStruct((padded, groups * lanes * CHUNK), F32),
+        partial(grad_kernel, layout, orders, tuple(bounds), chunks, counts, chunk_width),
+        out_shape=jax.ShapeDtypeStruct((padded, groups * lanes * chunk_width), F32),
         in_specs=[pl.BlockSpec(memory_space=pl.ANY)] * sum(counts),
         out_specs=pl.BlockSpec(memory_space=pltpu.VMEM),
         scratch_shapes=send_shapes
@@ -318,35 +318,58 @@
     return out[:rows, :total]
 
 
-def total_kernel(layout, value_ref, out_ref, send_ref, recv_ref, send_sem, recv_sem):
-    greet(layout)
+def greet_rounds(rounds):
+    barrier = pltpu.get_barrier_semaphore()
+    for partners in rounds:
+        for axes in partners:
+            other = {axis: 1 - lax.axis_index(axis) for axis in axes}
+            pl.semaphore_signal(barrier, inc=1, device_id=other, device_id_type=MESH)
+    pl.semaphore_wait(barrier, sum(len(partners) for partners in rounds))
+
+
+def total_kernel(rounds, value_ref, out_ref, send_ref, recv_ref, send_sem, recv_sem):
+    greet_rounds(rounds)
     held = value_ref[...]
-    for step, axis in enumerate(layout):
+    for step, partners in enumerate(rounds):
         send_ref[step] = held
-        copy = pltpu.make_async_remote_copy(
-            src_ref=send_ref.at[step],
-            dst_ref=recv_ref.at[step],
-            send_sem=send_sem.at[step],
-            recv_sem=recv_sem.at[step],
-            device_id={axis: 1 - lax.axis_index(axis)},
-            device_id_type=MESH,
-        )
-        copy.start()
-        copy.wait()
-        held = held + recv_ref[step]
+        copies = []
+        for k, axes in enumerate(partners):
+            copy = pltpu.make_async_remote_copy(
+                src_ref=send_ref.at[step],
+                dst_ref=recv_ref.at[step, k],
+                send_sem=send_sem.at[step, k],
+                recv_sem=recv_sem.at[step, k],
+                device_id={axis: 1 - lax.axis_index(axis) for axis in axes},
+                device_id_type=MESH,
+            )
+            copy.start()
+            copies.append(copy)
+        for copy in copies:
+            copy.wait()
+        held = held + recv_ref[step, 0]
+        if len(partners) > 1:
+            held = held + (recv_ref[step, 1] + recv_ref[step, 2])
     out_ref[...] = held
 
 
 def total_of(values, layout, collective):
-    depth = len(layout)
+    pairs = [layout[k : k + 2] for k in range(0, len(layout), 2)]
+    rounds = tuple(
+        ((pair[0],),) if len(pair) == 1 else ((pair[0],), (pair[1],), pair) for pair in pairs
+    )
+    depth = len(rounds)
     tile = jnp.broadcast_to(jnp.pad(values, (0, 8 - values.shape[0]))[:, None], (8, 128))
     sums = pl.pallas_call(
-        partial(total_kernel, layout),
+        partial(total_kernel, rounds),
         out_shape=jax.ShapeDtypeStruct(tile.shape, F32),
         in_specs=[pl.BlockSpec(memory_space=pltpu.VMEM)],
         out_specs=pl.BlockSpec(memory_space=pltpu.VMEM),
-        scratch_shapes=[pltpu.VMEM((depth, 8, 128), F32)] * 2
-        + [pltpu.SemaphoreType.DMA((depth,))] * 2,
+        scratch_shapes=[
+            pltpu.VMEM((depth, 8, 128), F32),
+            pltpu.VMEM((depth, 3, 8, 128), F32),
+            pltpu.SemaphoreType.DMA((depth, 3)),
+            pltpu.SemaphoreType.DMA((depth, 3)),
+        ],
         compiler_params=pltpu.CompilerParams(collective_id=collective, has_side_effects=True),
         name="sum_numbers",
     )(tile)
@@ -630,13 +653,15 @@
     found_d = look_up(1)
     mine_d = collect(found_d)
 
+    gain_all = gather_blocks(gains.astype(BF).T, every, gather_orders[0])
+    gain_all = gain_all.reshape(-1, gains.shape[0]).T.astype(F32)
     shards = [attn_in[0], attn_out[0], ff_in[0], ff_out[0]]
     shards += [attn_in[1], attn_out[1], attn_in[2], attn_out[2], ff_in[1], ff_out[1]]
     shards = [shard.astype(BF) for shard in shards]
     in_kernels = attn_in.shape[1] % 16 == 0
     if in_kernels:
-        *shards, found_e, found_d, table_rows = lax.optimization_barrier(
-            shards + [found_e, found_d, table_rows]
+        *shards, found_e, found_d, table_rows, gain_all = lax.optimization_barrier(
+            shards + [found_e, found_d, table_rows, gain_all]
         )
         behind = (8, 9,)
         full = [None] * len(shards)
@@ -654,9 +679,6 @@
     full = [got.reshape((-1,) + shard.shape[1:]) for got, shard in zip(full, shards)]
     a_in, a_out = (full[0], full[4], full[6]), (full[1], full[5], full[7])
     f_in, f_out = (full[2], full[8]), (full[3], full[9])
-    gain_all = gather_blocks(gains.astype(BF).T, every, gather_orders[0])
-    gain_all = gain_all.reshape(-1, gains.shape[0]).T.astype(F32)
-
     def spread_keys(own):
         return gather_blocks(own, row_axes, row_axes).reshape(length, -1)
 
@@ -786,7 +808,8 @@
         return trade(parts.reshape(two_dp + (rows, width))).reshape(-1, width)
 
     def look_back(which, spread):
-        places = (local_ids[which][None, :] == jnp.arange(vocab_part)[:, None]).astype(BF)
+        own_ids = local_ids[which].astype(jnp.int16)
+        places = (own_ids[None, :] == jnp.arange(vocab_part, dtype=jnp.int16)[:, None]).astype(BF)
         return mm(places, spread.reshape(-1, spread.shape[-1]))
 
     traded_y, traded_x = trade_rows(d_y), trade_rows(d_x)
@@ -824,7 +847,8 @@
     wide_spans = [right.shape[1] for right in wide_rights]
     if in_kernels:
         back_orders = tuple(order[::-1] for order in three)
-        own = grad_sums(lefts, rights, every, back_orders, spans, 1)
+        six_back = tuple(order[::-1] for order in six_orders)
+        own = grad_sums(lefts, rights, every, six_back, spans, 1, 128)
         wide = grad_sums(wide_lefts, wide_rights, every, back_orders[:2], wide_spans, 2)
         own, wide, spread_x, spread_y = lax.optimization_barrier((own, wide, spread_x, spread_y))
     else:

time: 1250 us -> 1230 us (0.984)
  Pallas kernels: 628 us -> 610 us
    all_gather x1, waiting for transfers between devices: 14.9 us -> 0.02 us  [on_device(): table_rows = lax.all_gather(table_bf, dp_axes, axis=1, tiled=True)]
    pallas_call x2, Pallas kernels: 276 us -> 262 us  [grad_sums(): pl.pallas_call(partial(grad_kernel, layout, orders, tuple(bounds), chunks...]
    ppermute x41, waiting for transfers between devices: 189 us -> 202 us  [swap(): return lax.ppermute(value, axis, [(0, 1), (1, 0)])]
  transfers between devices with their start and end apart: 49 -> 49, of which waited for: 31 -> 31; matrix products, arithmetic and copies ran while one was open for 13% -> 13% of each run, Pallas kernels for 50% -> 49%
where the time goes in v6:
time: 1230 us; the launch traced here: 1220 us
  Pallas kernels  610 us (50%)
  waiting for transfers between devices  211 us (17%)
  matrix products  174 us (14%)
  other arithmetic  80.6 us (7%)
  local copies, waits for them, and re-layouts  76.5 us (6%)
  starting transfers between devices  38.6 us (3%)
  between operations  25.5 us (2%)
    pallas_call x2, Pallas kernels, grad_sums(): pl.pallas_call(partial(grad_kernel, layout, orders, tuple(bounds), chunks...  262 us
    ppermute x41, waiting for transfers between devices, swap(): return lax.ppermute(value, axis, [(0, 1), (1, 0)])  202 us
    pallas_call x1, Pallas kernels, gather_all(): pl.pallas_call(partial(gather_kernel, layout, tuple(units), LANES, count)...  186 us
    dot_general x16, matrix products, mm(): return jnp.dot(left, right, preferred_element_type=F32)  92.2 us
    dot_general x14, matrix products, mm_nt(): lax.dot_general(left, right, (((1,), (1,)), ((), ())), preferred_element_...  64.2 us
    pallas_call x3, Pallas kernels, attend_backward(): pl.pallas_call(partial(attend_back_kernel, 0 if first_row is None else pe...  63.5 us
    pallas_call x2, Pallas kernels, rows_of(): pl.pallas_call(rows_kernel, grid=(count // step,), out_shape=jax.ShapeDty...  49.4 us
    ppermute x41, starting transfers between devices, swap(): return lax.ppermute(value, axis, [(0, 1), (1, 0)])  37.8 us
  transfers between devices with their start and end apart: 49, of which 31 were waited for; matrix products, arithmetic and copies ran while one was open for 13% of the time, Pallas kernels for 49%

profile of v6, /device:TPU:0, one launch (start us, length us, event | category | flops | bytes accessed | tf_op | source)
XLA Modules:
  0.0 1216.3 jit_solution(17858449623875467460)
XLA Ops:
  8.1 3.7 convert_element_type.338
  15.0 4.5 pad.26.table_ref
  29.0 24.7 %look_up.2 = bf16[8192,256]{1,0:T(8,128)(2,1)} custom-call(s32[8192]{0:T(1024)S(1)} %bitcast.438, f32[4024,256]{1,0:T(8,128)S(1)} %copy-done), custom_call_target="tpu_custom_call" | custom-call | bytes 167772160 | tf_op jit(solution)/shard_map/look_up/pallas_call | solution.py:396
  56.1 24.7 %look_up.3 = bf16[8192,256]{1,0:T(8,128)(2,1)} custom-call(s32[8192]{0:T(1024)S(1)} %bitcast.437, f32[4024,256]{1,0:T(8,128)S(1)} %copy-done.1), custom_call_target="tpu_custom_call" | custom-call | bytes 167772160 | tf_op jit(solution)/shard_map/look_up/pallas_call | solution.py:396
  90.5 3.5 collective-permute-done.4
  102.8 186.0 %gather_weights.1 = (bf16[2,2,2,2,2,32,2048]{6,5,4,3,2,1,0:T(8,128)(2,1)}, bf16[2,2,2,2,2,32,1024]{6,5,4,3,2,1,0:T(8,128)(2,1)}, bf16[2,2,2,2,2,32,5632]{6,5,4,3...) custom-call(bf16[32,2048]{1,0:T(8,128)(2,1)} %get-tuple-element.69.r, ...), custom_call_target="tpu_custom_call" | custom-call | tf_op jit(solution)/shard_map/gather_weights/pallas_call | solution.py:154
  291.3 7.6 collective-permute-done.7
  301.1 7.4 collective-permute-done.8
  313.7 24.9 %collective-permute-done.9 = bf16[256,1024]{1,0:T(8,128)(2,1)S(1)} collective-permute-done((bf16[256,1024]{1,0:T(8,128)(2,1)S(1)}, bf16[256,1024]{1,0:T(8,128)(2,1)S(1)}, u32[]{:S(2)}, u32[]{:S(2)}) %collective-permute-start.9) | collective-permute-done | bytes 524320 | tf_op jit(solution)/shard_map/ppermute | solution.py:47
  345.4 13.2 %attend.3.refs_1_ = bf16[256,1024]{1,0:T(8,128)(2,1)} custom-call(s32[1]{0:T(128)} %constant.321.clone.1.row_ref, bf16[256,1024]{1,0:T(8,128)(2,1)} %fusion.69.q_ref, bf16[1024,1024]{1,0:T(8,128)(2,1)} %bitcast.472, bf16[1024,1024]{1,0:T(8,128)(2,1)} %bitcast.473), custom_call_target="tpu_custom_call" | custom-call | flops 1073741824 | bytes 3145728 | tf_op jit(solution)/shard_map/attend/pallas_call | solution.py:512
  363.0 6.3 fusion.150
  378.0 5.3 collective-permute-done.12
  387.8 12.0 collective-permute-done.15
  400.9 9.9 collective-permute-done.13
  418.5 12.2 %attend.4.refs_3_ = bf16[208,1024]{1,0:T(8,128)(2,1)} custom-call(s32[1]{0:T(128)} %bitcast.72.row_ref, bf16[208,1024]{1,0:T(8,128)(2,1)} %fusion.81.q_ref, bf16[1024,1024]{1,0:T(8,128)(2,1)} %bitcast.480, bf16[1024,1024]{1,0:T(8,128)(2,1)} %bitcast.481), custom_call_target="tpu_custom_call" | custom-call | flops 872415232 | bytes 2949120 | tf_op jit(solution)/shard_map/attend/pallas_call | solution.py:512
  434.7 12.2 %attend.5.refs_6_ = bf16[208,1024]{1,0:T(8,128)(2,1)} custom-call(s32[1]{0:T(128)} %constant.321.clone.1.row_ref, bf16[208,1024]{1,0:T(8,128)(2,1)} %fusion.84.q_ref, bf16[1024,1024]{1,0:T(8,128)(2,1)} %bitcast.476, bf16[1024,1024]{1,0:T(8,128)(2,1)} %bitcast.477), custom_call_target="tpu_custom_call" | custom-call | flops 872415232 | bytes 2949120 | tf_op jit(solution)/shard_map/attend/pallas_call | solution.py:512
  450.2 5.8 fusion.151
  459.0 8.8 all-gather.10.cloned.1.call-done
  467.8 4.1 multiply_reduce_fusion.21
  474.6 19.7 %collective-permute-done.17 = bf16[208,1024]{1,0:T(8,128)(2,1)S(1)} collective-permute-done((bf16[208,1024]{1,0:T(8,128)(2,1)S(1)}, bf16[208,1024]{1,0:T(8,128)(2,1)S(1)}, u32[]{:S(2)}, u32[]{:S(2)}) %collective-permute-start.17) | collective-permute-done | bytes 426016 | tf_op jit(solution)/shard_map/ppermute | solution.py:47
  494.8 20.0 %collective-permute-done.18 = bf16[2,208,1024]{2,1,0:T(8,128)(2,1)S(1)} collective-permute-done((bf16[2,208,1024]{2,1,0:T(8,128)(2,1)S(1)}, bf16[2,208,1024]{2,1,0:T(8,128)(2,1)S(1)}, u32[]{:S(2)}, u32[]{:S(2)}) %collective-permute-start.18) | collective-permute-done | bytes 852000 | tf_op jit(solution)/shard_map/ppermute | solution.py:47
  521.3 18.8 %multiply_reduce_fusion = (f32[1664]{0:T(1024)S(1)}, f32[1664,4016]{0,1:T(8,128)S(1)}) fusion(bf16[1664,1024]{1,0:T(8,128)(2,1)} %bitcast.464, bf16[4016,1024]{1,0:T(8,128)(2,1)} %all-gather.6.cloned.1.call-done), kind=kOutput, calls=%fused_computation.17 | convolution fusion | flops 13699377152 | bytes 38369792 | tf_op jit(solution)/shard_map/dot_general | solution.py:419
  540.1 8.9 fusion.13
  559.5 13.9 %fusion.11 = bf16[1664,4016]{0,1:T(8,128)(2,1)S(1)} fusion(f32[1664,4016]{0,1:T(8,128)} %copy-done.2, f32[1664]{0:T(1024)S(1)} %div.70, f32[1664]{0:T(1024)S(1)} %subtract_exponential_fusion.1, s32[1664]{0:T(1024)S(1)} %eq.31, f32[1664]{0:T(1024)S(1)} %get-tuple-element.275, s32[4016]{0:T(1024)S(1)} %iota_add_fusion), kind=kLoop, calls=%fused_computation.13 | loop fusion | flops 66826240 | bytes 40138432 | tf_op jit(solution)/shard_map/convert_element_type | solution.py:742
  573.4 17.4 %multiply_convert_fusion.1 = bf16[1664,1024]{1,0:T(8,128)(2,1)S(1)} fusion(bf16[1664,4016]{0,1:T(8,128)(2,1)S(1)} %fusion.11, bf16[4016,1024]{1,0:T(8,128)(2,1)} %all-gather.6.cloned.1.call-done), kind=kOutput, calls=%fused_computation.19 | convolution fusion | flops 13689421824 | bytes 24997888 | tf_op jit(solution)/shard_map/dot_general | solution.py:415
  591.4 3.6 collective-permute-done.23
  597.0 17.5 %multiply_convert_fusion = bf16[4016,1024]{1,0:T(8,128)(2,1)} fusion(bf16[1664,4016]{0,1:T(8,128)(2,1)S(1)} %fusion.11, bf16[1664,1024]{1,0:T(8,128)(2,1)S(1)} %bitcast.465), kind=kOutput, calls=%fused_computation.18 | convolution fusion | flops 13694238720 | bytes 24997888 | tf_op jit(solution)/shard_map/dot_general | solution.py:423
  620.3 18.0 %collective-permute-done.25 = bf16[208,1024]{1,0:T(8,128)(2,1)S(1)} collective-permute-done((bf16[208,1024]{1,0:T(8,128)(2,1)S(1)}, bf16[208,1024]{1,0:T(8,128)(2,1)S(1)}, u32[]{:S(2)}, u32[]{:S(2)}) %collective-permute-start.25) | collective-permute-done | bytes 426016 | tf_op jit(solution)/shard_map/ppermute | solution.py:47
  638.9 8.5 fusion.34
  647.5 9.6 multiply_reduce_fusion.16
  660.5 21.1 %attend_back.3 = (bf16[256,1024]{1,0:T(8,128)(2,1)}, bf16[1024,512]{1,0:T(8,128)(2,1)}, bf16[1024,512]{1,0:T(8,128)(2,1)}) custom-call(s32[1]{0:T(128)} %constant.321.clone.1.row_ref, bf16[256,1024]{1,0:T(8,128)(2,1)} %pad.27.q_ref, bf16[1024,1024]{1,0:T(8,128)(2,1)} %bitcast.478, bf16[1024,1024]{1,0:T(8,128)(2,1)} %bitcast.479, bf16[256,1024]{1,0:T(8,128)(2,1)} %pad.28.d_ref), custom_call_target="tpu_custom_call" | custom-call | flops 2684354560 | bytes 5767168 | tf_op jit(solution)/shard_map/attend_back/pallas_call | solution.py:531
  688.0 21.2 %attend_back.5 = (bf16[256,1024]{1,0:T(8,128)(2,1)}, bf16[1024,512]{1,0:T(8,128)(2,1)}, bf16[1024,512]{1,0:T(8,128)(2,1)}) custom-call(s32[1]{0:T(128)} %bitcast.127.row_ref, bf16[256,1024]{1,0:T(8,128)(2,1)} %pad.29.q_ref, bf16[1024,1024]{1,0:T(8,128)(2,1)} %bitcast.482, bf16[1024,1024]{1,0:T(8,128)(2,1)} %bitcast.483, bf16[256,1024]{1,0:T(8,128)(2,1)} %pad.30.d_ref), custom_call_target="tpu_custom_call" | custom-call | flops 2684354560 | bytes 5767168 | tf_op jit(solution)/shard_map/attend_back/pallas_call | solution.py:531
  718.5 10.7 collective-permute-done.31
  733.6 6.2 collective-permute-done.27
  743.4 5.3 collective-permute-done.35
  750.5 9.3 fusion.27
  759.9 7.3 multiply_reduce_fusion.5
  770.6 21.2 %attend_back.4 = (bf16[256,1024]{1,0:T(8,128)(2,1)}, bf16[1024,512]{1,0:T(8,128)(2,1)}, bf16[1024,512]{1,0:T(8,128)(2,1)}) custom-call(s32[1]{0:T(128)} %constant.321.clone.1.row_ref, bf16[256,1024]{1,0:T(8,128)(2,1)} %fusion.69.q_ref, bf16[1024,1024]{1,0:T(8,128)(2,1)} %bitcast.474, bf16[1024,1024]{1,0:T(8,128)(2,1)} %bitcast.475, ...), custom_call_target="tpu_custom_call" | custom-call | flops 2684354560 | bytes 5767168 | tf_op jit(solution)/shard_map/attend_back/pallas_call | solution.py:531
  798.0 13.0 %collective-permute-done.29 = bf16[256,1024]{1,0:T(8,128)(2,1)S(1)} collective-permute-done((bf16[256,1024]{1,0:T(8,128)(2,1)S(1)}, bf16[256,1024]{1,0:T(8,128)(2,1)S(1)}, u32[]{:S(2)}, u32[]{:S(2)}) %collective-permute-start.29) | collective-permute-done | bytes 524320 | tf_op jit(solution)/shard_map/ppermute | solution.py:47
  814.8 5.9 collective-permute-done.32
  822.2 5.3 collective-permute-done.33
  851.2 74.0 %sum_gradients.3 = f32[96,2048]{1,0:T(8,128)} custom-call(bf16[256,2816]{1,0:T(8,128)(2,1)} %copy-done.27, bf16[208,2816]{1,0:T(8,128)(2,1)} %copy-done.29, bf16[256,1024]{1,0:T(8,128)(2,1)} %copy-done.58, bf16[208,1024]{1,0:T(8,128)(2,1)} %copy-done.59), custom_call_target="tpu_custom_call" | custom-call | tf_op jit(solution)/shard_map/sum_gradients/pallas_call | solution.py:297
  927.2 187.7 %sum_gradients.2 = f32[32,20736]{1,0:T(8,128)} custom-call(bf16[256,1024]{1,0:T(8,128)(2,1)} %copy-done.54, bf16[256,1024]{1,0:T(8,128)(2,1)} %attend.3.refs_1_, bf16[256,1024]{1,0:T(8,128)(2,1)} %copy-done.56, bf16[208,1024]{1,0:T(8,128)(2,1)} %attend.4.refs_3_, bf16[208,1024]{1,0:T(8,128)(2,1)} %copy-done.60, bf16[256,1024]{1,0:T(8,128)(2,1)} %copy-done.55, ...), custom_call_target="tpu_custom_call" | custom-call | tf_op jit(solution)/shard_map/sum_gradients/pallas_call | solution.py:297
  1120.5 19.0 %fusion = f32[4016,256]{1,0:T(8,128)} fusion(bf16[8192,256]{1,0:T(8,128)(2,1)S(1)} %bitcast.555, s16[8192]{0:T(1024)(128)(2,1)S(1)} %bitcast.532), kind=kOutput, calls=%fused_computation | convolution fusion | flops 16877223936 | bytes 8323072 | tf_op jit(solution)/shard_map/dot_general | solution.py:415
  1145.4 22.8 %multiply_reduce_fusion.1 = (f32[]{:T(128)}, f32[4016,256]{1,0:T(8,128)}) fusion(f32[4016,256]{1,0:T(8,128)} %fusion, bf16[8192,256]{1,0:T(8,128)(2,1)} %bitcast.554, s16[8192]{0:T(1024)(128)(2,1)S(1)} %bitcast.531, bf16[4016,256]{1,0:T(8,128)(2,1)S(1)} %copy-done.138), kind=kOutput, calls=%fused_computation.28 | convolution fusion | flops 16882364416 | bytes 14491652 | tf_op jit(solution)/shard_map/dot_general | solution.py:415
  1170.9 12.1 sum_numbers.1
  1185.0 3.5 multiply_add_fusion.6
  1195.0 11.7 multiply_add_fusion
  (646 shorter events, 200.9 us)
Async XLA Ops:
  8.0 94.8 %all-gather.6.cloned.1.call-start = ((), (), s32[]{:S(2)}) async-start(), calls=%async_computation.3 | async-start | bytes 10280960 | tf_op jit(solution)/shard_map/all_gather | solution.py:621
  11.8 277.1 %reduce-scatter.4.cloned.1.call-start = ((), (), s32[]{:S(2)}) async-start(), calls=%async_computation.4 | async-start | bytes 4718592 | tf_op jit(solution)/shard_map/reduce_scatter | solution.py:644
  11.9 7.6 collective-permute-start
  19.5 4.0 collective-permute-start.1
  53.7 235.2 %reduce-scatter.6.cloned.1.call-start = ((), (), s32[]{:S(2)}) async-start(), calls=%async_computation.5 | async-start | bytes 4718592 | tf_op jit(solution)/shard_map/reduce_scatter | solution.py:644
  80.8 368.6 %all-gather.8.cloned.1.call-start = ((), (), s32[]{:S(2)}) async-start(), calls=%async_computation.6 | async-start | bytes 11894784 | tf_op jit(solution)/shard_map/all_gather | solution.py:674
  81.5 4.7 collective-permute-start.2
  86.2 3.9 collective-permute-start.3
  90.2 3.8 collective-permute-start.4
  94.1 4.1 collective-permute-start.5
  98.1 2.7 collective-permute-start.6
  288.9 178.9 %all-gather.10.cloned.1.call-start = ((), (), s32[]{:S(2)}) async-start(), calls=%async_computation.7 | async-start | bytes 5947392 | tf_op jit(solution)/shard_map/all_gather | solution.py:674
  290.0 8.9 collective-permute-start.7
  299.9 8.6 collective-permute-start.8
  312.1 26.5 %collective-permute-start.9 = (bf16[256,1024]{1,0:T(8,128)(2,1)S(1)}, bf16[256,1024]{1,0:T(8,128)(2,1)S(1)}, u32[]{:S(2)}, u32[]{:S(2)}) collective-permute-start(bf16[256,1024]{1,0:T(8,128)(2,1)S(1)} %get-tuple-element.262), channel_id=1, source_target_pairs={{0,2},{2,0},{1,3},{3,1},{4,6},{6,4},{5,7},{7,5},{8,10},{10,8},{9,1... | collective-permute-start | bytes 1572872 | tf_op jit(solution)/shard_map/ppermute | solution.py:47
  338.6 4.1 collective-permute-start.10
  338.7 411.1 %reduce-scatter.8.cloned.1.call-start = ((), (), s32[]{:S(2)}) async-start(), calls=%async_computation.8 | async-start | bytes 10280960 | tf_op jit(solution)/shard_map/reduce_scatter | solution.py:753
  360.5 14.7 %collective-permute-start.11 = (bf16[2,256,256]{2,1,0:T(8,128)(2,1)S(1)}, bf16[2,256,256]{2,1,0:T(8,128)(2,1)S(1)}, u32[]{:S(2)}, u32[]{:S(2)}) collective-permute-start(bf16[2,256,256]{2,1,0:T(8,128)(2,1)S(1)} %dynamic-slice_bitcast_fusion.10), channel_id=1, source_target_pairs={{0,16},{16,0},{1,17},{17,1},{2,18},{18,2},{3,19},{19,3},{4,20},{20... | collective-permute-start | bytes 786440 | tf_op jit(solution)/shard_map/ppermute | solution.py:47
  375.2 8.0 collective-permute-start.12
  377.9 21.8 %collective-permute-start.15 = (bf16[256,1024]{1,0:T(8,128)(2,1)}, bf16[256,1024]{1,0:T(8,128)(2,1)}, u32[]{:S(2)}, u32[]{:S(2)}) collective-permute-start(bf16[256,1024]{1,0:T(8,128)(2,1)} %get-tuple-element.270), channel_id=1, source_target_pairs={{0,2},{2,0},{1,3},{3,1},{4,6},{6,4},{5,7},{7,5},{8,10},{10,8},{9,1... | collective-permute-start | bytes 1572872 | tf_op jit(solution)/shard_map/ppermute | solution.py:47
  387.8 23.0 %collective-permute-start.13 = (bf16[256,1024]{1,0:T(8,128)(2,1)}, bf16[256,1024]{1,0:T(8,128)(2,1)}, u32[]{:S(2)}, u32[]{:S(2)}) collective-permute-start(bf16[256,1024]{1,0:T(8,128)(2,1)} %get-tuple-element.264), channel_id=1, source_target_pairs={{0,2},{2,0},{1,3},{3,1},{4,6},{6,4},{5,7},{7,5},{8,10},{10,8},{9,1... | collective-permute-start | bytes 1572872 | tf_op jit(solution)/shard_map/ppermute | solution.py:47
  400.8 15.3 %collective-permute-start.16 = (bf16[2,256,1024]{2,1,0:T(8,128)(2,1)S(1)}, bf16[2,256,1024]{2,1,0:T(8,128)(2,1)S(1)}, u32[]{:S(2)}, u32[]{:S(2)}) collective-permute-start(bf16[2,256,1024]{2,1,0:T(8,128)(2,1)S(1)} %bitcast_dynamic-update-slice_fusion.10), channel_id=1, source_target_pairs={{0,1},{1,0},{2,3},{3,2},{4,5},{5,4},{6,7},{7,6},{8,9},{9,8},{10,11... | collective-permute-start | bytes 3145736 | tf_op jit(solution)/shard_map/ppermute | solution.py:47
  411.9 4.3 collective-permute-start.14
  472.3 22.1 %collective-permute-start.17 = (bf16[208,1024]{1,0:T(8,128)(2,1)S(1)}, bf16[208,1024]{1,0:T(8,128)(2,1)S(1)}, u32[]{:S(2)}, u32[]{:S(2)}) collective-permute-start(bf16[208,1024]{1,0:T(8,128)(2,1)S(1)} %get-tuple-element.173), channel_id=1, source_target_pairs={{0,4},{4,0},{1,5},{5,1},{2,6},{6,2},{3,7},{7,3},{8,12},{12,8},{9,1... | collective-permute-start | bytes 1277960 | tf_op jit(solution)/shard_map/ppermute | solution.py:47
  494.4 20.4 %collective-permute-start.18 = (bf16[2,208,1024]{2,1,0:T(8,128)(2,1)S(1)}, bf16[2,208,1024]{2,1,0:T(8,128)(2,1)S(1)}, u32[]{:S(2)}, u32[]{:S(2)}) collective-permute-start(bf16[2,208,1024]{2,1,0:T(8,128)(2,1)S(1)} %bitcast_dynamic-update-slice_fusion.16), channel_id=1, source_target_pairs={{0,2},{2,0},{1,3},{3,1},{4,6},{6,4},{5,7},{7,5},{8,10},{10,8},{9,1... | collective-permute-start | bytes 2555912 | tf_op jit(solution)/shard_map/ppermute | solution.py:47
  514.8 4.5 collective-permute-start.19
  549.1 1.4 collective-permute-start.20
  550.6 3.9 collective-permute-start.21
  554.6 4.8 collective-permute-start.22
  591.4 3.7 collective-permute-start.23
  595.9 21.1 %collective-permute-start.24 = (bf16[2,208,1024]{2,1,0:T(8,128)(2,1)S(1)}, bf16[2,208,1024]{2,1,0:T(8,128)(2,1)S(1)}, u32[]{:S(2)}, u32[]{:S(2)}) collective-permute-start(bf16[2,208,1024]{2,1,0:T(8,128)(2,1)S(1)} %dynamic-slice_bitcast_fusion.3), channel_id=1, source_target_pairs={{0,2},{2,0},{1,3},{3,1},{4,6},{6,4},{5,7},{7,5},{8,10},{10,8},{9,1... | collective-permute-start | bytes 2555912 | tf_op jit(solution)/shard_map/ppermute | solution.py:47
  617.0 500.5 %all-gather.14.cloned.1.call-start = ((), (), s32[]{:S(2)}) async-start(), calls=%async_computation.10 | async-start | bytes 4718592 | tf_op jit(solution)/shard_map/all_gather | solution.py:816
  617.4 20.9 %collective-permute-start.25 = (bf16[208,1024]{1,0:T(8,128)(2,1)S(1)}, bf16[208,1024]{1,0:T(8,128)(2,1)S(1)}, u32[]{:S(2)}, u32[]{:S(2)}) collective-permute-start(bf16[208,1024]{1,0:T(8,128)(2,1)S(1)} %dynamic-slice_bitcast_fusion.7), channel_id=1, source_target_pairs={{0,4},{4,0},{1,5},{5,1},{2,6},{6,2},{3,7},{7,3},{8,12},{12,8},{9,1... | collective-permute-start | bytes 1277960 | tf_op jit(solution)/shard_map/ppermute | solution.py:47
  711.2 2.7 collective-permute-start.30
  711.8 3.7 collective-permute-start.26
  714.4 14.8 %collective-permute-start.31 = (bf16[256,1024]{1,0:T(8,128)(2,1)S(1)}, bf16[256,1024]{1,0:T(8,128)(2,1)S(1)}, u32[]{:S(2)}, u32[]{:S(2)}) collective-permute-start(bf16[256,1024]{1,0:T(8,128)(2,1)S(1)} %dynamic-slice_bitcast_fusion.4), channel_id=1, source_target_pairs={{0,2},{2,0},{1,3},{3,1},{4,6},{6,4},{5,7},{7,5},{8,10},{10,8},{9,1... | collective-permute-start | bytes 1572872 | tf_op jit(solution)/shard_map/ppermute | solution.py:47
  716.7 23.0 %collective-permute-start.27 = (bf16[256,1024]{1,0:T(8,128)(2,1)}, bf16[256,1024]{1,0:T(8,128)(2,1)}, u32[]{:S(2)}, u32[]{:S(2)}) collective-permute-start(bf16[256,1024]{1,0:T(8,128)(2,1)} %dynamic-slice_bitcast_fusion.6), channel_id=1, source_target_pairs={{0,2},{2,0},{1,3},{3,1},{4,6},{6,4},{5,7},{7,5},{8,10},{10,8},{9,1... | collective-permute-start | bytes 1572872 | tf_op jit(solution)/shard_map/ppermute | solution.py:47
  731.9 9.1 collective-permute-start.34
  741.1 7.6 collective-permute-start.35
  749.7 367.8 %all-gather.12.cloned.1.call-start = ((), (), s32[]{:S(2)}) async-start(), calls=%async_computation.9 | async-start | bytes 4718592 | tf_op jit(solution)/shard_map/all_gather | solution.py:816
  793.7 2.8 collective-permute-start.28
  797.0 14.0 %collective-permute-start.29 = (bf16[256,1024]{1,0:T(8,128)(2,1)S(1)}, bf16[256,1024]{1,0:T(8,128)(2,1)S(1)}, u32[]{:S(2)}, u32[]{:S(2)}) collective-permute-start(bf16[256,1024]{1,0:T(8,128)(2,1)S(1)} %dynamic-slice_bitcast_fusion.5), channel_id=1, source_target_pairs={{0,2},{2,0},{1,3},{3,1},{4,6},{6,4},{5,7},{7,5},{8,10},{10,8},{9,1... | collective-permute-start | bytes 1572872 | tf_op jit(solution)/shard_map/ppermute | solution.py:47
  813.2 7.6 collective-permute-start.32
  820.9 6.7 collective-permute-start.33
  834.6 3.9 collective-permute-start.37
  838.6 3.8 collective-permute-start.38
  842.5 4.5 collective-permute-start.39
  847.0 269.8 %collective-permute-start.40 = (f32[7,32]{1,0:T(8,128)S(1)}, f32[7,32]{1,0:T(8,128)S(1)}, u32[]{:S(2)}, u32[]{:S(2)}) collective-permute-start(f32[7,32]{1,0:T(8,128)S(1)} %bitcast.535), channel_id=1, source_target_pairs={{0,4},{4,0},{1,5},{5,1},{2,6},{6,2},{3,7},{7,3},{8,12},{12,8},{9,1... | collective-permute-start | bytes 2696 | tf_op jit(solution)/shard_map/ppermute | solution.py:47
  (143 other events, 1588.2 us)
Sparse Core Ops, SparseCore 0:
  11.9 89.1 all-gather.5
  289.1 105.5 all-gather.7
  398.2 69.6 all-gather.9
  617.1 85.2 reduce-scatter.7
Sparse Core Ops, SparseCore 1:
  53.8 50.2 reduce-scatter.3
  106.2 55.3 reduce-scatter.5
  749.8 46.6 all-gather.13
  828.6 46.0 all-gather.11

commit v7 on v6

--- a/solution.py
+++ b/solution.py
@@ -669,10 +669,13 @@
         for k, got in zip(ahead, gather_all([shards[k] for k in ahead], every, six_orders)):
             full[k] = got
         full[0], mine_e, mine_d = lax.optimization_barrier((full[0], mine_e, mine_d))
-        full[0], *sent = lax.optimization_barrier([full[0]] + [shards[k] for k in behind])
+        stream_e, *sent = lax.optimization_barrier(
+            [embed(mine_e)] + [shards[k] for k in behind]
+        )
         for k, shard in zip(behind, sent):
             full[k] = lax.all_gather(shard, every, axis=0, tiled=True)
     else:
+        stream_e = embed(mine_e)
         full = [
             gather_blocks(shard, every, gather_orders[k % 3]) for k, shard in enumerate(shards)
         ]
@@ -699,7 +702,6 @@
         hidden_act = (jax.nn.gelu(both[:, :FF], approximate=True) * both[:, FF:]).astype(BF)
         return (stream + mm(hidden_act, f_out[which]), (stream, normed, both, hidden_act))
 
-    stream_e = embed(mine_e)
     stream_e, enc_attn = attention_forward(stream_e, None, 0, gain_all[0], None)
     stream_e, mine_d = lax.optimization_barrier((stream_e, mine_d))
     stream_d = embed(mine_d)

time: 1230 us -> 1250 us (1.016)
  waiting for transfers between devices: 211 us -> 233 us
    all_gather x2, waiting for transfers between devices: 8.82 us -> 26.4 us  [on_device(): full[k] = lax.all_gather(shard, every, axis=0, tiled=True)]
    unnamed x295 -> x293, local copies, waits for them, and re-layouts: 29.3 us -> 27.6 us
  transfers between devices with their start and end apart: 49 -> 49, of which waited for: 31 -> 30; matrix products, arithmetic and copies ran while one was open for 13% -> 13% of each run, Pallas kernels for 49% -> 48%
where the time goes in v7:
time: 1250 us; the launch traced here: 1240 us
  Pallas kernels  612 us (49%)
  waiting for transfers between devices  233 us (19%)
  matrix products  175 us (14%)
  other arithmetic  80.9 us (6%)
  local copies, waits for them, and re-layouts  75 us (6%)
  starting transfers between devices  43 us (3%)
  between operations  25.5 us (2%)
    pallas_call x2, Pallas kernels, grad_sums(): pl.pallas_call(partial(grad_kernel, layout, orders, tuple(bounds), chunks...  263 us
    ppermute x41, waiting for transfers between devices, swap(): return lax.ppermute(value, axis, [(0, 1), (1, 0)])  206 us
    pallas_call x1, Pallas kernels, gather_all(): pl.pallas_call(partial(gather_kernel, layout, tuple(units), LANES, count)...  186 us
    dot_general x16, matrix products, mm(): return jnp.dot(left, right, preferred_element_type=F32)  93.8 us
    dot_general x14, matrix products, mm_nt(): lax.dot_general(left, right, (((1,), (1,)), ((), ())), preferred_element_...  64.2 us
    pallas_call x3, Pallas kernels, attend_backward(): pl.pallas_call(partial(attend_back_kernel, 0 if first_row is None else pe...  63.5 us
    pallas_call x2, Pallas kernels, rows_of(): pl.pallas_call(rows_kernel, grid=(count // step,), out_shape=jax.ShapeDty...  49.4 us
    ppermute x41, starting transfers between devices, swap(): return lax.ppermute(value, axis, [(0, 1), (1, 0)])  42.2 us
  transfers between devices with their start and end apart: 49, of which 30 were waited for; matrix products, arithmetic and copies ran while one was open for 13% of the time, Pallas kernels for 48%

profile of v7, /device:TPU:0, one launch (start us, length us, event | category | flops | bytes accessed | tf_op | source)
XLA Modules:
  0.0 1244.2 jit_solution(15595343613435729919)
XLA Ops:
  8.1 3.7 convert_element_type.333
  15.0 4.5 pad.26.table_ref
  29.0 24.7 %look_up.2 = bf16[8192,256]{1,0:T(8,128)(2,1)} custom-call(s32[8192]{0:T(1024)S(1)} %bitcast.440, f32[4024,256]{1,0:T(8,128)S(1)} %copy-done), custom_call_target="tpu_custom_call" | custom-call | bytes 167772160 | tf_op jit(solution)/shard_map/look_up/pallas_call | solution.py:396
  56.1 24.7 %look_up.3 = bf16[8192,256]{1,0:T(8,128)(2,1)} custom-call(s32[8192]{0:T(1024)S(1)} %bitcast.439, f32[4024,256]{1,0:T(8,128)S(1)} %copy-done.1), custom_call_target="tpu_custom_call" | custom-call | bytes 167772160 | tf_op jit(solution)/shard_map/look_up/pallas_call | solution.py:396
  90.5 3.5 collective-permute-done.4
  102.9 186.0 %gather_weights.1 = (bf16[2,2,2,2,2,32,2048]{6,5,4,3,2,1,0:T(8,128)(2,1)}, bf16[2,2,2,2,2,32,1024]{6,5,4,3,2,1,0:T(8,128)(2,1)}, bf16[2,2,2,2,2,32,5632]{6,5,4,3...) custom-call(bf16[32,2048]{1,0:T(8,128)(2,1)} %get-tuple-element.69.r, ...), custom_call_target="tpu_custom_call" | custom-call | tf_op jit(solution)/shard_map/gather_weights/pallas_call | solution.py:154
  291.3 7.5 collective-permute-done.7
  300.8 7.1 collective-permute-done.8
  312.9 17.5 %collective-permute-done.9 = bf16[256,1024]{1,0:T(8,128)(2,1)S(1)} collective-permute-done((bf16[256,1024]{1,0:T(8,128)(2,1)S(1)}, bf16[256,1024]{1,0:T(8,128)(2,1)S(1)}, u32[]{:S(2)}, u32[]{:S(2)}) %collective-permute-start.9) | collective-permute-done | bytes 524320 | tf_op jit(solution)/shard_map/ppermute | solution.py:47
  337.2 13.2 %attend.3.refs_1_ = bf16[256,1024]{1,0:T(8,128)(2,1)} custom-call(s32[1]{0:T(128)} %constant.321.clone.1.row_ref, bf16[256,1024]{1,0:T(8,128)(2,1)} %fusion.69.q_ref, bf16[1024,1024]{1,0:T(8,128)(2,1)} %bitcast.474, bf16[1024,1024]{1,0:T(8,128)(2,1)} %bitcast.475), custom_call_target="tpu_custom_call" | custom-call | flops 1073741824 | bytes 3145728 | tf_op jit(solution)/shard_map/attend/pallas_call | solution.py:512
  354.4 6.3 fusion.150
  371.9 8.6 collective-permute-done.12
  387.6 18.4 %collective-permute-done.15 = bf16[256,1024]{1,0:T(8,128)(2,1)} collective-permute-done((bf16[256,1024]{1,0:T(8,128)(2,1)}, bf16[256,1024]{1,0:T(8,128)(2,1)}, u32[]{:S(2)}, u32[]{:S(2)}) %collective-permute-start.15) | collective-permute-done | bytes 524320 | tf_op jit(solution)/shard_map/ppermute | solution.py:47
  407.4 12.1 collective-permute-done.13
  427.2 12.2 attend.4.refs_3_
  443.4 12.2 attend.5.refs_6_
  458.9 5.8 fusion.151
  467.8 26.4 %all-gather.10.cloned.1.call-done = bf16[2816,1024]{1,0:T(8,128)(2,1)} async-done(((bf16[88,1024]{1,0:T(8,128)(2,1)}), bf16[2816,1024]{1,0:T(8,128)(2,1)}) %all-gather.10.cloned.1.call-update) | async-done | bytes 5767184 | tf_op jit(solution)/shard_map/all_gather | solution.py:676
  494.2 4.1 multiply_reduce_fusion.21
  500.9 19.7 %collective-permute-done.17 = bf16[208,1024]{1,0:T(8,128)(2,1)S(1)} collective-permute-done((bf16[208,1024]{1,0:T(8,128)(2,1)S(1)}, bf16[208,1024]{1,0:T(8,128)(2,1)S(1)}, u32[]{:S(2)}, u32[]{:S(2)}) %collective-permute-start.17) | collective-permute-done | bytes 426016 | tf_op jit(solution)/shard_map/ppermute | solution.py:47
  521.1 20.0 %collective-permute-done.18 = bf16[2,208,1024]{2,1,0:T(8,128)(2,1)S(1)} collective-permute-done((bf16[2,208,1024]{2,1,0:T(8,128)(2,1)S(1)}, bf16[2,208,1024]{2,1,0:T(8,128)(2,1)S(1)}, u32[]{:S(2)}, u32[]{:S(2)}) %collective-permute-start.18) | collective-permute-done | bytes 852000 | tf_op jit(solution)/shard_map/ppermute | solution.py:47
  547.6 18.8 %multiply_reduce_fusion = (f32[1664]{0:T(1024)S(1)}, f32[1664,4016]{0,1:T(8,128)S(1)}) fusion(bf16[1664,1024]{1,0:T(8,128)(2,1)} %bitcast.466, bf16[4016,1024]{1,0:T(8,128)(2,1)} %all-gather.6.cloned.1.call-done), kind=kOutput, calls=%fused_computation.17 | convolution fusion | flops 13699377152 | bytes 38369792 | tf_op jit(solution)/shard_map/dot_general | solution.py:419
  566.4 8.9 fusion.13
  585.8 13.9 %fusion.11 = bf16[1664,4016]{0,1:T(8,128)(2,1)S(1)} fusion(f32[1664,4016]{0,1:T(8,128)} %copy-done.2, f32[1664]{0:T(1024)S(1)} %div.70, f32[1664]{0:T(1024)S(1)} %subtract_exponential_fusion.1, s32[1664]{0:T(1024)S(1)} %eq.31, f32[1664]{0:T(1024)S(1)} %get-tuple-element.275, s32[4016]{0:T(1024)S(1)} %iota_add_fusion), kind=kLoop, calls=%fused_computation.13 | loop fusion | flops 66826240 | bytes 40138432 | tf_op jit(solution)/shard_map/convert_element_type | solution.py:744
  599.7 17.4 %multiply_convert_fusion.1 = bf16[1664,1024]{1,0:T(8,128)(2,1)S(1)} fusion(bf16[1664,4016]{0,1:T(8,128)(2,1)S(1)} %fusion.11, bf16[4016,1024]{1,0:T(8,128)(2,1)} %all-gather.6.cloned.1.call-done), kind=kOutput, calls=%fused_computation.19 | convolution fusion | flops 13689421824 | bytes 24997888 | tf_op jit(solution)/shard_map/dot_general | solution.py:415
  617.8 3.6 collective-permute-done.23
  623.3 17.5 %multiply_convert_fusion = bf16[4016,1024]{1,0:T(8,128)(2,1)} fusion(bf16[1664,4016]{0,1:T(8,128)(2,1)S(1)} %fusion.11, bf16[1664,1024]{1,0:T(8,128)(2,1)S(1)} %bitcast.467), kind=kOutput, calls=%fused_computation.18 | convolution fusion | flops 13694238720 | bytes 24997888 | tf_op jit(solution)/shard_map/dot_general | solution.py:423
  646.6 18.0 %collective-permute-done.25 = bf16[208,1024]{1,0:T(8,128)(2,1)S(1)} collective-permute-done((bf16[208,1024]{1,0:T(8,128)(2,1)S(1)}, bf16[208,1024]{1,0:T(8,128)(2,1)S(1)}, u32[]{:S(2)}, u32[]{:S(2)}) %collective-permute-start.25) | collective-permute-done | bytes 426016 | tf_op jit(solution)/shard_map/ppermute | solution.py:47
  665.3 8.5 fusion.34
  673.8 9.6 multiply_reduce_fusion.16
  686.9 21.1 %attend_back.3 = (bf16[256,1024]{1,0:T(8,128)(2,1)}, bf16[1024,512]{1,0:T(8,128)(2,1)}, bf16[1024,512]{1,0:T(8,128)(2,1)}) custom-call(s32[1]{0:T(128)} %constant.321.clone.1.row_ref, bf16[256,1024]{1,0:T(8,128)(2,1)} %pad.27.q_ref, bf16[1024,1024]{1,0:T(8,128)(2,1)} %bitcast.480, bf16[1024,1024]{1,0:T(8,128)(2,1)} %bitcast.481, bf16[256,1024]{1,0:T(8,128)(2,1)} %pad.28.d_ref), custom_call_target="tpu_custom_call" | custom-call | flops 2684354560 | bytes 5767168 | tf_op jit(solution)/shard_map/attend_back/pallas_call | solution.py:531
  714.3 21.2 %attend_back.5 = (bf16[256,1024]{1,0:T(8,128)(2,1)}, bf16[1024,512]{1,0:T(8,128)(2,1)}, bf16[1024,512]{1,0:T(8,128)(2,1)}) custom-call(s32[1]{0:T(128)} %bitcast.127.row_ref, bf16[256,1024]{1,0:T(8,128)(2,1)} %pad.29.q_ref, bf16[1024,1024]{1,0:T(8,128)(2,1)} %bitcast.484, bf16[1024,1024]{1,0:T(8,128)(2,1)} %bitcast.485, bf16[256,1024]{1,0:T(8,128)(2,1)} %pad.30.d_ref), custom_call_target="tpu_custom_call" | custom-call | flops 2684354560 | bytes 5767168 | tf_op jit(solution)/shard_map/attend_back/pallas_call | solution.py:531
  744.9 10.7 collective-permute-done.31
  759.8 6.3 collective-permute-done.27
  769.6 5.4 collective-permute-done.35
  776.8 9.3 fusion.27
  786.2 7.3 multiply_reduce_fusion.5
  796.9 21.2 %attend_back.4 = (bf16[256,1024]{1,0:T(8,128)(2,1)}, bf16[1024,512]{1,0:T(8,128)(2,1)}, bf16[1024,512]{1,0:T(8,128)(2,1)}) custom-call(s32[1]{0:T(128)} %constant.321.clone.1.row_ref, bf16[256,1024]{1,0:T(8,128)(2,1)} %fusion.69.q_ref, bf16[1024,1024]{1,0:T(8,128)(2,1)} %bitcast.476, bf16[1024,1024]{1,0:T(8,128)(2,1)} %bitcast.477, ...), custom_call_target="tpu_custom_call" | custom-call | flops 2684354560 | bytes 5767168 | tf_op jit(solution)/shard_map/attend_back/pallas_call | solution.py:531
  824.3 13.0 %collective-permute-done.29 = bf16[256,1024]{1,0:T(8,128)(2,1)S(1)} collective-permute-done((bf16[256,1024]{1,0:T(8,128)(2,1)S(1)}, bf16[256,1024]{1,0:T(8,128)(2,1)S(1)}, u32[]{:S(2)}, u32[]{:S(2)}) %collective-permute-start.29) | collective-permute-done | bytes 524320 | tf_op jit(solution)/shard_map/ppermute | solution.py:47
  841.0 6.0 collective-permute-done.32
  848.4 5.4 collective-permute-done.33
  877.5 73.8 %sum_gradients.3 = f32[96,2048]{1,0:T(8,128)} custom-call(bf16[256,2816]{1,0:T(8,128)(2,1)} %copy-done.27, bf16[208,2816]{1,0:T(8,128)(2,1)} %copy-done.29, bf16[256,1024]{1,0:T(8,128)(2,1)} %copy-done.58, bf16[208,1024]{1,0:T(8,128)(2,1)} %copy-done.59), custom_call_target="tpu_custom_call" | custom-call | tf_op jit(solution)/shard_map/sum_gradients/pallas_call | solution.py:297
  953.4 189.3 %sum_gradients.2 = f32[32,20736]{1,0:T(8,128)} custom-call(bf16[256,1024]{1,0:T(8,128)(2,1)} %copy-done.54, bf16[256,1024]{1,0:T(8,128)(2,1)} %attend.3.refs_1_, bf16[256,1024]{1,0:T(8,128)(2,1)} %copy-done.56, bf16[208,1024]{1,0:T(8,128)(2,1)} %attend.4.refs_3_, bf16[208,1024]{1,0:T(8,128)(2,1)} %copy-done.60, bf16[256,1024]{1,0:T(8,128)(2,1)} %copy-done.55, ...), custom_call_target="tpu_custom_call" | custom-call | tf_op jit(solution)/shard_map/sum_gradients/pallas_call | solution.py:297
  1148.3 19.0 %fusion = f32[4016,256]{1,0:T(8,128)} fusion(bf16[8192,256]{1,0:T(8,128)(2,1)S(1)} %bitcast.557, s16[8192]{0:T(1024)(128)(2,1)S(1)} %bitcast.534), kind=kOutput, calls=%fused_computation | convolution fusion | flops 16877223936 | bytes 8323072 | tf_op jit(solution)/shard_map/dot_general | solution.py:415
  1173.2 22.8 %multiply_reduce_fusion.1 = (f32[]{:T(128)}, f32[4016,256]{1,0:T(8,128)}) fusion(f32[4016,256]{1,0:T(8,128)} %fusion, bf16[8192,256]{1,0:T(8,128)(2,1)} %bitcast.556, s16[8192]{0:T(1024)(128)(2,1)S(1)} %bitcast.533, bf16[4016,256]{1,0:T(8,128)(2,1)S(1)} %copy-done.137), kind=kOutput, calls=%fused_computation.28 | convolution fusion | flops 16882364416 | bytes 14491652 | tf_op jit(solution)/shard_map/dot_general | solution.py:415
  1198.8 12.2 sum_numbers.1
  1213.0 3.5 multiply_add_fusion.6
  1222.9 11.7 multiply_add_fusion
  (645 shorter events, 205.2 us)
Async XLA Ops:
  8.0 94.8 %all-gather.6.cloned.1.call-start = ((), (), s32[]{:S(2)}) async-start(), calls=%async_computation.3 | async-start | bytes 10280960 | tf_op jit(solution)/shard_map/all_gather | solution.py:621
  11.8 277.1 %reduce-scatter.4.cloned.1.call-start = ((), (), s32[]{:S(2)}) async-start(), calls=%async_computation.4 | async-start | bytes 4718592 | tf_op jit(solution)/shard_map/reduce_scatter | solution.py:644
  11.9 7.6 collective-permute-start
  19.5 4.0 collective-permute-start.1
  53.7 235.2 %reduce-scatter.6.cloned.1.call-start = ((), (), s32[]{:S(2)}) async-start(), calls=%async_computation.5 | async-start | bytes 4718592 | tf_op jit(solution)/shard_map/reduce_scatter | solution.py:644
  80.8 377.3 %all-gather.8.cloned.1.call-start = ((), (), s32[]{:S(2)}) async-start(), calls=%async_computation.6 | async-start | bytes 11894784 | tf_op jit(solution)/shard_map/all_gather | solution.py:676
  81.5 4.7 collective-permute-start.2
  86.2 3.9 collective-permute-start.3
  90.3 3.8 collective-permute-start.4
  94.1 4.1 collective-permute-start.5
  98.2 2.7 collective-permute-start.6
  289.9 8.9 collective-permute-start.7
  299.9 8.1 collective-permute-start.8
  308.3 185.8 %all-gather.10.cloned.1.call-start = ((), (), s32[]{:S(2)}) async-start(), calls=%async_computation.7 | async-start | bytes 5947392 | tf_op jit(solution)/shard_map/all_gather | solution.py:676
  311.9 18.5 %collective-permute-start.9 = (bf16[256,1024]{1,0:T(8,128)(2,1)S(1)}, bf16[256,1024]{1,0:T(8,128)(2,1)S(1)}, u32[]{:S(2)}, u32[]{:S(2)}) collective-permute-start(bf16[256,1024]{1,0:T(8,128)(2,1)S(1)} %get-tuple-element.262), channel_id=1, source_target_pairs={{0,2},{2,0},{1,3},{3,1},{4,6},{6,4},{5,7},{7,5},{8,10},{10,8},{9,1... | collective-permute-start | bytes 1572872 | tf_op jit(solution)/shard_map/ppermute | solution.py:47
  330.4 4.1 collective-permute-start.10
  330.5 445.6 %reduce-scatter.8.cloned.1.call-start = ((), (), s32[]{:S(2)}) async-start(), calls=%async_computation.8 | async-start | bytes 10280960 | tf_op jit(solution)/shard_map/reduce_scatter | solution.py:755
  352.3 13.5 %collective-permute-start.11 = (bf16[2,256,256]{2,1,0:T(8,128)(2,1)S(1)}, bf16[2,256,256]{2,1,0:T(8,128)(2,1)S(1)}, u32[]{:S(2)}, u32[]{:S(2)}) collective-permute-start(bf16[2,256,256]{2,1,0:T(8,128)(2,1)S(1)} %dynamic-slice_bitcast_fusion.10), channel_id=1, source_target_pairs={{0,16},{16,0},{1,17},{17,1},{2,18},{18,2},{3,19},{19,3},{4,20},{20... | collective-permute-start | bytes 786440 | tf_op jit(solution)/shard_map/ppermute | solution.py:47
  365.9 14.6 %collective-permute-start.12 = (bf16[2,256,256]{2,1,0:T(8,128)(2,1)S(1)}, bf16[2,256,256]{2,1,0:T(8,128)(2,1)S(1)}, u32[]{:S(2)}, u32[]{:S(2)}) collective-permute-start(bf16[2,256,256]{2,1,0:T(8,128)(2,1)S(1)} %fusion.101), channel_id=1, source_target_pairs={{0,8},{8,0},{1,9},{9,1},{2,10},{10,2},{3,11},{11,3},{4,12},{12,4},... | collective-permute-start | bytes 786440 | tf_op jit(solution)/shard_map/ppermute | solution.py:47
  369.3 36.7 %collective-permute-start.15 = (bf16[256,1024]{1,0:T(8,128)(2,1)}, bf16[256,1024]{1,0:T(8,128)(2,1)}, u32[]{:S(2)}, u32[]{:S(2)}) collective-permute-start(bf16[256,1024]{1,0:T(8,128)(2,1)} %get-tuple-element.270), channel_id=1, source_target_pairs={{0,2},{2,0},{1,3},{3,1},{4,6},{6,4},{5,7},{7,5},{8,10},{10,8},{9,1... | collective-permute-start | bytes 1572872 | tf_op jit(solution)/shard_map/ppermute | solution.py:47
  385.0 34.5 %collective-permute-start.13 = (bf16[256,1024]{1,0:T(8,128)(2,1)}, bf16[256,1024]{1,0:T(8,128)(2,1)}, u32[]{:S(2)}, u32[]{:S(2)}) collective-permute-start(bf16[256,1024]{1,0:T(8,128)(2,1)} %get-tuple-element.264), channel_id=1, source_target_pairs={{0,2},{2,0},{1,3},{3,1},{4,6},{6,4},{5,7},{7,5},{8,10},{10,8},{9,1... | collective-permute-start | bytes 1572872 | tf_op jit(solution)/shard_map/ppermute | solution.py:47
  407.3 17.6 %collective-permute-start.16 = (bf16[2,256,1024]{2,1,0:T(8,128)(2,1)S(1)}, bf16[2,256,1024]{2,1,0:T(8,128)(2,1)S(1)}, u32[]{:S(2)}, u32[]{:S(2)}) collective-permute-start(bf16[2,256,1024]{2,1,0:T(8,128)(2,1)S(1)} %bitcast_dynamic-update-slice_fusion.10), channel_id=1, source_target_pairs={{0,1},{1,0},{2,3},{3,2},{4,5},{5,4},{6,7},{7,6},{8,9},{9,8},{10,11... | collective-permute-start | bytes 3145736 | tf_op jit(solution)/shard_map/ppermute | solution.py:47
  420.6 4.3 collective-permute-start.14
  498.6 22.1 %collective-permute-start.17 = (bf16[208,1024]{1,0:T(8,128)(2,1)S(1)}, bf16[208,1024]{1,0:T(8,128)(2,1)S(1)}, u32[]{:S(2)}, u32[]{:S(2)}) collective-permute-start(bf16[208,1024]{1,0:T(8,128)(2,1)S(1)} %get-tuple-element.173), channel_id=1, source_target_pairs={{0,4},{4,0},{1,5},{5,1},{2,6},{6,2},{3,7},{7,3},{8,12},{12,8},{9,1... | collective-permute-start | bytes 1277960 | tf_op jit(solution)/shard_map/ppermute | solution.py:47
  520.7 20.4 %collective-permute-start.18 = (bf16[2,208,1024]{2,1,0:T(8,128)(2,1)S(1)}, bf16[2,208,1024]{2,1,0:T(8,128)(2,1)S(1)}, u32[]{:S(2)}, u32[]{:S(2)}) collective-permute-start(bf16[2,208,1024]{2,1,0:T(8,128)(2,1)S(1)} %bitcast_dynamic-update-slice_fusion.16), channel_id=1, source_target_pairs={{0,2},{2,0},{1,3},{3,1},{4,6},{6,4},{5,7},{7,5},{8,10},{10,8},{9,1... | collective-permute-start | bytes 2555912 | tf_op jit(solution)/shard_map/ppermute | solution.py:47
  541.1 4.5 collective-permute-start.19
  575.4 1.4 collective-permute-start.20
  576.9 3.9 collective-permute-start.21
  580.9 4.8 collective-permute-start.22
  617.7 3.7 collective-permute-start.23
  622.2 21.1 %collective-permute-start.24 = (bf16[2,208,1024]{2,1,0:T(8,128)(2,1)S(1)}, bf16[2,208,1024]{2,1,0:T(8,128)(2,1)S(1)}, u32[]{:S(2)}, u32[]{:S(2)}) collective-permute-start(bf16[2,208,1024]{2,1,0:T(8,128)(2,1)S(1)} %dynamic-slice_bitcast_fusion.3), channel_id=1, source_target_pairs={{0,2},{2,0},{1,3},{3,1},{4,6},{6,4},{5,7},{7,5},{8,10},{10,8},{9,1... | collective-permute-start | bytes 2555912 | tf_op jit(solution)/shard_map/ppermute | solution.py:47
  643.3 502.0 %all-gather.14.cloned.1.call-start = ((), (), s32[]{:S(2)}) async-start(), calls=%async_computation.10 | async-start | bytes 4718592 | tf_op jit(solution)/shard_map/all_gather | solution.py:818
  643.7 20.9 %collective-permute-start.25 = (bf16[208,1024]{1,0:T(8,128)(2,1)S(1)}, bf16[208,1024]{1,0:T(8,128)(2,1)S(1)}, u32[]{:S(2)}, u32[]{:S(2)}) collective-permute-start(bf16[208,1024]{1,0:T(8,128)(2,1)S(1)} %dynamic-slice_bitcast_fusion.7), channel_id=1, source_target_pairs={{0,4},{4,0},{1,5},{5,1},{2,6},{6,2},{3,7},{7,3},{8,12},{12,8},{9,1... | collective-permute-start | bytes 1277960 | tf_op jit(solution)/shard_map/ppermute | solution.py:47
  737.5 2.7 collective-permute-start.30
  738.1 3.7 collective-permute-start.26
  740.7 14.8 %collective-permute-start.31 = (bf16[256,1024]{1,0:T(8,128)(2,1)S(1)}, bf16[256,1024]{1,0:T(8,128)(2,1)S(1)}, u32[]{:S(2)}, u32[]{:S(2)}) collective-permute-start(bf16[256,1024]{1,0:T(8,128)(2,1)S(1)} %dynamic-slice_bitcast_fusion.4), channel_id=1, source_target_pairs={{0,2},{2,0},{1,3},{3,1},{4,6},{6,4},{5,7},{7,5},{8,10},{10,8},{9,1... | collective-permute-start | bytes 1572872 | tf_op jit(solution)/shard_map/ppermute | solution.py:47
  743.1 23.0 %collective-permute-start.27 = (bf16[256,1024]{1,0:T(8,128)(2,1)}, bf16[256,1024]{1,0:T(8,128)(2,1)}, u32[]{:S(2)}, u32[]{:S(2)}) collective-permute-start(bf16[256,1024]{1,0:T(8,128)(2,1)} %dynamic-slice_bitcast_fusion.6), channel_id=1, source_target_pairs={{0,2},{2,0},{1,3},{3,1},{4,6},{6,4},{5,7},{7,5},{8,10},{10,8},{9,1... | collective-permute-start | bytes 1572872 | tf_op jit(solution)/shard_map/ppermute | solution.py:47
  758.3 9.1 collective-permute-start.34
  767.4 7.6 collective-permute-start.35
  776.0 369.2 %all-gather.12.cloned.1.call-start = ((), (), s32[]{:S(2)}) async-start(), calls=%async_computation.9 | async-start | bytes 4718592 | tf_op jit(solution)/shard_map/all_gather | solution.py:818
  820.0 2.8 collective-permute-start.28
  823.3 14.0 %collective-permute-start.29 = (bf16[256,1024]{1,0:T(8,128)(2,1)S(1)}, bf16[256,1024]{1,0:T(8,128)(2,1)S(1)}, u32[]{:S(2)}, u32[]{:S(2)}) collective-permute-start(bf16[256,1024]{1,0:T(8,128)(2,1)S(1)} %dynamic-slice_bitcast_fusion.5), channel_id=1, source_target_pairs={{0,2},{2,0},{1,3},{3,1},{4,6},{6,4},{5,7},{7,5},{8,10},{10,8},{9,1... | collective-permute-start | bytes 1572872 | tf_op jit(solution)/shard_map/ppermute | solution.py:47
  839.5 7.6 collective-permute-start.32
  847.2 6.7 collective-permute-start.33
  860.9 3.9 collective-permute-start.37
  864.9 3.8 collective-permute-start.38
  868.8 4.5 collective-permute-start.39
  873.3 271.3 %collective-permute-start.40 = (f32[7,32]{1,0:T(8,128)S(1)}, f32[7,32]{1,0:T(8,128)S(1)}, u32[]{:S(2)}, u32[]{:S(2)}) collective-permute-start(f32[7,32]{1,0:T(8,128)S(1)} %bitcast.537), channel_id=1, source_target_pairs={{0,4},{4,0},{1,5},{5,1},{2,6},{6,2},{3,7},{7,3},{8,12},{12,8},{9,1... | collective-permute-start | bytes 2696 | tf_op jit(solution)/shard_map/ppermute | solution.py:47
  (142 other events, 1559.2 us)
Sparse Core Ops, SparseCore 0:
  11.9 89.1 all-gather.5
  308.4 108.6 all-gather.7
  420.6 73.4 all-gather.9
  643.4 85.2 reduce-scatter.7
Sparse Core Ops, SparseCore 1:
  53.8 50.2 reduce-scatter.3
  106.2 55.3 reduce-scatter.5
  776.1 46.6 all-gather.13
  854.9 46.0 all-gather.11
